TPU v7x, 256 devices: a whole 4x4x8 slice. The times are simulated.
256 devices in a mesh: pair: 8 (over y_lo, x), grow: 8 (over z), gcol: 4 (over y_hi, core).
Axes of the slice: x: 4, y: 4 (y_hi: 2, y_lo: 2; y = y_hi * 2 + y_lo), z: 8, core: 2. Of those that a mesh axis runs over, the one named last changes fastest.
Arguments:
- valence: bfloat16 [2, 64, 128, 16384], P(None, None, ('grow', 'gcol')), may hold values from -6 to 6
- conduction: bfloat16 [2, 8, 128, 16384], P(None, 'pair', ('grow', 'gcol')), may hold values from -6 to 6
- pair_bands: int32 [8, 32], P('pair'), may hold values from 0 to 63, as said below
- e_val: float32 [64], replicated, may hold values from -12 to -1
- e_cond: float32 [8], P('pair'), may hold values from 1 to 12
- g_index: int32 [30720], replicated, may hold values from 0 to 2097151, as said below
- slab_index: int32 [2048], replicated, may hold values from 0 to 2097151, as said below
Outputs:
- chi_slab: float32 [2, 30720, 2048], P(None, ('pair', 'grow'), 'gcol')
Inputs may be any that keep to these rules, and one draw needn't show every extreme that they name: `pair_bands`: each row lists 32 different valence bands. All entries of g_index and slab_index name different grid points. Write G = ((p * 8 + g) * 4 + c) * 120 + j with j < 120; the grid point of row G has q2 within [c * 32, (c + 1) * 32) and q3 within [b w, (b + 1) w) with b = g * 4 + c and w = 4. `slab_index`: write H = ((c * 8 + p) * 8 + g) * 8 + j with j < 8; the grid point of column H lies in the same range of q2 and q3 as the rows of g_index with these g and c.
All inputs are finite; a program needn't handle non-finite values.
Results may differ from a plain program's by a relative error of at most 0.012.
Values may be sent and summed in bfloat16 or wider, within the bound.
No kernel may reach another device: no remote copies, remote signals or barrier semaphores. Data moves between devices by JAX's collectives and lax.ppermute only.
A program may use at most 192 MiB of HBM per device.

v0:
```python
import math

import jax
import jax.numpy as jnp
from jax import lax
from jax.sharding import PartitionSpec as P

NGRID = 128


def transform_table(count, positions):
    freq = jnp.arange(count, dtype=jnp.int32)
    phase = freq[:, None] * positions[None, :] % count
    angle = phase.astype(jnp.float32) * (2.0 * math.pi / count)
    scale = 1.0 / math.sqrt(count)
    cosine = (jnp.cos(angle) * scale).astype(jnp.bfloat16)
    sine = (jnp.sin(angle) * scale).astype(jnp.bfloat16)
    upper = jnp.stack([cosine, sine], axis=1)
    lower = jnp.stack([-sine, cosine], axis=1)
    return jnp.stack([upper, lower])


def on_device(valence, conduction, pair_bands, e_val, e_cond, g_index, slab_index):
    n_pair = lax.axis_size("pair")
    n_grow = lax.axis_size("grow")
    n_gcol = lax.axis_size("gcol")
    grow_at = lax.axis_index("grow")
    gcol_at = lax.axis_index("gcol")
    planes = valence.shape[2]
    bands_here, partners = pair_bands.shape
    pairs_here = bands_here * partners
    total_pairs = pairs_here * n_pair
    picked = jnp.take(valence, pair_bands.reshape(-1), axis=1).astype(jnp.float32)
    cond_rep = jnp.repeat(conduction, partners, axis=1).astype(jnp.float32)
    real_part = picked[0] * cond_rep[0] + picked[1] * cond_rep[1]
    imag_part = picked[0] * cond_rep[1] - picked[1] * cond_rep[0]
    density = jnp.stack([real_part, imag_part]).astype(jnp.bfloat16)
    density = jnp.transpose(density.reshape(2, pairs_here, planes, NGRID, NGRID), (0, 2, 3, 4, 1))
    natural = transform_table(NGRID, jnp.arange(NGRID, dtype=jnp.int32))
    third = jnp.einsum(
        "okix,iabxp->oabkp", natural, density, preferred_element_type=jnp.float32
    ).astype(jnp.bfloat16)
    second = jnp.einsum(
        "okix,iaxbp->oakbp", natural, third, preferred_element_type=jnp.float32
    ).astype(jnp.bfloat16)
    moved = lax.all_to_all(second, ("grow", "gcol"), split_axis=3, concat_axis=1, tiled=True)
    positions = jnp.arange(NGRID, dtype=jnp.int32)
    wide_two = NGRID
    base_three = (grow_at * n_gcol + gcol_at) * planes
    table_first = transform_table(NGRID, positions)
    elements = jnp.einsum(
        "okix,ixabp->okabp", table_first, moved, preferred_element_type=jnp.float32
    ).astype(jnp.bfloat16)
    flat = elements.reshape(2, -1, pairs_here)

    def local_offset(index):
        first_q = index // (NGRID * NGRID)
        second_q = index // NGRID % NGRID
        third_q = index % NGRID
        return (first_q * wide_two + second_q) * planes + third_q - base_three

    row_count = g_index.shape[0] // (n_pair * n_grow * n_gcol)
    row_ids = g_index.reshape(n_pair, n_grow, n_gcol, row_count)[:, grow_at, gcol_at]
    rows = jnp.take(flat, local_offset(row_ids).reshape(-1), axis=1).reshape(
        2, n_pair, row_count, pairs_here
    )
    gaps = jnp.take(e_val, pair_bands) - e_cond[:, None]
    weight = (2.0 / (gaps * math.sqrt(total_pairs))).reshape(-1)
    weighted = (rows.astype(jnp.float32) * weight).astype(jnp.bfloat16)
    col_count = slab_index.shape[0] // (n_pair * n_grow * n_gcol)
    col_ids = slab_index.reshape(n_gcol, n_pair, n_grow, col_count)[gcol_at, :, grow_at]
    cols = jnp.take(flat, local_offset(col_ids).reshape(-1), axis=1).reshape(
        2, n_pair, col_count, pairs_here
    )
    row_block = lax.all_to_all(weighted, "pair", split_axis=1, concat_axis=3, tiled=True).reshape(
        2, row_count, total_pairs
    )
    spread = lax.all_gather(
        cols.reshape(2, n_pair, 1, col_count, pairs_here), "grow", axis=2, tiled=True
    )
    slab = lax.all_gather(spread, "pair", axis=4, tiled=True).reshape(2, -1, total_pairs)
    conjugate = jnp.stack([jnp.stack([slab[0], slab[1]]), jnp.stack([-slab[1], slab[0]])])
    return jnp.einsum(
        "irk,oick->orc",
        lax.all_gather(row_block, "gcol", axis=1, tiled=True),
        conjugate,
        preferred_element_type=jnp.float32,
    )


def solution(mesh):
    in_specs = (
        P(None, None, ("grow", "gcol"), None),
        P(None, "pair", ("grow", "gcol"), None),
        P("pair", None),
        P(),
        P("pair"),
        P(),
        P(),
    )
    out_specs = P(None, ("pair", "grow"), "gcol")
    return jax.shard_map(
        on_device, mesh=mesh, in_specs=in_specs, out_specs=out_specs, check_vma=False
    )
```

profile of v0, /device:TPU:1, one launch (start us, length us, event | category | flops | bytes accessed | tf_op | source)
XLA Modules:
  0.0 530.3 jit_solution(9529081428122668184)
XLA Ops:
  0.0 0.0 copy-start
  0.0 0.3 multiply_convert_fusion.1
  0.3 0.3 fusion.24
  0.6 0.7 fusion.49
  1.2 0.7 compare_and_fusion.2
  1.9 1.0 convert_element_type.90
  2.9 14.9 %gather_fusion = bf16[32,2,4,16384]{3,2,1,0:T(4,128)(2,1)} fusion(bf16[2,64,4,16384]{3,2,1,0:T(4,128)(2,1)} %param.7, s32[1024]{0:T(1024)S(1)} %pad_clamp_fusion.3), kind=kCustom, calls=%fused_computation | custom fusion | bytes 16777344 | tf_op jit(solution)/shard_map/jit(_take)/gather | solution.py:33
  17.8 5.6 %convert_bitcast_fusion = f32[2,32,4,16384]{3,2,0,1:T(4,128)S(1)} fusion(bf16[32,2,4,16384]{3,2,1,0:T(4,128)(2,1)} %gather_fusion, pred[32]{0:T(512)(128)(4,1)S(1)} %compare_and_fusion.2), kind=kLoop, calls=%fused_computation.7 | loop fusion | flops 8388608 | bytes 25165856 | tf_op jit(solution)/shard_map/convert_element_type | solution.py:33
  23.4 6.2 %add_convert_fusion = (bf16[1,32,4,16384]{3,2,0,1:T(4,128)(2,1)}, bf16[1,32,4,16384]{3,2,0,1:T(4,128)(2,1)}) fusion(f32[2,32,4,16384]{3,2,0,1:T(4,128)S(1)} %convert_bitcast_fusion, f32[4,16384]{1,0:T(4,128)S(1)} %get-tuple-element.14, f32[4,16384]{1,0:T(4,128)S(1)} %get-tuple-element.13), kind=kLoop, calls=%fused_computation.12 | loop fusion | flops 16777216 | bytes 25690112 | tf_op jit(solution)/shard_map/convert.3
  29.6 8.4 %reshape.640 = bf16[1,32,4,128,128]{4,3,2,1,0:T(8,128)(2,1)} reshape(bf16[1,32,4,16384]{3,2,0,1:T(4,128)(2,1)} %get-tuple-element.10) | data formatting | bytes 8388608 | tf_op jit(solution)/shard_map/stack | solution.py:37
  38.0 8.4 %reshape.639 = bf16[1,32,4,128,128]{4,3,2,1,0:T(8,128)(2,1)} reshape(bf16[1,32,4,16384]{3,2,0,1:T(4,128)(2,1)} %get-tuple-element.9) | data formatting | bytes 8388608 | tf_op jit(solution)/shard_map/stack | solution.py:37
  46.5 9.3 %fusion.6 = bf16[2,4,128,128,32]{2,3,0,4,1:T(8,128)(2,1)} fusion(bf16[1,128,2,128]{3,1,2,0:T(8,128)(2,1)S(1)} %get-tuple-element.18, bf16[1,128,2,128]{3,1,2,0:T(8,128)(2,1)S(1)} %get-tuple-element.17, bf16[1,32,4,128,128]{4,3,2,1,0:T(8,128)(2,1)} %reshape.640, bf16[1,32,4,128,128]{4,3,2,1,0:T(8,128)(2,1)} %reshape.639), kind=kOutput, calls=%fused_computation.13 | convolution fusion | flops 4308074496 | bytes 16908288 | tf_op jit(solution)/shard_map/okix,iaxbp->oakbp/dot_general | solution.py:43
  55.8 13.1 %copy.35 = bf16[2,4,128,128,32]{2,0,4,1,3:T(2,128)(2,1)} copy(bf16[2,4,128,128,32]{2,3,0,4,1:T(8,128)(2,1)} %fusion.6) | data formatting | bytes 16777216 | tf_op jit(solution)/shard_map/convert_element_type | solution.py:45
  68.9 0.0 copy-start.4
  68.9 13.0 %all-to-all-start = ((bf16[2,4,128,128,32]{2,0,4,1,3:T(2,128)(2,1)}), bf16[2,4,128,128,32]{2,0,4,1,3:T(2,128)(2,1)}, u32[]{:S(2)}, u32[]{:S(2)}) async-start(bf16[2,4,128,128,32]{2,0,4,1,3:T(2,128)(2,1)} %copy.35), calls=%async_computation | async-start | bytes 16777216 | tf_op jit(solution)/shard_map/all_to_all | solution.py:46
  81.9 0.1 reshape.589
  82.0 0.5 broadcast.855
  82.5 0.7 fusion.57
  83.2 0.1 squeeze.9
  83.9 0.3 reshape.595
  84.2 0.7 fusion.56
  84.9 0.1 squeeze.22
  85.0 0.0 copy-done.4
  85.0 0.7 gather_fusion.3
  85.8 0.1 compare_select_fusion
  85.9 182.5 %all-to-all-done = bf16[2,4,128,128,32]{2,0,4,1,3:T(2,128)(2,1)} async-done(((bf16[2,4,128,128,32]{2,0,4,1,3:T(2,128)(2,1)}), bf16[2,4,128,128,32]{2,0,4,1,3:T(2,128)(2,1)}, u32[]{:S(2)}, u32[]{:S(2)}) %all-to-all-start) | async-done | bytes 8388640 | tf_op jit(solution)/shard_map/all_to_all | solution.py:46
  268.4 8.4 %copy.36 = bf16[2,4,128,32,4,32]{2,1,3,0,5,4:T(4,128)(2,1)S(1)} copy(bf16[2,4,128,32,4,32]{2,0,5,1,4,3:T(2,128)(2,1)} %bitcast.22) | data formatting | bytes 16777216 | tf_op jit(solution)/shard_map/all_to_all | solution.py:46
  276.8 4.5 bitcast_convert_fusion
  281.4 33.0 %copy.37 = bf16[2,128,128,4,32]{4,3,2,1,0:T(4,128)(2,1)} copy(bf16[2,128,128,4,32]{2,1,4,3,0:T(8,128)(2,1)} %bitcast_convert_fusion) | data formatting | bytes 16777216 | tf_op jit(solution)/shard_map/convert_element_type | solution.py:53
  314.4 60.1 %copy.38 = bf16[2,65536,32]{2,0,1:T(2,128)(2,1)} copy(bf16[2,65536,32]{2,1,0:T(8,128)(2,1)} %bitcast.113) | data formatting | bytes 16777216 | tf_op jit(solution)/shard_map/reshape | solution.py:54
  374.5 1.5 gather_fusion.1
  376.0 0.1 copy_select_fusion
  376.1 18.8 %all_gather.9 = bf16[2,8,8,8,32]{4,3,1,0,2:T(8,128)(2,1)S(1)} all-gather(bf16[2,8,1,8,32]{4,3,1,0,2:T(8,128)(2,1)S(1)} %copy_select_fusion), channel_id=1, replica_groups=mesh['pair'=8,'grow'=8,'gcol'=4] {'grow'}, dimensions={2}, use_global_device_ids=true | all-gather | bytes 73728 | tf_op jit(solution)/shard_map/all_gather | solution.py:78
  394.9 1.7 copy.40
  396.7 77.1 %all_gather.10 = bf16[2,8,8,8,256]{3,2,1,0,4:T(8,128)(2,1)S(1)} all-gather(bf16[2,8,8,8,32]{3,2,1,0,4:T(8,128)(2,1)S(1)} %copy.40), channel_id=1, replica_groups=mesh['pair'=8,'grow'=8,'gcol'=4] {'pair'}, dimensions={4}, use_global_device_ids=true | all-gather | bytes 589824 | tf_op jit(solution)/shard_map/all_gather | solution.py:81
  473.8 4.2 fusion.58
  478.0 4.8 copy.42
  482.8 4.8 copy.41
  487.6 13.6 %gather_fusion.2 = bf16[960,2,32]{2,1,0:T(2,128)(2,1)S(1)} fusion(bf16[2,65536,32]{2,0,1:T(2,128)(2,1)} %copy.38, s32[1024]{0:T(1024)S(1)} %pad_clamp_fusion.1), kind=kCustom, calls=%fused_computation.2 | custom fusion | bytes 249600 | tf_op jit(solution)/shard_map/jit(_take)/gather | solution.py:64
  501.3 0.2 copy.62
  501.5 0.1 multiply_convert_fusion
  501.6 0.7 copy.45
  502.3 3.9 all-to-all-start.1
  506.2 0.1 maximum_bitcast_fusion.1
  506.3 5.3 %all-to-all-done.1 = bf16[2,8,120,32]{2,3,0,1:T(8,128)(2,1)S(1)} async-done(((bf16[2,8,120,32]{2,3,0,1:T(8,128)(2,1)}), bf16[2,8,120,32]{2,3,0,1:T(8,128)(2,1)S(1)}, u32[]{:S(2)}, u32[]{:S(2)}) %all-to-all-start.1) | async-done | bytes 122912 | tf_op jit(solution)/shard_map/all_to_all | solution.py:75
  511.6 0.1 copy.47
  511.7 16.6 %all_gather.11 = bf16[2,480,256]{2,1,0:T(8,128)(2,1)S(1)} all-gather(bf16[2,120,256]{2,1,0:T(8,128)(2,1)S(1)} %copy.47), channel_id=1, replica_groups=mesh['pair'=8,'grow'=8,'gcol'=4] {'gcol'}, dimensions={1}, use_global_device_ids=true | all-gather | bytes 614400 | tf_op jit(solution)/shard_map/all_gather | solution.py:85
  528.3 2.0 convolution_bitcast_fusion
  (20 shorter events, 0.2 us)
Async XLA Ops:
  0.0 85.0 %copy-start = (f32[64]{0:T(128)S(1)}, f32[64]{0:T(128)}, u32[]{:S(2)}) copy-start(f32[64]{0:T(128)} %param.10) | copy-start | bytes 772
  68.9 13.0 %copy-start.3 = (s32[2048]{0:T(1024)S(1)}, s32[2048]{0:T(1024)}, u32[]{:S(2)}) copy-start(s32[2048]{0:T(1024)} %param.13) | copy-start | bytes 24580
  68.9 15.0 %copy-start.2 = (s32[30720]{0:T(1024)S(1)}, s32[30720]{0:T(1024)}, u32[]{:S(2)}) copy-start(s32[30720]{0:T(1024)} %param.12) | copy-start | bytes 368644
  68.9 16.1 %copy-start.4 = (s32[1,32]{1,0:T(1,128)S(1)}, s32[1,32]{1,0:T(1,128)}, u32[]{:S(2)}) copy-start(s32[1,32]{1,0:T(1,128)} %param.9) | copy-start | bytes 388
  68.9 199.5 %all-to-all-start = ((bf16[2,4,128,128,32]{2,0,4,1,3:T(2,128)(2,1)}), bf16[2,4,128,128,32]{2,0,4,1,3:T(2,128)(2,1)}, u32[]{:S(2)}, u32[]{:S(2)}) async-start(bf16[2,4,128,128,32]{2,0,4,1,3:T(2,128)(2,1)} %copy.35), calls=%async_computation | async-start | bytes 16777216 | tf_op jit(solution)/shard_map/all_to_all | solution.py:46
  478.0 52.4 %copy-start.1 = (f32[64]{0:T(128)S(1)}, f32[64]{0:T(128)}, u32[]{:S(2)}) copy-start(f32[64]{0:T(128)} %param.10) | copy-start | bytes 772
  502.3 9.3 %all-to-all-start.1 = ((bf16[2,8,120,32]{2,3,0,1:T(8,128)(2,1)}), bf16[2,8,120,32]{2,3,0,1:T(8,128)(2,1)S(1)}, u32[]{:S(2)}, u32[]{:S(2)}) async-start(bf16[2,8,120,32]{2,3,0,1:T(8,128)(2,1)} %copy.45), calls=%async_computation.1 | async-start | bytes 262144 | tf_op jit(solution)/shard_map/all_to_all | solution.py:75
where the time goes:
time: 532 us; the launch traced here: 530 us
  waiting for transfers between devices  188 us (35%)
  local copies, waits for them, and re-layouts  181 us (34%)
  blocking collectives  113 us (21%)
  starting transfers between devices  16.8 us (3%)
  matrix products  15.8 us (3%)
  other arithmetic  15.1 us (3%)
    all_to_all x1, waiting for transfers between devices, on_device(): lax.all_to_all(second, ('grow', 'gcol'), split_axis=3, concat_axis=1, til...  182 us
    all_gather x1, blocking collectives, on_device(): lax.all_gather(spread, 'pair', axis=4, tiled=True)  77.1 us
    reshape x1, local copies, waits for them, and re-layouts, on_device(): flat = elements.reshape(2, -1, pairs_here)  60.1 us
    convert_element_type x1, local copies, waits for them, and re-layouts, on_device(): elements = jnp.einsum('okix,ixabp->okabp', table_first, moved, preferred_...  33 us
    all_gather x1, blocking collectives, on_device(): lax.all_gather(cols.reshape(2, n_pair, 1, col_count, pairs_here), 'grow',...  18.8 us
    another operation x2, local copies, waits for them, and re-layouts, on_device(): density = jnp.stack([real_part, imag_part]).astype(jnp.bfloat16)  16.8 us
    all_gather x1, blocking collectives, on_device(): lax.all_gather(row_block, 'gcol', axis=1, tiled=True)  16.6 us
    gather x1, local copies, waits for them, and re-layouts, on_device(): jnp.take(valence, pair_bands.reshape(-1), axis=1).astype(jnp.float32)  14.9 us
  transfers between devices with their start and end apart: 2, of which 2 were waited for; matrix products, arithmetic and copies ran while one was open for 1% of the time, Pallas kernels for 0%

commit v1 on v0

v1 whole, which is shorter than its diff:
```python
import math
import numpy as np
import ml_dtypes
import jax
import jax.numpy as jnp
from jax import lax
from jax.sharding import PartitionSpec as P
from jax.experimental import pallas as pl
from jax.experimental.pallas import tpu as pltpu
BF=jnp.bfloat16
NG=128; GR=8; GC=4; PL=4; QW=32; PAIRS=32; J=4
NT=(((1,),(1,)),((),()))
NN=(((1,),(0,)),((),()))

def cs(freq,pos):
    ph=(freq[:,None]*pos[None,:])%NG
    ang=ph.astype(np.float64)*(2*math.pi/NG)
    return np.cos(ang)/math.sqrt(NG), np.sin(ang)/math.sqrt(NG)

def tables():
    ar=np.arange(NG)
    c,w,g=np.meshgrid(np.arange(GC),np.arange(PL),np.arange(GR),indexing="ij")
    q3=((g*GC+c)*PL+w).reshape(-1)
    co,si=cs(q3,ar)
    t3=np.block([[co,si],[-si,co]])
    t2=np.zeros((GC,J,2,NG,2,J,QW))
    for cc in range(GC):
        co,si=cs(cc*QW+np.arange(QW),ar)
        for j in range(J):
            t2[cc,j,0,:,0,j,:]=co.T
            t2[cc,j,1,:,0,j,:]=si.T
            t2[cc,j,0,:,1,j,:]=-si.T
            t2[cc,j,1,:,1,j,:]=co.T
    t2=t2.reshape(GC,J*2*NG,2*J*QW)
    perm=np.zeros((256,256))
    for cc in range(GC):
        for s in range(PL):
            for o in range(2):
                for g_ in range(GR):
                    perm[((g_*GC+cc)*PL+s)*2+o, ((cc*PL+s)*2+o)*GR+g_]=1
    return [np.asarray(t,np.float32).astype(ml_dtypes.bfloat16) for t in (t3,t2,perm)]

def kern_a(bands, v0,v1,v2,v3, cond, t3, t2, perm, out, vs, third):
    for j,v in enumerate((v0,v1,v2,v3)):
        vs[0]=v[0,0].astype(jnp.float32)
        vs[1]=v[1,0].astype(jnp.float32)
        for sp in range(PL//2):
            rows=[]
            for s in (2*sp,2*sp+1):
                vr=vs[0,pl.ds(s,NG,stride=PL),:]
                vi=vs[1,pl.ds(s,NG,stride=PL),:]
                cr=cond[0,s]
                ci=cond[1,s]
                re=vr*cr+vi*ci
                im=vr*ci-vi*cr
                rows.append(jnp.concatenate([re.astype(BF),im.astype(BF)],axis=1))
            d=jnp.concatenate(rows,axis=0)
            th=lax.dot_general(t3[...],d,NT,preferred_element_type=jnp.float32)
            third[j,sp]=th.astype(BF)
    ys=[]
    for c in range(GC):
        lhs=[]
        for s in range(PL):
            lhs.append(jnp.concatenate([third[j,s//2,i*NG+c*QW:i*NG+(c+1)*QW,(s%2)*NG:(s%2+1)*NG] for j in range(J) for i in range(2)],axis=1))
        lhs=jnp.concatenate(lhs,axis=0)
        ys.append(jnp.dot(lhs,t2[c],preferred_element_type=jnp.float32))
    for wp in range(PL//2):
        cols=[]
        for w in (2*wp,2*wp+1):
            pieces=[ys[c][s*QW+w*GR:s*QW+(w+1)*GR,o*NG:(o+1)*NG] for c in range(GC) for s in range(PL) for o in range(2)]
            cols.append(jnp.concatenate(pieces,axis=0).astype(BF))
        y=jnp.concatenate(cols,axis=1)
        out[:,wp*256:(wp+1)*256]=jnp.dot(perm[...],y,preferred_element_type=jnp.float32).astype(BF)

def stage_a(valence, cond, bands):
    nval=valence.shape[1]
    v=jnp.transpose(valence.reshape(2,nval,PL,NG,NG),(0,1,3,2,4)).reshape(2,nval,NG*PL,NG)
    cf=cond.reshape(2,PL,NG,NG).astype(jnp.float32)
    t3,t2,perm=tables()
    def vspec(j):
        return pl.BlockSpec((2,1,NG*PL,NG),lambda q,b: (0,b[q*J+j],0,0))
    full=lambda shape: pl.BlockSpec(shape,lambda q,b:(0,)*len(shape))
    return pl.pallas_call(kern_a,
        grid_spec=pltpu.PrefetchScalarGridSpec(num_scalar_prefetch=1,grid=(bands.shape[0]//J,),
            in_specs=[vspec(j) for j in range(J)]+[full((2,PL,NG,NG)),full((256,256)),full((GC,1024,256)),full((256,256))],
            out_specs=pl.BlockSpec((256,512),lambda q,b:(0,q)),
            scratch_shapes=[pltpu.VMEM((2,NG*PL,NG),jnp.float32),pltpu.VMEM((J,PL//2,256,256),BF)]),
        out_shape=jax.ShapeDtypeStruct((256,bands.shape[0]//J*512),BF),
        compiler_params=pltpu.CompilerParams(vmem_limit_bytes=48*2**20),
        name="partial_transform")(bands,v,v,v,v,cf,t3,t2,perm)

ROWS=GR*64; COLS=32; PTS=ROWS+COLS

def tables_c():
    ar=np.arange(NG)
    co,si=cs(ar,ar)
    t1=np.zeros((NG,2,NG,2))
    t1[:,0,:,0]=co; t1[:,0,:,1]=si; t1[:,1,:,0]=-si; t1[:,1,:,1]=co
    t1=t1.reshape(256,256)
    lp=np.zeros((PAIRS,QW,QW,PAIRS))
    for p in range(PAIRS):
        for q in range(QW):
            lp[p,q,q,p]=1
    lp=lp.reshape(1024,1024)
    pick=np.zeros((2,2,4,PAIRS,2,2,PAIRS))
    for h in range(2):
        for o in range(2):
            for p in range(PAIRS):
                pick[h,o,:,p,h,o,p]=1
    pick=pick.reshape(512,128)
    return [np.asarray(t,np.float32).astype(ml_dtypes.bfloat16) for t in (t1,lp,pick)]

def kern_c(place, x, t1, lp, pick, mask, weight, rows_out, cols_out, field, found):
    for w in range(PL):
        xw=jnp.concatenate([x[:,(q*PL+w)*NG:(q*PL+w+1)*NG] for q in range(8)],axis=1)
        e=jnp.dot(t1[...],xw,preferred_element_type=jnp.float32).astype(BF)
        f=jnp.dot(e,lp[...],preferred_element_type=jnp.float32)
        for t in range(8):
            field[(w*8+t)*256:(w*8+t+1)*256,:]=f[:,t*NG:(t+1)*NG]
    def body(r,carry):
        for h in range(2):
            at=pl.multiple_of(place[2*r+h],2)
            found[pl.ds(pl.multiple_of(4*r+2*h,2),2),:]=field[pl.ds(at,2),:]
        return carry
    lax.fori_loop(0,PTS,body,0,unroll=8)
    parts=[]
    for h in range(2):
        for o in range(2):
            parts.append(found[pl.ds(2*h+o,PTS,stride=4),:].astype(BF)*mask[:,h*NG:(h+1)*NG])
    got=jnp.dot(jnp.concatenate(parts,axis=1),pick[...],preferred_element_type=jnp.float32)
    rows_out[...]=(got[:ROWS]*weight[...]).astype(BF)
    cols_out[...]=got[ROWS:].astype(BF)

def point_lists(g_index, slab_index, n_pair,n_grow,n_gcol,grow_at,gcol_at):
    rc=g_index.shape[0]//(n_pair*n_grow*n_gcol)
    cc=slab_index.shape[0]//(n_pair*n_grow*n_gcol)
    row_ids=g_index.reshape(n_pair,n_grow,n_gcol,rc)[:,grow_at,gcol_at]
    row_ids=jnp.pad(row_ids,((0,0),(0,NG-rc)),mode="edge")
    row_ids=jnp.transpose(row_ids.reshape(n_pair,2,64),(0,2,1)).reshape(ROWS,2)
    col_ids=slab_index.reshape(n_gcol,n_pair,n_grow,cc)[gcol_at,:,grow_at]
    col_ids=jnp.transpose(col_ids.reshape(2,COLS),(1,0))
    return jnp.concatenate([row_ids,col_ids],axis=0)

def stage_c(moved, ids, weight):
    q1=ids//(NG*NG); q2=ids//NG%QW; w=ids%PL
    place=((w*8+q2//4)*256+2*q1).reshape(-1)
    lane=jnp.arange(NG,dtype=jnp.int32)//PAIRS
    mask=((q2%4)[:,:,None]==lane).astype(BF).reshape(PTS,2*NG)
    wl=jnp.tile(weight,4).reshape(1,NG)
    t1,lp,pick=tables_c()
    vm=pl.BlockSpec(memory_space=pltpu.VMEM)
    return pl.pallas_call(kern_c,
        in_specs=[pl.BlockSpec(memory_space=pltpu.SMEM)]+[vm]*6,
        out_specs=[vm,vm],
        out_shape=[jax.ShapeDtypeStruct((ROWS,NG),BF),jax.ShapeDtypeStruct((COLS,NG),BF)],
        scratch_shapes=[pltpu.VMEM((PL*8*256,NG),jnp.float32),pltpu.VMEM((4*PTS,NG),jnp.float32)],
        compiler_params=pltpu.CompilerParams(vmem_limit_bytes=48*2**20),
        name="last_transform")(place,moved,t1,lp,pick,mask,wl)

def tables_d():
    q=np.zeros((2,2,2,PAIRS,2,2,2,2,PAIRS))
    for hc in range(2):
        for hr in range(2):
            for p in range(PAIRS):
                q[hc,hc,0,p,hr,0,hr,0,p]=1
                q[hc,hc,1,p,hr,0,hr,1,p]=1
                q[hc,hc,1,p,hr,1,hr,0,p]=-1
                q[hc,hc,0,p,hr,1,hr,1,p]=1
    q=q.reshape(2,128,512)
    return np.asarray(q,np.float32).astype(ml_dtypes.bfloat16)

def kern_d(rows, cols, turn, out, rhs):
    for p in range(8):
        s=cols[p]
        for hc in range(2):
            v=jnp.dot(s,turn[hc],preferred_element_type=jnp.float32)
            for pb in range(4):
                piece=jnp.concatenate([v[(g*4+pb)*8:(g*4+pb+1)*8] for g in range(8)],axis=0).astype(BF)
                for k in range(4):
                    rhs[k,(hc*4+pb)*64:(hc*4+pb+1)*64,p*NG:(p+1)*NG]=piece[:,k*NG:(k+1)*NG]
    lhs=jnp.concatenate([rows[p] for p in range(8)],axis=1)
    for hr in range(2):
        n=64 if hr==0 else 56
        for o in range(2):
            z=lax.dot_general(lhs,rhs[hr*2+o],NT,preferred_element_type=jnp.float32)
            for c in range(4):
                out[o,c*120+64*hr:c*120+64*hr+n,:]=z[c*64:c*64+n]

def stage_d(rows, cols):
    vm=pl.BlockSpec(memory_space=pltpu.VMEM)
    return pl.pallas_call(kern_d,
        in_specs=[vm]*3,out_specs=vm,
        out_shape=jax.ShapeDtypeStruct((2,480,512),jnp.float32),
        scratch_shapes=[pltpu.VMEM((4,512,1024),BF)],
        compiler_params=pltpu.CompilerParams(vmem_limit_bytes=48*2**20),
        name="pair_sums")(rows,cols,tables_d())

def on_device(valence, conduction, pair_bands, e_val, e_cond, g_index, slab_index):
    n_pair = lax.axis_size("pair")
    n_grow = lax.axis_size("grow")
    n_gcol = lax.axis_size("gcol")
    grow_at = lax.axis_index("grow")
    gcol_at = lax.axis_index("gcol")
    bands = pair_bands.reshape(-1)
    part = stage_a(valence, conduction, bands)
    moved = lax.all_to_all(part.reshape(32, 8, 4096), ("grow", "gcol"), 0, 0, tiled=True)
    ids = point_lists(g_index, slab_index, n_pair, n_grow, n_gcol, grow_at, gcol_at)
    gaps = jnp.take(e_val, bands) - e_cond[0]
    weight = 2.0 / (gaps * math.sqrt(PAIRS * n_pair))
    rows, cols = stage_c(moved.reshape(256, 4096), ids, weight)
    rows = jnp.broadcast_to(rows.reshape(8, 1, 64, NG), (8, 4, 64, NG)).reshape(32, 64, NG)
    rows = lax.all_to_all(rows, ("pair", "gcol"), 0, 0, tiled=True).reshape(8, 256, NG)
    cols = jnp.broadcast_to(cols[None], (64, COLS, NG))
    cols = lax.all_to_all(cols, ("pair", "grow"), 0, 0, tiled=True).reshape(8, 256, NG)
    return stage_d(rows, cols)


def solution(mesh):
    in_specs = (
        P(None, None, ("grow", "gcol"), None),
        P(None, "pair", ("grow", "gcol"), None),
        P("pair", None),
        P(),
        P("pair"),
        P(),
        P(),
    )
    out_specs = P(None, ("pair", "grow"), "gcol")
    return jax.shard_map(
        on_device, mesh=mesh, in_specs=in_specs, out_specs=out_specs, check_vma=False
    )
```

time: 532 us -> 133 us (0.25)
  local copies, waits for them, and re-layouts: 181 us -> 10.6 us
  waiting for transfers between devices: 188 us -> 45.4 us
  blocking collectives: 113 us -> 39.6 us
  Pallas kernels: 0 us -> 21.3 us
  matrix products: 15.8 us -> 0 us
  other arithmetic: 15.1 us -> 0.23 us
    all_to_all x2 -> x1, waiting for transfers between devices: 188 us -> 45.4 us  [on_device(): lax.all_to_all(part.reshape(32, 8, 4096), ('grow', 'gcol'), 0, 0, tiled=T...]
    all_gather x3 -> x0, blocking collectives: 113 us -> none  [the longest x1 77.1 us: on_device(): lax.all_gather(spread, 'pair', axis=4, tiled=True)]
    reshape x4 -> x5, local copies, waits for them, and re-layouts: 60.6 us -> 0.63 us  [the longest x1 0.3 us: point_lists(): row_ids = g_index.reshape(n_pair, n_grow, n_gcol, rc)[:, grow_at, gcol_at]]
    convert_element_type x3 -> x1, local copies, waits for them, and re-layouts: 46.8 us -> 1.2 us  [stage_a(): cf = cond.reshape(2, PL, NG, NG).astype(jnp.float32)]
    all_to_all x0 -> x2, blocking collectives: none -> 39.6 us  [the longest x1 20.7 us: on_device(): lax.all_to_all(cols, ('pair', 'grow'), 0, 0, tiled=True).reshape(8, 256, NG)]
    gather x5 -> x1, local copies, waits for them, and re-layouts: 31 us -> 0.7 us  [on_device(): gaps = jnp.take(e_val, bands) - e_cond[0]]
    pallas_call x0 -> x3, Pallas kernels: none -> 21.3 us  [the longest x1 12.4 us: stage_a(): pl.pallas_call(kern_a, grid_spec=pltpu.PrefetchScalarGridSpec(num_scalar_...]
    another operation x2 -> x3, local copies, waits for them, and re-layouts: 16.8 us -> 0.16 us  [the longest x2 0.09 us: stage_c(): wl = jnp.tile(weight, 4).reshape(1, NG)]
  transfers between devices with their start and end apart: 2 -> 1, of which waited for: 2 -> 1; matrix products, arithmetic and copies ran while one was open for 1% -> 3% of each run, Pallas kernels for 0% -> 0%
where the time goes in v1:
time: 133 us; the launch traced here: 131 us
  waiting for transfers between devices  45.4 us (34%)
  blocking collectives  39.6 us (30%)
  Pallas kernels  21.3 us (16%)
  starting transfers between devices  12.9 us (10%)
  local copies, waits for them, and re-layouts  10.6 us (8%)
    all_to_all x1, waiting for transfers between devices, on_device(): lax.all_to_all(part.reshape(32, 8, 4096), ('grow', 'gcol'), 0, 0, tiled=T...  45.4 us
    all_to_all x1, blocking collectives, on_device(): lax.all_to_all(cols, ('pair', 'grow'), 0, 0, tiled=True).reshape(8, 256, NG)  20.7 us
    all_to_all x1, blocking collectives, on_device(): lax.all_to_all(rows, ('pair', 'gcol'), 0, 0, tiled=True).reshape(8, 256, NG)  18.9 us
    all_to_all x1, starting transfers between devices, on_device(): lax.all_to_all(part.reshape(32, 8, 4096), ('grow', 'gcol'), 0, 0, tiled=T...  12.9 us
    pallas_call x1, Pallas kernels, stage_a(): pl.pallas_call(kern_a, grid_spec=pltpu.PrefetchScalarGridSpec(num_scalar_...  12.4 us
    unnamed x24, local copies, waits for them, and re-layouts  5.68 us
    pallas_call x1, Pallas kernels, stage_c(): pl.pallas_call(kern_c, in_specs=[pl.BlockSpec(memory_space=pltpu.SMEM)] +...  5.03 us
    pallas_call x1, Pallas kernels, stage_d(): pl.pallas_call(kern_d, in_specs=[vm] * 3, out_specs=vm, out_shape=jax.Sha...  3.82 us
  transfers between devices with their start and end apart: 1, of which 1 were waited for; matrix products, arithmetic and copies ran while one was open for 3% of the time, Pallas kernels for 0%

profile of v1, /device:TPU:1, one launch (start us, length us, event | category | flops | bytes accessed | tf_op | source)
XLA Modules:
  0.0 130.9 jit_solution(7294653109804078642)
XLA Ops:
  0.0 0.0 copy-start
  0.0 1.2 reshape.204.cond
  1.2 0.0 copy-start.1
  1.2 1.6 %copy-done.1 = bf16[4,1024,256]{2,1,0:T(8,128)(2,1)S(1)} copy-done((bf16[4,1024,256]{2,1,0:T(8,128)(2,1)S(1)}, bf16[4,1024,256]{2,1,0:T(8,128)(2,1)}, u32[]{:S(2)}) %copy-start.1) | copy-done | bytes 2097176
  2.8 0.0 copy-start.4
  2.8 0.9 copy-done.4
  3.7 0.0 copy-start.5
  3.7 0.9 copy-done.5
  4.6 0.7 copy-done.8
  5.3 12.4 %partial_transform.1 = bf16[256,4096]{1,0:T(8,128)(2,1)} custom-call(s32[32]{0:T(128)S(1)} %bitcast.40, bf16[2,64,512,128]{3,2,1,0:T(8,128)(2,1)} %bitcast.41, bf16[2,64,512,128]{3,2,1,0:T(8,128)(2,1)} %bitcast.42, bf16[2,64,512,128]{3,2,1,0:T(8,128)(2,1)} %bitcast.43, bf16[2,64,512,128]{3,2,1,0:T(8,128)(2,1)} %bitcast.44, ...), custom_call_target="tpu_custom_call" | custom-call | tf_op jit(solution)/shard_map/partial_transform/pallas_call | solution.py:83
  17.7 0.0 copy-start.11
  17.7 0.0 copy-start.10
  17.7 0.0 copy-start.9
  17.7 12.9 %all-to-all-start = ((bf16[32,8,4096]{2,1,0:T(8,128)(2,1)}), bf16[32,8,4096]{2,1,0:T(8,128)(2,1)S(1)}, u32[]{:S(2)}, u32[]{:S(2)}) async-start(bf16[32,8,4096]{2,1,0:T(8,128)(2,1)} %bitcast.7), calls=%async_computation | async-start | bytes 4194304 | tf_op jit(solution)/shard_map/all_to_all | solution.py:206
  30.6 0.0 copy-start.6
  30.6 0.0 copy-start.7
  30.6 0.0 copy-done.11
  30.7 0.1 reshape.194
  30.8 0.1 reshape_squeeze.3
  30.9 0.0 copy-done.10
  30.9 0.3 reshape.190
  31.2 0.2 slice_reduce_fusion
  31.4 0.1 reshape.191
  31.5 0.1 pad_add_fusion.1
  31.5 0.1 reshape.192
  31.6 0.1 reshape.193
  31.8 0.1 copy.25
  31.9 0.2 concatenate.24
  32.1 0.1 copy.27
  32.9 0.0 copy-done.9
  32.9 0.0 copy-done
  33.0 0.7 gather_fusion
  33.7 0.1 reshape_tile.3.weight
  33.8 1.4 %eq.24 = s32[544,2,128]{2,1,0:T(2,128)S(1)} broadcast(s32[544,2]{1,0:T(8,128)S(1)} %copy.27), dimensions={0,1} | broadcast | bytes 561408 | tf_op jit(solution)/shard_map/eq | solution.py:148
  35.2 0.1 fusion.mask
  35.3 45.4 %all-to-all-done = bf16[32,8,4096]{2,1,0:T(8,128)(2,1)S(1)} async-done(((bf16[32,8,4096]{2,1,0:T(8,128)(2,1)}), bf16[32,8,4096]{2,1,0:T(8,128)(2,1)S(1)}, u32[]{:S(2)}, u32[]{:S(2)}) %all-to-all-start) | async-done | bytes 2097184 | tf_op jit(solution)/shard_map/all_to_all | solution.py:206
  80.7 0.0 copy-done.6
  80.7 0.0 copy-done.7
  80.7 0.0 copy-start.2
  80.7 1.6 %copy-done.2 = bf16[1024,1024]{1,0:T(8,128)(2,1)S(1)} copy-done((bf16[1024,1024]{1,0:T(8,128)(2,1)S(1)}, bf16[1024,1024]{1,0:T(8,128)(2,1)}, u32[]{:S(2)}) %copy-start.2) | copy-done | bytes 2097176
  82.3 5.0 %last_transform.1 = (bf16[512,128]{1,0:T(8,128)(2,1)S(1)}, bf16[32,128]{1,0:T(8,128)(2,1)S(1)}) custom-call(s32[1088]{0:T(1024)S(1)} %fusion.4.place, bf16[256,4096]{1,0:T(8,128)(2,1)S(1)} %bitcast.36, bf16[256,256]{1,0:T(8,128)(2,1)S(1)} %copy-done.6, bf16[1024,1024]{1,0:T(8,128)(2,1)S(1)} %copy-done.2, bf16[512,128]{1,0:T(8,128)(2,1)S(1)} %copy-done.7, ...), custom_call_target="tpu_custom_call" | custom-call | tf_op jit(solution)/shard_map/last_transform/pallas_call | solution.py:152
  87.3 0.0 copy-start.3
  87.3 0.1 broadcast_in_dim.25
  87.5 18.9 %all_to_all.15 = bf16[32,64,128]{2,1,0:T(8,128)(2,1)S(1)} all-to-all(bf16[32,64,128]{2,1,0:T(8,128)(2,1)S(1)} %bitcast.46), channel_id=1, replica_groups=mesh['pair'=8,'grow'=8,'gcol'=4] {'pair','gcol'}, dimensions={0} | all-to-all | bytes 1048576 | tf_op jit(solution)/shard_map/all_to_all | solution.py:212
  106.4 0.1 broadcast_in_dim.26
  106.4 20.7 %all_to_all.16 = bf16[64,32,128]{2,1,0:T(8,128)(2,1)S(1)} all-to-all(bf16[64,32,128]{2,1,0:T(8,128)(2,1)S(1)} %broadcast_in_dim.26), channel_id=1, replica_groups=mesh['pair'=8,'grow'=8,'gcol'=4] {'pair','grow'}, dimensions={0} | all-to-all | bytes 1048576 | tf_op jit(solution)/shard_map/all_to_all | solution.py:214
  127.1 0.0 copy-done.3
  127.1 3.8 %pair_sums.1 = f32[2,480,512]{2,1,0:T(8,128)} custom-call(bf16[8,256,128]{2,1,0:T(8,128)(2,1)S(1)} %bitcast.37, bf16[8,256,128]{2,1,0:T(8,128)(2,1)S(1)} %bitcast.38, bf16[2,128,512]{2,1,0:T(8,128)(2,1)S(1)} %copy-done.3), custom_call_target="tpu_custom_call" | custom-call | tf_op jit(solution)/shard_map/pair_sums/pallas_call | solution.py:191
  (12 shorter events, 0.2 us)
Async XLA Ops:
  0.0 32.9 %copy-start = (f32[64]{0:T(128)S(1)}, f32[64]{0:T(128)}, u32[]{:S(2)}) copy-start(f32[64]{0:T(128)} %param.17) | copy-start | bytes 772
  1.2 1.6 %copy-start.1 = (bf16[4,1024,256]{2,1,0:T(8,128)(2,1)S(1)}, bf16[4,1024,256]{2,1,0:T(8,128)(2,1)}, u32[]{:S(2)}) copy-start(bf16[4,1024,256]{2,1,0:T(8,128)(2,1)} %constant.131.clone.t2) | copy-start | bytes 6291460
  2.8 0.9 copy-start.4
  3.7 0.9 copy-start.5
  4.6 0.7 copy-start.8
  17.7 12.9 %copy-start.11 = (s32[2048]{0:T(1024)S(1)}, s32[2048]{0:T(1024)}, u32[]{:S(2)}) copy-start(s32[2048]{0:T(1024)} %param.20) | copy-start | bytes 24580
  17.7 13.2 %copy-start.10 = (s32[30720]{0:T(1024)S(1)}, s32[30720]{0:T(1024)}, u32[]{:S(2)}) copy-start(s32[30720]{0:T(1024)} %param.19) | copy-start | bytes 368644
  17.7 15.2 %copy-start.9 = (s32[1,32]{1,0:T(1,128)S(1)}, s32[1,32]{1,0:T(1,128)}, u32[]{:S(2)}) copy-start(s32[1,32]{1,0:T(1,128)} %param.16) | copy-start | bytes 388
  17.7 63.0 %all-to-all-start = ((bf16[32,8,4096]{2,1,0:T(8,128)(2,1)}), bf16[32,8,4096]{2,1,0:T(8,128)(2,1)S(1)}, u32[]{:S(2)}, u32[]{:S(2)}) async-start(bf16[32,8,4096]{2,1,0:T(8,128)(2,1)} %bitcast.7), calls=%async_computation | async-start | bytes 4194304 | tf_op jit(solution)/shard_map/all_to_all | solution.py:206
  30.6 50.1 %copy-start.6 = (bf16[256,256]{1,0:T(8,128)(2,1)S(1)}, bf16[256,256]{1,0:T(8,128)(2,1)}, u32[]{:S(2)}) copy-start(bf16[256,256]{1,0:T(8,128)(2,1)} %constant.133.clone.t1) | copy-start | bytes 393220
  30.6 50.1 %copy-start.7 = (bf16[512,128]{1,0:T(8,128)(2,1)S(1)}, bf16[512,128]{1,0:T(8,128)(2,1)}, u32[]{:S(2)}) copy-start(bf16[512,128]{1,0:T(8,128)(2,1)} %constant.135.clone.pick) | copy-start | bytes 393220
  80.7 1.6 %copy-start.2 = (bf16[1024,1024]{1,0:T(8,128)(2,1)S(1)}, bf16[1024,1024]{1,0:T(8,128)(2,1)}, u32[]{:S(2)}) copy-start(bf16[1024,1024]{1,0:T(8,128)(2,1)} %constant.134.clone.lp) | copy-start | bytes 6291460
  87.3 39.8 %copy-start.3 = (bf16[2,128,512]{2,1,0:T(8,128)(2,1)S(1)}, bf16[2,128,512]{2,1,0:T(8,128)(2,1)}, u32[]{:S(2)}) copy-start(bf16[2,128,512]{2,1,0:T(8,128)(2,1)} %constant.136.clone.turn) | copy-start | bytes 786436

commit v2 on v1

--- a/solution.py
+++ b/solution.py
@@ -40,7 +40,20 @@
                     perm[((g_*GC+cc)*PL+s)*2+o, ((cc*PL+s)*2+o)*GR+g_]=1
     return [np.asarray(t,np.float32).astype(ml_dtypes.bfloat16) for t in (t3,t2,perm)]
 
-def kern_a(bands, v0,v1,v2,v3, cond, t3, t2, perm, out, vs, third):
+def kern_a(bands, v0, v1, v2, v3, cnd, t3_hbm, t2_hbm, perm_hbm, out, vs, third, cond, t3, t2, perm, sems):
+    first = pl.program_id(0) == 0
+    loads = [pltpu.make_async_copy(a, b, sems.at[k]) for k, (a, b) in enumerate(((t3_hbm, t3), (t2_hbm, t2), (perm_hbm, perm)))]
+
+    @pl.when(first)
+    def _():
+        for load in loads:
+            load.start()
+        for i in range(2):
+            vs[i] = cnd[i].astype(jnp.float32)
+            for s in range(PL):
+                cond[i, s] = vs[i, pl.ds(s, NG, stride=PL), :]
+        loads[0].wait()
+
     for j,v in enumerate((v0,v1,v2,v3)):
         vs[0]=v[0,0].astype(jnp.float32)
         vs[1]=v[1,0].astype(jnp.float32)
@@ -57,6 +70,11 @@
             d=jnp.concatenate(rows,axis=0)
             th=lax.dot_general(t3[...],d,NT,preferred_element_type=jnp.float32)
             third[j,sp]=th.astype(BF)
+    @pl.when(first)
+    def _():
+        loads[1].wait()
+        loads[2].wait()
+
     ys=[]
     for c in range(GC):
         lhs=[]
@@ -75,16 +93,16 @@
 def stage_a(valence, cond, bands):
     nval=valence.shape[1]
     v=jnp.transpose(valence.reshape(2,nval,PL,NG,NG),(0,1,3,2,4)).reshape(2,nval,NG*PL,NG)
-    cf=cond.reshape(2,PL,NG,NG).astype(jnp.float32)
+    cf=jnp.transpose(cond.reshape(2,PL,NG,NG),(0,2,1,3)).reshape(2,NG*PL,NG)
     t3,t2,perm=tables()
     def vspec(j):
         return pl.BlockSpec((2,1,NG*PL,NG),lambda q,b: (0,b[q*J+j],0,0))
     full=lambda shape: pl.BlockSpec(shape,lambda q,b:(0,)*len(shape))
     return pl.pallas_call(kern_a,
         grid_spec=pltpu.PrefetchScalarGridSpec(num_scalar_prefetch=1,grid=(bands.shape[0]//J,),
-            in_specs=[vspec(j) for j in range(J)]+[full((2,PL,NG,NG)),full((256,256)),full((GC,1024,256)),full((256,256))],
+            in_specs=[vspec(j) for j in range(J)]+[full((2,NG*PL,NG))]+[pl.BlockSpec(memory_space=pltpu.HBM)]*3,
             out_specs=pl.BlockSpec((256,512),lambda q,b:(0,q)),
-            scratch_shapes=[pltpu.VMEM((2,NG*PL,NG),jnp.float32),pltpu.VMEM((J,PL//2,256,256),BF)]),
+            scratch_shapes=[pltpu.VMEM((2,NG*PL,NG),jnp.float32),pltpu.VMEM((J,PL//2,256,256),BF),pltpu.VMEM((2,PL,NG,NG),jnp.float32),pltpu.VMEM((256,256),BF),pltpu.VMEM((GC,1024,256),BF),pltpu.VMEM((256,256),BF),pltpu.SemaphoreType.DMA((3,))]),
         out_shape=jax.ShapeDtypeStruct((256,bands.shape[0]//J*512),BF),
         compiler_params=pltpu.CompilerParams(vmem_limit_bytes=48*2**20),
         name="partial_transform")(bands,v,v,v,v,cf,t3,t2,perm)
@@ -110,10 +128,14 @@
     pick=pick.reshape(512,128)
     return [np.asarray(t,np.float32).astype(ml_dtypes.bfloat16) for t in (t1,lp,pick)]
 
-def kern_c(place, x, t1, lp, pick, mask, weight, rows_out, cols_out, field, found):
+def kern_c(place, x, t1, lp_hbm, pick, mask, weight, rows_out, cols_out, field, found, lp, sem):
+    load = pltpu.make_async_copy(lp_hbm, lp, sem)
+    load.start()
     for w in range(PL):
         xw=jnp.concatenate([x[:,(q*PL+w)*NG:(q*PL+w+1)*NG] for q in range(8)],axis=1)
         e=jnp.dot(t1[...],xw,preferred_element_type=jnp.float32).astype(BF)
+        if w==0:
+            load.wait()
         f=jnp.dot(e,lp[...],preferred_element_type=jnp.float32)
         for t in range(8):
             field[(w*8+t)*256:(w*8+t+1)*256,:]=f[:,t*NG:(t+1)*NG]
@@ -150,55 +172,83 @@
     t1,lp,pick=tables_c()
     vm=pl.BlockSpec(memory_space=pltpu.VMEM)
     return pl.pallas_call(kern_c,
-        in_specs=[pl.BlockSpec(memory_space=pltpu.SMEM)]+[vm]*6,
+        in_specs=[pl.BlockSpec(memory_space=pltpu.SMEM)]+[vm,vm,pl.BlockSpec(memory_space=pltpu.HBM),vm,vm,vm],
         out_specs=[vm,vm],
         out_shape=[jax.ShapeDtypeStruct((ROWS,NG),BF),jax.ShapeDtypeStruct((COLS,NG),BF)],
-        scratch_shapes=[pltpu.VMEM((PL*8*256,NG),jnp.float32),pltpu.VMEM((4*PTS,NG),jnp.float32)],
+        scratch_shapes=[pltpu.VMEM((PL*8*256,NG),jnp.float32),pltpu.VMEM((4*PTS,NG),jnp.float32),pltpu.VMEM((1024,1024),BF),pltpu.SemaphoreType.DMA],
         compiler_params=pltpu.CompilerParams(vmem_limit_bytes=48*2**20),
         name="last_transform")(place,moved,t1,lp,pick,mask,wl)
 
 def tables_d():
     q=np.zeros((2,2,2,PAIRS,2,2,2,2,PAIRS))
-    for hc in range(2):
-        for hr in range(2):
+    for b in range(2):
+        for h in range(2):
             for p in range(PAIRS):
-                q[hc,hc,0,p,hr,0,hr,0,p]=1
-                q[hc,hc,1,p,hr,0,hr,1,p]=1
-                q[hc,hc,1,p,hr,1,hr,0,p]=-1
-                q[hc,hc,0,p,hr,1,hr,1,p]=1
-    q=q.reshape(2,128,512)
-    return np.asarray(q,np.float32).astype(ml_dtypes.bfloat16)
-
-def kern_d(rows, cols, turn, out, rhs):
-    for p in range(8):
-        s=cols[p]
-        for hc in range(2):
-            v=jnp.dot(s,turn[hc],preferred_element_type=jnp.float32)
-            for pb in range(4):
-                piece=jnp.concatenate([v[(g*4+pb)*8:(g*4+pb+1)*8] for g in range(8)],axis=0).astype(BF)
-                for k in range(4):
-                    rhs[k,(hc*4+pb)*64:(hc*4+pb+1)*64,p*NG:(p+1)*NG]=piece[:,k*NG:(k+1)*NG]
-    lhs=jnp.concatenate([rows[p] for p in range(8)],axis=1)
+                q[b,h,0,p,h,0,b,0,p]=1
+                q[b,h,1,p,h,0,b,1,p]=1
+                q[b,h,1,p,h,1,b,0,p]=1
+                q[b,h,0,p,h,1,b,1,p]=-1
+    return np.asarray(q.reshape(256,512),np.float32).astype(ml_dtypes.bfloat16)
+
+def kern_d(order, rows, cols, turn, out, slab):
+    @pl.when(pl.program_id(0) == 0)
+    def _():
+        for pp in range(4):
+            a=cols[2*pp].astype(jnp.float32)
+            b=cols[2*pp+1].astype(jnp.float32)
+            for h in range(2):
+                v=jnp.concatenate([a[:,h*64:(h+1)*64],b[:,h*64:(h+1)*64]],axis=1)
+                v=jnp.concatenate([v[(g*4+pb)*8:(g*4+pb+1)*8] for pb in range(4) for g in range(8)],axis=0)
+                slab[h*256:(h+1)*256,pp*NG:(pp+1)*NG]=v.astype(BF)
+    turned=[]
+    for pp in range(4):
+        pair=jnp.concatenate([rows[0,order[4+2*pp+k]] for k in range(2)],axis=1)
+        turned.append(jnp.dot(pair,turn[...],preferred_element_type=jnp.float32).astype(BF))
+    lhs=jnp.concatenate([jnp.concatenate([t[:,k*NG:(k+1)*NG] for t in turned],axis=1) for k in range(4)],axis=0)
+    z=lax.dot_general(lhs,slab[...],NT,preferred_element_type=jnp.float32)
     for hr in range(2):
         n=64 if hr==0 else 56
         for o in range(2):
-            z=lax.dot_general(lhs,rhs[hr*2+o],NT,preferred_element_type=jnp.float32)
-            for c in range(4):
-                out[o,c*120+64*hr:c*120+64*hr+n,:]=z[c*64:c*64+n]
-
-def stage_d(rows, cols):
-    vm=pl.BlockSpec(memory_space=pltpu.VMEM)
+            k=hr*2+o
+            out[o,0,64*hr:64*hr+n,:]=z[k*64:k*64+n]
+
+def stage_d(order, rows, cols):
     return pl.pallas_call(kern_d,
-        in_specs=[vm]*3,out_specs=vm,
-        out_shape=jax.ShapeDtypeStruct((2,480,512),jnp.float32),
-        scratch_shapes=[pltpu.VMEM((4,512,1024),BF)],
-        compiler_params=pltpu.CompilerParams(vmem_limit_bytes=48*2**20),
-        name="pair_sums")(rows,cols,tables_d())
+        grid_spec=pltpu.PrefetchScalarGridSpec(num_scalar_prefetch=1,grid=(4,),
+            in_specs=[pl.BlockSpec((1,8,64,NG),lambda c,o:(o[c],0,0,0)),
+                pl.BlockSpec((8,256,NG),lambda c,o:(0,0,0)),pl.BlockSpec((256,512),lambda c,o:(0,0))],
+            out_specs=pl.BlockSpec((2,1,120,512),lambda c,o:(0,c,0,0)),
+            scratch_shapes=[pltpu.VMEM((512,512),BF)]),
+        out_shape=jax.ShapeDtypeStruct((2,4,120,512),jnp.float32),
+        compiler_params=pltpu.CompilerParams(vmem_limit_bytes=32*2**20),
+        name="pair_sums")(order,rows,cols,tables_d()).reshape(2,480,512)
+
+def at(x, k, axis):
+    return lax.dynamic_index_in_dim(x, k, axis, False)
+
+
+def spread_rows(rows, pair_at, gcol_at):
+    x_at, y_at = pair_at % 4, pair_at // 4
+    both = ("pair", "gcol")
+    got = [at(rows, x_at, 1)]
+    for d in range(1, 4):
+        perm = [(y * 4 + x, y * 4 + (x + d) % 4) for y in range(2) for x in range(4)]
+        got.append(lax.ppermute(at(rows, (x_at + d) % 4, 1), "pair", perm))
+    got = jnp.stack(got, axis=1)
+    own, other = at(got, y_at, 0), at(got, 1 - y_at, 0)
+
+    def swap(block, flip_pair, flip_gcol):
+        return lax.ppermute(block, both, [(k, k ^ (flip_pair * 4 + flip_gcol)) for k in range(32)])
+
+    block = jnp.stack([own, swap(other, 4, 0), swap(own, 0, 2), swap(other, 4, 2)]).reshape(2, 8, 64, NG)
+    return jnp.concatenate([block, swap(block, 0, 1)])
+
 
 def on_device(valence, conduction, pair_bands, e_val, e_cond, g_index, slab_index):
     n_pair = lax.axis_size("pair")
     n_grow = lax.axis_size("grow")
     n_gcol = lax.axis_size("gcol")
+    pair_at = lax.axis_index("pair")
     grow_at = lax.axis_index("grow")
     gcol_at = lax.axis_index("gcol")
     bands = pair_bands.reshape(-1)
@@ -208,11 +258,14 @@
     gaps = jnp.take(e_val, bands) - e_cond[0]
     weight = 2.0 / (gaps * math.sqrt(PAIRS * n_pair))
     rows, cols = stage_c(moved.reshape(256, 4096), ids, weight)
-    rows = jnp.broadcast_to(rows.reshape(8, 1, 64, NG), (8, 4, 64, NG)).reshape(32, 64, NG)
-    rows = lax.all_to_all(rows, ("pair", "gcol"), 0, 0, tiled=True).reshape(8, 256, NG)
     cols = jnp.broadcast_to(cols[None], (64, COLS, NG))
     cols = lax.all_to_all(cols, ("pair", "grow"), 0, 0, tiled=True).reshape(8, 256, NG)
-    return stage_d(rows, cols)
+    rows = spread_rows(rows.reshape(2, 4, 64, NG), pair_at, gcol_at)
+    c = jnp.arange(4, dtype=jnp.int32)
+    blocks = (c % 2 ^ gcol_at % 2) * 2 + (c // 2 ^ gcol_at // 2)
+    p = jnp.arange(8, dtype=jnp.int32)
+    places = (p // 4 ^ pair_at // 4) * 4 + (pair_at - p) % 4
+    return stage_d(jnp.concatenate([blocks, places]).astype(jnp.int32), rows, cols)
 
 
 def solution(mesh):

time: 133 us -> 122 us (0.917); the launches traced: 131 us -> 122 us
  blocking collectives: 39.6 us -> 0 us
  starting transfers between devices: 12.9 us -> 29.6 us
  waiting for transfers between devices: 45.4 us -> 56.4 us
  Pallas kernels: 21.3 us -> 23.5 us
    all_to_all x2 -> x0, blocking collectives: 39.6 us -> none  [the longest x1 20.7 us: on_device(): lax.all_to_all(cols, ('pair', 'grow'), 0, 0, tiled=True).reshape(8, 256, NG)]
    ppermute x0 -> x7, waiting for transfers between devices: none -> 10.9 us  [the longest x4 5.6 us: swap(): lax.ppermute(block, both, [(k, k ^ flip_pair * 4 + flip_gcol) for k in ra...]
    all_to_all x0 -> x1, starting transfers between devices: none -> 8.75 us  [on_device(): lax.all_to_all(cols, ('pair', 'grow'), 0, 0, tiled=True).reshape(8, 256, NG)]
    ppermute x0 -> x7, starting transfers between devices: none -> 7.94 us  [the longest x4 4.48 us: swap(): lax.ppermute(block, both, [(k, k ^ flip_pair * 4 + flip_gcol) for k in ra...]
    pallas_call x1, Pallas kernels: 12.4 us -> 14.3 us  [stage_a(): pl.pallas_call(kern_a, grid_spec=pltpu.PrefetchScalarGridSpec(num_scalar_...]
    unnamed x24 -> x26, local copies, waits for them, and re-layouts: 5.68 us -> 6.65 us
  transfers between devices with their start and end apart: 1 -> 9, of which waited for: 1 -> 7; matrix products, arithmetic and copies ran while one was open for 3% -> 3% of each run, Pallas kernels for 0% -> 0%
where the time goes in v2:
time: 122 us
  waiting for transfers between devices  56.4 us (46%)
  starting transfers between devices  29.6 us (24%)
  Pallas kernels  23.5 us (19%)
  local copies, waits for them, and re-layouts  11.1 us (9%)
    all_to_all x1, waiting for transfers between devices, on_device(): lax.all_to_all(part.reshape(32, 8, 4096), ('grow', 'gcol'), 0, 0, tiled=T...  45.4 us
    pallas_call x1, Pallas kernels, stage_a(): pl.pallas_call(kern_a, grid_spec=pltpu.PrefetchScalarGridSpec(num_scalar_...  14.3 us
    all_to_all x1, starting transfers between devices, on_device(): lax.all_to_all(part.reshape(32, 8, 4096), ('grow', 'gcol'), 0, 0, tiled=T...  12.9 us
    all_to_all x1, starting transfers between devices, on_device(): lax.all_to_all(cols, ('pair', 'grow'), 0, 0, tiled=True).reshape(8, 256, NG)  8.75 us
    unnamed x26, local copies, waits for them, and re-layouts  6.65 us
    ppermute x4, waiting for transfers between devices, swap(): lax.ppermute(block, both, [(k, k ^ flip_pair * 4 + flip_gcol) for k in ra...  5.6 us
    ppermute x3, waiting for transfers between devices, spread_rows(): got.append(lax.ppermute(at(rows, (x_at + d) % 4, 1), 'pair', perm))  5.32 us
    pallas_call x1, Pallas kernels, stage_c(): pl.pallas_call(kern_c, in_specs=[pl.BlockSpec(memory_space=pltpu.SMEM)] +...  5.31 us
  transfers between devices with their start and end apart: 9, of which 7 were waited for; matrix products, arithmetic and copies ran while one was open for 3% of the time, Pallas kernels for 0%

profile of v2, /device:TPU:1, one launch (start us, length us, event | category | flops | bytes accessed | tf_op | source)
XLA Modules:
  0.0 122.0 jit_solution(6555501394170136066)
XLA Ops:
  0.0 1.6 %copy-done.1 = bf16[4,1024,256]{2,1,0:T(8,128)(2,1)S(1)} copy-done((bf16[4,1024,256]{2,1,0:T(8,128)(2,1)S(1)}, bf16[4,1024,256]{2,1,0:T(8,128)(2,1)}, u32[]{:S(2)}) %copy-start.1) | copy-done | bytes 2097176
  1.6 0.9 copy-done.3
  2.6 0.9 copy-done.5
  3.5 0.9 copy-done.6
  4.4 0.7 copy-done.9
  5.0 14.3 %partial_transform.1 = bf16[256,4096]{1,0:T(8,128)(2,1)} custom-call(s32[32]{0:T(128)S(1)} %bitcast.60, bf16[2,64,512,128]{3,2,1,0:T(8,128)(2,1)} %bitcast.61, bf16[2,64,512,128]{3,2,1,0:T(8,128)(2,1)} %bitcast.62, bf16[2,64,512,128]{3,2,1,0:T(8,128)(2,1)} %bitcast.63, bf16[2,64,512,128]{3,2,1,0:T(8,128)(2,1)} %bitcast.64, ...), custom_call_target="tpu_custom_call" | custom-call | tf_op jit(solution)/shard_map/partial_transform/pallas_call | solution.py:101
  19.3 0.0 copy-start.12
  19.3 0.0 copy-start.11
  19.3 0.0 copy-start.10
  19.3 12.9 %all-to-all-start = ((bf16[32,8,4096]{2,1,0:T(8,128)(2,1)}), bf16[32,8,4096]{2,1,0:T(8,128)(2,1)S(1)}, u32[]{:S(2)}, u32[]{:S(2)}) async-start(bf16[32,8,4096]{2,1,0:T(8,128)(2,1)} %bitcast.10), calls=%async_computation | async-start | bytes 4194304 | tf_op jit(solution)/shard_map/all_to_all | solution.py:256
  32.2 0.0 copy-start.7
  32.2 0.0 copy-start.8
  32.3 0.1 reshape.198
  32.4 0.1 reshape_squeeze.3
  32.5 0.3 reshape.194
  32.8 0.2 slice_reduce_fusion
  33.0 0.1 reshape.195
  33.1 0.1 pad_add_fusion.1
  33.2 0.1 reshape.196
  33.2 0.1 reshape.197
  33.4 0.1 copy.28
  33.5 0.2 concatenate.31
  33.7 0.1 copy.31
  34.6 0.7 gather_fusion
  35.3 0.1 reshape_tile.3.weight
  35.4 1.4 %eq.34 = s32[544,2,128]{2,1,0:T(2,128)S(1)} broadcast(s32[544,2]{1,0:T(8,128)S(1)} %copy.31), dimensions={0,1} | broadcast | bytes 561408 | tf_op jit(solution)/shard_map/eq | solution.py:170
  36.8 0.1 fusion.mask
  36.9 45.4 %all-to-all-done = bf16[32,8,4096]{2,1,0:T(8,128)(2,1)S(1)} async-done(((bf16[32,8,4096]{2,1,0:T(8,128)(2,1)}), bf16[32,8,4096]{2,1,0:T(8,128)(2,1)S(1)}, u32[]{:S(2)}, u32[]{:S(2)}) %all-to-all-start) | async-done | bytes 2097184 | tf_op jit(solution)/shard_map/all_to_all | solution.py:256
  82.3 1.6 %copy-done.2 = bf16[1024,1024]{1,0:T(8,128)(2,1)S(1)} copy-done((bf16[1024,1024]{1,0:T(8,128)(2,1)S(1)}, bf16[1024,1024]{1,0:T(8,128)(2,1)}, u32[]{:S(2)}) %copy-start.2) | copy-done | bytes 2097176
  83.9 5.3 %last_transform.1 = (bf16[512,128]{1,0:T(8,128)(2,1)S(1)}, bf16[32,128]{1,0:T(8,128)(2,1)S(1)}) custom-call(s32[1088]{0:T(1024)S(1)} %fusion.4.place, bf16[256,4096]{1,0:T(8,128)(2,1)S(1)} %bitcast.56, bf16[256,256]{1,0:T(8,128)(2,1)S(1)} %copy-done.7, bf16[1024,1024]{1,0:T(8,128)(2,1)S(1)} %copy-done.2, bf16[512,128]{1,0:T(8,128)(2,1)S(1)} %copy-done.8, ...), custom_call_target="tpu_custom_call" | custom-call | tf_op jit(solution)/shard_map/last_transform/pallas_call | solution.py:174
  89.2 0.0 copy-start.4
  89.2 0.9 broadcast_in_dim.11
  90.1 8.8 %all-to-all-start.1 = ((bf16[64,32,128]{2,1,0:T(8,128)(2,1)}), bf16[64,32,128]{2,1,0:T(8,128)(2,1)S(1)}, u32[]{:S(2)}, u32[]{:S(2)}) async-start(bf16[64,32,128]{2,1,0:T(8,128)(2,1)} %broadcast_in_dim.11), calls=%async_computation.1 | async-start | bytes 1048576 | tf_op jit(solution)/shard_map/all_to_all | solution.py:262
  98.9 2.3 %collective-permute-start.2 = (bf16[2,64,128]{2,1,0:T(8,128)(2,1)S(1)}, bf16[2,64,128]{2,1,0:T(8,128)(2,1)S(1)}, u32[]{:S(2)}, u32[]{:S(2)}) collective-permute-start(bf16[2,64,128]{2,1,0:T(8,128)(2,1)S(1)} %get-tuple-element.12), channel_id=1, source_target_pairs={{0,96},{32,0},{64,32},{96,64},{128,224},{160,128},{192,160},{224,1... | collective-permute-start | bytes 98312 | tf_op jit(solution)/shard_map/ppermute | solution.py:236
  101.3 0.5 collective-permute-start.1
  101.8 0.6 collective-permute-start
  102.4 4.8 %collective-permute-done.1 = bf16[2,64,128]{2,1,0:T(8,128)(2,1)S(1)} collective-permute-done((bf16[2,64,128]{2,1,0:T(8,128)(2,1)S(1)}, bf16[2,64,128]{2,1,0:T(8,128)(2,1)S(1)}, u32[]{:S(2)}, u32[]{:S(2)}) %collective-permute-start.1) | collective-permute-done | bytes 32800 | tf_op jit(solution)/shard_map/ppermute | solution.py:236
  107.2 0.6 collective-permute-done
  107.8 0.3 collective-permute-start.5
  108.1 3.0 %collective-permute-start.4 = (bf16[4,64,128]{2,1,0:T(8,128)(2,1)S(1)}, bf16[4,64,128]{2,1,0:T(8,128)(2,1)S(1)}, u32[]{:S(2)}, u32[]{:S(2)}) collective-permute-start(bf16[4,64,128]{2,1,0:T(8,128)(2,1)S(1)} %bitcast.68), channel_id=1, source_target_pairs={{0,2},{1,3},{2,0},{3,1},{32,34},{33,35},{34,32},{35,33},{64,66},{6... | collective-permute-start | bytes 196616 | tf_op jit(solution)/shard_map/ppermute | solution.py:241
  111.1 0.1 collective-permute-start.3
  111.1 1.4 %collective-permute-done.5 = bf16[4,64,128]{2,1,0:T(8,128)(2,1)S(1)} collective-permute-done((bf16[4,64,128]{2,1,0:T(8,128)(2,1)S(1)}, bf16[4,64,128]{2,1,0:T(8,128)(2,1)S(1)}, u32[]{:S(2)}, u32[]{:S(2)}) %collective-permute-start.5) | collective-permute-done | bytes 65568 | tf_op jit(solution)/shard_map/ppermute | solution.py:241
  112.5 1.2 %collective-permute-done.4 = bf16[4,64,128]{2,1,0:T(8,128)(2,1)S(1)} collective-permute-done((bf16[4,64,128]{2,1,0:T(8,128)(2,1)S(1)}, bf16[4,64,128]{2,1,0:T(8,128)(2,1)S(1)}, u32[]{:S(2)}, u32[]{:S(2)}) %collective-permute-start.4) | collective-permute-done | bytes 65568 | tf_op jit(solution)/shard_map/ppermute | solution.py:241
  113.7 1.9 %collective-permute-done.3 = bf16[4,64,128]{2,1,0:T(8,128)(2,1)S(1)} collective-permute-done((bf16[4,64,128]{2,1,0:T(8,128)(2,1)S(1)}, bf16[4,64,128]{2,1,0:T(8,128)(2,1)S(1)}, u32[]{:S(2)}, u32[]{:S(2)}) %collective-permute-start.3) | collective-permute-done | bytes 65568 | tf_op jit(solution)/shard_map/ppermute | solution.py:241
  115.7 1.1 collective-permute-start.6
  116.9 0.1 pad_add_fusion.2.order
  116.9 1.1 collective-permute-done.6
  118.1 3.9 %pair_sums.1 = f32[2,4,120,512]{3,2,1,0:T(8,128)} custom-call(s32[12]{0:T(128)S(1)} %pad_add_fusion.2.order, bf16[4,8,64,128]{3,2,1,0:T(8,128)(2,1)S(1)} %pad_maximum_fusion.rows, bf16[8,256,128]{2,1,0:T(8,128)(2,1)S(1)} %bitcast.57, bf16[256,512]{1,0:T(8,128)(2,1)S(1)} %copy-done.4), custom_call_target="tpu_custom_call" | custom-call | tf_op jit(solution)/shard_map/pair_sums/pallas_call | solution.py:216
  (34 shorter events, 0.3 us)
Async XLA Ops:
  0.0 34.6 %copy-start = (f32[64]{0:T(128)S(1)}, f32[64]{0:T(128)}, u32[]{:S(2)}) copy-start(f32[64]{0:T(128)} %param.17) | copy-start | bytes 772
  0.0 1.6 %copy-start.1 = (bf16[4,1024,256]{2,1,0:T(8,128)(2,1)S(1)}, bf16[4,1024,256]{2,1,0:T(8,128)(2,1)}, u32[]{:S(2)}) copy-start(bf16[4,1024,256]{2,1,0:T(8,128)(2,1)} %constant.240.clone.t2_hbm) | copy-start | bytes 6291460
  1.6 0.9 copy-start.3
  2.6 0.9 copy-start.5
  3.5 0.9 copy-start.6
  4.4 0.7 copy-start.9
  19.3 13.0 %copy-start.12 = (s32[2048]{0:T(1024)S(1)}, s32[2048]{0:T(1024)}, u32[]{:S(2)}) copy-start(s32[2048]{0:T(1024)} %param.20) | copy-start | bytes 24580
  19.3 13.2 %copy-start.11 = (s32[30720]{0:T(1024)S(1)}, s32[30720]{0:T(1024)}, u32[]{:S(2)}) copy-start(s32[30720]{0:T(1024)} %param.19) | copy-start | bytes 368644
  19.3 15.2 %copy-start.10 = (s32[1,32]{1,0:T(1,128)S(1)}, s32[1,32]{1,0:T(1,128)}, u32[]{:S(2)}) copy-start(s32[1,32]{1,0:T(1,128)} %param.16) | copy-start | bytes 388
  19.3 63.0 %all-to-all-start = ((bf16[32,8,4096]{2,1,0:T(8,128)(2,1)}), bf16[32,8,4096]{2,1,0:T(8,128)(2,1)S(1)}, u32[]{:S(2)}, u32[]{:S(2)}) async-start(bf16[32,8,4096]{2,1,0:T(8,128)(2,1)} %bitcast.10), calls=%async_computation | async-start | bytes 4194304 | tf_op jit(solution)/shard_map/all_to_all | solution.py:256
  32.2 50.1 %copy-start.7 = (bf16[256,256]{1,0:T(8,128)(2,1)S(1)}, bf16[256,256]{1,0:T(8,128)(2,1)}, u32[]{:S(2)}) copy-start(bf16[256,256]{1,0:T(8,128)(2,1)} %constant.242.clone.t1) | copy-start | bytes 393220
  32.2 50.1 %copy-start.8 = (bf16[512,128]{1,0:T(8,128)(2,1)S(1)}, bf16[512,128]{1,0:T(8,128)(2,1)}, u32[]{:S(2)}) copy-start(bf16[512,128]{1,0:T(8,128)(2,1)} %constant.244.clone.pick) | copy-start | bytes 393220
  82.3 1.6 %copy-start.2 = (bf16[1024,1024]{1,0:T(8,128)(2,1)S(1)}, bf16[1024,1024]{1,0:T(8,128)(2,1)}, u32[]{:S(2)}) copy-start(bf16[1024,1024]{1,0:T(8,128)(2,1)} %constant.243.clone.lp_hbm) | copy-start | bytes 6291460
  89.2 28.9 %copy-start.4 = (bf16[256,512]{1,0:T(8,128)(2,1)S(1)}, bf16[256,512]{1,0:T(8,128)(2,1)}, u32[]{:S(2)}) copy-start(bf16[256,512]{1,0:T(8,128)(2,1)} %constant.245.clone.turn) | copy-start | bytes 786436
  90.1 28.0 %all-to-all-start.1 = ((bf16[64,32,128]{2,1,0:T(8,128)(2,1)}), bf16[64,32,128]{2,1,0:T(8,128)(2,1)S(1)}, u32[]{:S(2)}, u32[]{:S(2)}) async-start(bf16[64,32,128]{2,1,0:T(8,128)(2,1)} %broadcast_in_dim.11), calls=%async_computation.1 | async-start | bytes 1048576 | tf_op jit(solution)/shard_map/all_to_all | solution.py:262
  98.9 3.5 %collective-permute-start.2 = (bf16[2,64,128]{2,1,0:T(8,128)(2,1)S(1)}, bf16[2,64,128]{2,1,0:T(8,128)(2,1)S(1)}, u32[]{:S(2)}, u32[]{:S(2)}) collective-permute-start(bf16[2,64,128]{2,1,0:T(8,128)(2,1)S(1)} %get-tuple-element.12), channel_id=1, source_target_pairs={{0,96},{32,0},{64,32},{96,64},{128,224},{160,128},{192,160},{224,1... | collective-permute-start | bytes 98312 | tf_op jit(solution)/shard_map/ppermute | solution.py:236
  101.3 5.9 %collective-permute-start.1 = (bf16[2,64,128]{2,1,0:T(8,128)(2,1)S(1)}, bf16[2,64,128]{2,1,0:T(8,128)(2,1)S(1)}, u32[]{:S(2)}, u32[]{:S(2)}) collective-permute-start(bf16[2,64,128]{2,1,0:T(8,128)(2,1)S(1)} %get-tuple-element.13), channel_id=1, source_target_pairs={{0,64},{32,96},{64,0},{96,32},{128,192},{160,224},{192,128},{224,1... | collective-permute-start | bytes 98312 | tf_op jit(solution)/shard_map/ppermute | solution.py:236
  101.8 5.9 %collective-permute-start = (bf16[2,64,128]{2,1,0:T(8,128)(2,1)S(1)}, bf16[2,64,128]{2,1,0:T(8,128)(2,1)S(1)}, u32[]{:S(2)}, u32[]{:S(2)}) collective-permute-start(bf16[2,64,128]{2,1,0:T(8,128)(2,1)S(1)} %get-tuple-element.14), channel_id=1, source_target_pairs={{0,32},{32,64},{64,96},{96,0},{128,160},{160,192},{192,224},{224,1... | collective-permute-start | bytes 98312 | tf_op jit(solution)/shard_map/ppermute | solution.py:236
  107.8 4.7 %collective-permute-start.5 = (bf16[4,64,128]{2,1,0:T(8,128)(2,1)S(1)}, bf16[4,64,128]{2,1,0:T(8,128)(2,1)S(1)}, u32[]{:S(2)}, u32[]{:S(2)}) collective-permute-start(bf16[4,64,128]{2,1,0:T(8,128)(2,1)S(1)} %get-tuple-element.10), channel_id=1, source_target_pairs={{0,130},{1,131},{2,128},{3,129},{32,162},{33,163},{34,160},{35,161... | collective-permute-start | bytes 196616 | tf_op jit(solution)/shard_map/ppermute | solution.py:241
  108.1 5.7 %collective-permute-start.4 = (bf16[4,64,128]{2,1,0:T(8,128)(2,1)S(1)}, bf16[4,64,128]{2,1,0:T(8,128)(2,1)S(1)}, u32[]{:S(2)}, u32[]{:S(2)}) collective-permute-start(bf16[4,64,128]{2,1,0:T(8,128)(2,1)S(1)} %bitcast.68), channel_id=1, source_target_pairs={{0,2},{1,3},{2,0},{3,1},{32,34},{33,35},{34,32},{35,33},{64,66},{6... | collective-permute-start | bytes 196616 | tf_op jit(solution)/shard_map/ppermute | solution.py:241
  111.1 4.6 %collective-permute-start.3 = (bf16[4,64,128]{2,1,0:T(8,128)(2,1)S(1)}, bf16[4,64,128]{2,1,0:T(8,128)(2,1)S(1)}, u32[]{:S(2)}, u32[]{:S(2)}) collective-permute-start(bf16[4,64,128]{2,1,0:T(8,128)(2,1)S(1)} %get-tuple-element.10), channel_id=1, source_target_pairs={{0,128},{1,129},{2,130},{3,131},{32,160},{33,161},{34,162},{35,163... | collective-permute-start | bytes 196616 | tf_op jit(solution)/shard_map/ppermute | solution.py:241
  115.7 2.3 %collective-permute-start.6 = (bf16[2,8,64,128]{3,2,1,0:T(8,128)(2,1)S(1)}, bf16[2,8,64,128]{3,2,1,0:T(8,128)(2,1)S(1)}, u32[]{:S(2)}, u32[]{:S(2)}) collective-permute-start(bf16[2,8,64,128]{3,2,1,0:T(8,128)(2,1)S(1)} %bitcast.66), channel_id=1, source_target_pairs={{0,1},{1,0},{2,3},{3,2},{32,33},{33,32},{34,35},{35,34},{64,65},{6... | collective-permute-start | bytes 786440 | tf_op jit(solution)/shard_map/ppermute | solution.py:241

commit v3 on v2

--- a/solution.py
+++ b/solution.py
@@ -8,6 +8,9 @@
 from jax.experimental import pallas as pl
 from jax.experimental.pallas import tpu as pltpu
 BF=jnp.bfloat16
+VM_A=62
+CH=64
+Q=4
 NG=128; GR=8; GC=4; PL=4; QW=32; PAIRS=32; J=4
 NT=(((1,),(1,)),((),()))
 NN=(((1,),(0,)),((),()))
@@ -23,15 +26,14 @@
     q3=((g*GC+c)*PL+w).reshape(-1)
     co,si=cs(q3,ar)
     t3=np.block([[co,si],[-si,co]])
-    t2=np.zeros((GC,J,2,NG,2,J,QW))
+    t2=np.zeros((GC,2,NG,2,J,QW))
     for cc in range(GC):
         co,si=cs(cc*QW+np.arange(QW),ar)
-        for j in range(J):
-            t2[cc,j,0,:,0,j,:]=co.T
-            t2[cc,j,1,:,0,j,:]=si.T
-            t2[cc,j,0,:,1,j,:]=-si.T
-            t2[cc,j,1,:,1,j,:]=co.T
-    t2=t2.reshape(GC,J*2*NG,2*J*QW)
+        t2[cc,0,:,0]=co.T[:,None]
+        t2[cc,1,:,0]=si.T[:,None]
+        t2[cc,0,:,1]=-si.T[:,None]
+        t2[cc,1,:,1]=co.T[:,None]
+    t2=t2.reshape(GC,2*NG,2*J*QW)
     perm=np.zeros((256,256))
     for cc in range(GC):
         for s in range(PL):
@@ -40,74 +42,89 @@
                     perm[((g_*GC+cc)*PL+s)*2+o, ((cc*PL+s)*2+o)*GR+g_]=1
     return [np.asarray(t,np.float32).astype(ml_dtypes.bfloat16) for t in (t3,t2,perm)]
 
-def kern_a(bands, v0, v1, v2, v3, cnd, t3_hbm, t2_hbm, perm_hbm, out, vs, third, cond, t3, t2, perm, sems):
-    first = pl.program_id(0) == 0
-    loads = [pltpu.make_async_copy(a, b, sems.at[k]) for k, (a, b) in enumerate(((t3_hbm, t3), (t2_hbm, t2), (perm_hbm, perm)))]
+def kern_a(bands, val, cnd, t3, t2_hbm, perm_hbm, out, vbuf, dens, third, cond, t2_all, t2, perm, sems, vsems):
+    step = pl.program_id(0)
+    first = step == 0
+    loads = [pltpu.make_async_copy(a, b, sems.at[k]) for k, (a, b) in enumerate(((t2_hbm, t2_all), (perm_hbm, perm)))]
+
+    def band_load(k):
+        return pltpu.make_async_copy(val.at[:, bands[k]], vbuf.at[k], vsems.at[k])
+
+    @pl.when(first)
+    def _():
+        for k in range(Q*J):
+            band_load(k).start()
+        for load in loads:
+            load.start()
+        cond[...] = cnd[...].astype(jnp.float32)
+
+    @pl.when(step < PAIRS//(Q*J) - 1)
+    def _():
+        for k in range(Q*J):
+            band_load((step+1)*Q*J+k).start()
+
+    for j in range(Q*J):
+        k = step*Q*J+j
+        band_load(k).wait()
+        for r in range(0, NG*PL, CH):
+            cr = cond[0, r:r+CH]
+            ci = cond[1, r:r+CH]
+            vr = vbuf[k, 0, r:r+CH].astype(jnp.float32)
+            vi = vbuf[k, 1, r:r+CH].astype(jnp.float32)
+            dens[j, 0, r:r+CH] = vr*cr+vi*ci
+            dens[j, 1, r:r+CH] = vr*ci-vi*cr
+    for j in range(Q*J):
+        for sp in range(PL//2):
+            rows = []
+            for s in (2*sp, 2*sp+1):
+                rows.append(jnp.concatenate([dens[j, i, pl.ds(s, NG, stride=PL), :].astype(BF) for i in range(2)], axis=1))
+            d = jnp.concatenate(rows, axis=0)
+            th = lax.dot_general(t3[...], d, NT, preferred_element_type=jnp.float32)
+            third[j, sp] = th.astype(BF)
 
     @pl.when(first)
     def _():
         for load in loads:
-            load.start()
-        for i in range(2):
-            vs[i] = cnd[i].astype(jnp.float32)
-            for s in range(PL):
-                cond[i, s] = vs[i, pl.ds(s, NG, stride=PL), :]
-        loads[0].wait()
-
-    for j,v in enumerate((v0,v1,v2,v3)):
-        vs[0]=v[0,0].astype(jnp.float32)
-        vs[1]=v[1,0].astype(jnp.float32)
-        for sp in range(PL//2):
-            rows=[]
-            for s in (2*sp,2*sp+1):
-                vr=vs[0,pl.ds(s,NG,stride=PL),:]
-                vi=vs[1,pl.ds(s,NG,stride=PL),:]
-                cr=cond[0,s]
-                ci=cond[1,s]
-                re=vr*cr+vi*ci
-                im=vr*ci-vi*cr
-                rows.append(jnp.concatenate([re.astype(BF),im.astype(BF)],axis=1))
-            d=jnp.concatenate(rows,axis=0)
-            th=lax.dot_general(t3[...],d,NT,preferred_element_type=jnp.float32)
-            third[j,sp]=th.astype(BF)
-    @pl.when(first)
-    def _():
-        loads[1].wait()
-        loads[2].wait()
+            load.wait()
+        part = lax.broadcasted_iota(jnp.int32, (2*NG, 2*J*QW), 1) // QW % J
+        for c in range(GC):
+            for j in range(J):
+                t2[c, j*2*NG:(j+1)*2*NG] = jnp.where(part == j, t2_all[c].astype(jnp.float32), 0.0).astype(BF)
 
     ys=[]
     for c in range(GC):
         lhs=[]
-        for s in range(PL):
-            lhs.append(jnp.concatenate([third[j,s//2,i*NG+c*QW:i*NG+(c+1)*QW,(s%2)*NG:(s%2+1)*NG] for j in range(J) for i in range(2)],axis=1))
+        for q in range(Q):
+            for s in range(PL):
+                lhs.append(jnp.concatenate([third[q*J+j,s//2,i*NG+c*QW:i*NG+(c+1)*QW,(s%2)*NG:(s%2+1)*NG] for j in range(J) for i in range(2)],axis=1))
         lhs=jnp.concatenate(lhs,axis=0)
         ys.append(jnp.dot(lhs,t2[c],preferred_element_type=jnp.float32))
-    for wp in range(PL//2):
-        cols=[]
-        for w in (2*wp,2*wp+1):
-            pieces=[ys[c][s*QW+w*GR:s*QW+(w+1)*GR,o*NG:(o+1)*NG] for c in range(GC) for s in range(PL) for o in range(2)]
-            cols.append(jnp.concatenate(pieces,axis=0).astype(BF))
-        y=jnp.concatenate(cols,axis=1)
-        out[:,wp*256:(wp+1)*256]=jnp.dot(perm[...],y,preferred_element_type=jnp.float32).astype(BF)
+    for q in range(Q):
+        for wp in range(PL//2):
+            cols=[]
+            for w in (2*wp,2*wp+1):
+                pieces=[ys[c][(q*PL+s)*QW+w*GR:(q*PL+s)*QW+(w+1)*GR,o*NG:(o+1)*NG] for c in range(GC) for s in range(PL) for o in range(2)]
+                cols.append(jnp.concatenate(pieces,axis=0).astype(BF))
+            y=jnp.concatenate(cols,axis=1)
+            out[:,(q*2+wp)*256:(q*2+wp+1)*256]=jnp.dot(perm[...],y,preferred_element_type=jnp.float32).astype(BF)
 
 def stage_a(valence, cond, bands):
     nval=valence.shape[1]
     v=jnp.transpose(valence.reshape(2,nval,PL,NG,NG),(0,1,3,2,4)).reshape(2,nval,NG*PL,NG)
     cf=jnp.transpose(cond.reshape(2,PL,NG,NG),(0,2,1,3)).reshape(2,NG*PL,NG)
     t3,t2,perm=tables()
-    def vspec(j):
-        return pl.BlockSpec((2,1,NG*PL,NG),lambda q,b: (0,b[q*J+j],0,0))
     full=lambda shape: pl.BlockSpec(shape,lambda q,b:(0,)*len(shape))
     return pl.pallas_call(kern_a,
-        grid_spec=pltpu.PrefetchScalarGridSpec(num_scalar_prefetch=1,grid=(bands.shape[0]//J,),
-            in_specs=[vspec(j) for j in range(J)]+[full((2,NG*PL,NG))]+[pl.BlockSpec(memory_space=pltpu.HBM)]*3,
-            out_specs=pl.BlockSpec((256,512),lambda q,b:(0,q)),
-            scratch_shapes=[pltpu.VMEM((2,NG*PL,NG),jnp.float32),pltpu.VMEM((J,PL//2,256,256),BF),pltpu.VMEM((2,PL,NG,NG),jnp.float32),pltpu.VMEM((256,256),BF),pltpu.VMEM((GC,1024,256),BF),pltpu.VMEM((256,256),BF),pltpu.SemaphoreType.DMA((3,))]),
+        grid_spec=pltpu.PrefetchScalarGridSpec(num_scalar_prefetch=1,grid=(bands.shape[0]//(Q*J),),
+            in_specs=[pl.BlockSpec(memory_space=pltpu.HBM),full((2,NG*PL,NG)),full((256,256))]+[pl.BlockSpec(memory_space=pltpu.HBM)]*2,
+            out_specs=pl.BlockSpec((256,512*Q),lambda q,b:(0,q)),
+            scratch_shapes=[pltpu.VMEM((PAIRS,2,NG*PL,NG),BF),pltpu.VMEM((Q*J,2,NG*PL,NG),jnp.float32),pltpu.VMEM((Q*J,PL//2,256,256),BF),pltpu.VMEM((2,NG*PL,NG),jnp.float32),
+                pltpu.VMEM((GC,256,256),BF),pltpu.VMEM((GC,1024,256),BF),pltpu.VMEM((256,256),BF),pltpu.SemaphoreType.DMA((2,)),pltpu.SemaphoreType.DMA((PAIRS,))]),
         out_shape=jax.ShapeDtypeStruct((256,bands.shape[0]//J*512),BF),
-        compiler_params=pltpu.CompilerParams(vmem_limit_bytes=48*2**20),
-        name="partial_transform")(bands,v,v,v,v,cf,t3,t2,perm)
-
-ROWS=GR*64; COLS=32; PTS=ROWS+COLS
+        compiler_params=pltpu.CompilerParams(vmem_limit_bytes=VM_A*2**20),
+        name="partial_transform")(bands,v,cf,t3,t2,perm)
+
+ROWS=GR*64; COLS=32; COPIES=64; PTS=ROWS+COLS
 
 def tables_c():
     ar=np.arange(NG)
@@ -115,43 +132,40 @@
     t1=np.zeros((NG,2,NG,2))
     t1[:,0,:,0]=co; t1[:,0,:,1]=si; t1[:,1,:,0]=-si; t1[:,1,:,1]=co
     t1=t1.reshape(256,256)
-    lp=np.zeros((PAIRS,QW,QW,PAIRS))
-    for p in range(PAIRS):
-        for q in range(QW):
-            lp[p,q,q,p]=1
-    lp=lp.reshape(1024,1024)
     pick=np.zeros((2,2,4,PAIRS,2,2,PAIRS))
     for h in range(2):
         for o in range(2):
             for p in range(PAIRS):
                 pick[h,o,:,p,h,o,p]=1
     pick=pick.reshape(512,128)
-    return [np.asarray(t,np.float32).astype(ml_dtypes.bfloat16) for t in (t1,lp,pick)]
-
-def kern_c(place, x, t1, lp_hbm, pick, mask, weight, rows_out, cols_out, field, found, lp, sem):
-    load = pltpu.make_async_copy(lp_hbm, lp, sem)
-    load.start()
+    return [np.asarray(t,np.float32).astype(ml_dtypes.bfloat16) for t in (t1,pick)]
+
+def kern_c(place, x, t1, lp, pick, mask, weight, rows_out, cols_hbm, field, found, cols, sem):
     for w in range(PL):
         xw=jnp.concatenate([x[:,(q*PL+w)*NG:(q*PL+w+1)*NG] for q in range(8)],axis=1)
         e=jnp.dot(t1[...],xw,preferred_element_type=jnp.float32).astype(BF)
-        if w==0:
-            load.wait()
         f=jnp.dot(e,lp[...],preferred_element_type=jnp.float32)
         for t in range(8):
             field[(w*8+t)*256:(w*8+t+1)*256,:]=f[:,t*NG:(t+1)*NG]
-    def body(r,carry):
+
+    def find(first, last):
+        def body(r,carry):
+            for h in range(2):
+                at=pl.multiple_of(place[2*r+h],2)
+                found[pl.ds(pl.multiple_of(4*r+2*h,2),2),:]=field[pl.ds(at,2),:]
+            return carry
+        lax.fori_loop(first,last,body,0,unroll=8)
+        parts=[]
         for h in range(2):
-            at=pl.multiple_of(place[2*r+h],2)
-            found[pl.ds(pl.multiple_of(4*r+2*h,2),2),:]=field[pl.ds(at,2),:]
-        return carry
-    lax.fori_loop(0,PTS,body,0,unroll=8)
-    parts=[]
-    for h in range(2):
-        for o in range(2):
-            parts.append(found[pl.ds(2*h+o,PTS,stride=4),:].astype(BF)*mask[:,h*NG:(h+1)*NG])
-    got=jnp.dot(jnp.concatenate(parts,axis=1),pick[...],preferred_element_type=jnp.float32)
-    rows_out[...]=(got[:ROWS]*weight[...]).astype(BF)
-    cols_out[...]=got[ROWS:].astype(BF)
+            for o in range(2):
+                parts.append(found[pl.ds(4*first+2*h+o,last-first,stride=4),:].astype(BF)*mask[first:last,h*NG:(h+1)*NG])
+        return jnp.dot(jnp.concatenate(parts,axis=1),pick[...],preferred_element_type=jnp.float32)
+
+    cols[...]=jnp.broadcast_to(find(ROWS,PTS).astype(BF)[None],(COPIES,COLS,NG))
+    send=pltpu.make_async_copy(cols,cols_hbm,sem)
+    send.start()
+    rows_out[...]=(find(0,ROWS)*weight[...]).astype(BF)
+    send.wait()
 
 def point_lists(g_index, slab_index, n_pair,n_grow,n_gcol,grow_at,gcol_at):
     rc=g_index.shape[0]//(n_pair*n_grow*n_gcol)
@@ -169,14 +183,17 @@
     lane=jnp.arange(NG,dtype=jnp.int32)//PAIRS
     mask=((q2%4)[:,:,None]==lane).astype(BF).reshape(PTS,2*NG)
     wl=jnp.tile(weight,4).reshape(1,NG)
-    t1,lp,pick=tables_c()
+    t1,pick=tables_c()
+    r=lax.broadcasted_iota(jnp.int32,(1024,1024),0)
+    l=lax.broadcasted_iota(jnp.int32,(1024,1024),1)
+    lp=((r//QW==l%PAIRS)&(r%QW==l//PAIRS)).astype(BF)
     vm=pl.BlockSpec(memory_space=pltpu.VMEM)
     return pl.pallas_call(kern_c,
-        in_specs=[pl.BlockSpec(memory_space=pltpu.SMEM)]+[vm,vm,pl.BlockSpec(memory_space=pltpu.HBM),vm,vm,vm],
-        out_specs=[vm,vm],
-        out_shape=[jax.ShapeDtypeStruct((ROWS,NG),BF),jax.ShapeDtypeStruct((COLS,NG),BF)],
-        scratch_shapes=[pltpu.VMEM((PL*8*256,NG),jnp.float32),pltpu.VMEM((4*PTS,NG),jnp.float32),pltpu.VMEM((1024,1024),BF),pltpu.SemaphoreType.DMA],
-        compiler_params=pltpu.CompilerParams(vmem_limit_bytes=48*2**20),
+        in_specs=[pl.BlockSpec(memory_space=pltpu.SMEM)]+[vm]*6,
+        out_specs=[vm,pl.BlockSpec(memory_space=pltpu.HBM)],
+        out_shape=[jax.ShapeDtypeStruct((ROWS,NG),BF),jax.ShapeDtypeStruct((COPIES,COLS,NG),BF)],
+        scratch_shapes=[pltpu.VMEM((PL*8*256,NG),jnp.float32),pltpu.VMEM((4*PTS,NG),jnp.float32),pltpu.VMEM((COPIES,COLS,NG),BF),pltpu.SemaphoreType.DMA],
+        compiler_params=pltpu.CompilerParams(vmem_limit_bytes=40*2**20),
         name="last_transform")(place,moved,t1,lp,pick,mask,wl)
 
 def tables_d():
@@ -258,7 +275,6 @@
     gaps = jnp.take(e_val, bands) - e_cond[0]
     weight = 2.0 / (gaps * math.sqrt(PAIRS * n_pair))
     rows, cols = stage_c(moved.reshape(256, 4096), ids, weight)
-    cols = jnp.broadcast_to(cols[None], (64, COLS, NG))
     cols = lax.all_to_all(cols, ("pair", "grow"), 0, 0, tiled=True).reshape(8, 256, NG)
     rows = spread_rows(rows.reshape(2, 4, 64, NG), pair_at, gcol_at)
     c = jnp.arange(4, dtype=jnp.int32)

time: 122 us -> 116 us (0.951)
  local copies, waits for them, and re-layouts: 11.1 us -> 5.25 us
  waiting for transfers between devices: 56.4 us -> 53.7 us
  other arithmetic: 0.42 us -> 3.09 us
    unnamed x26 -> x16, local copies, waits for them, and re-layouts: 6.65 us -> 1.64 us
    convert_element_type x0 -> x1, other arithmetic: none -> 2.65 us  [stage_c(): lp = ((r // QW == l % PAIRS) & (r % QW == l // PAIRS)).astype(BF)]
    all_to_all x1, waiting for transfers between devices: 45.4 us -> 42.8 us  [on_device(): lax.all_to_all(part.reshape(32, 8, 4096), ('grow', 'gcol'), 0, 0, tiled=T...]
    pallas_call x1, Pallas kernels: 14.3 us -> 12.8 us  [stage_a(): pl.pallas_call(kern_a, grid_spec=pltpu.PrefetchScalarGridSpec(num_scalar_...]
  transfers between devices with their start and end apart: 9 -> 9, of which waited for: 7 -> 7; matrix products, arithmetic and copies ran while one was open for 3% -> 6% of each run, Pallas kernels for 0% -> 0%
where the time goes in v3:
time: 116 us
  waiting for transfers between devices  53.7 us (46%)
  starting transfers between devices  29.7 us (26%)
  Pallas kernels  22.9 us (20%)
  local copies, waits for them, and re-layouts  5.25 us (5%)
  other arithmetic  3.09 us (3%)
    all_to_all x1, waiting for transfers between devices, on_device(): lax.all_to_all(part.reshape(32, 8, 4096), ('grow', 'gcol'), 0, 0, tiled=T...  42.8 us
    all_to_all x1, starting transfers between devices, on_device(): lax.all_to_all(part.reshape(32, 8, 4096), ('grow', 'gcol'), 0, 0, tiled=T...  13 us
    pallas_call x1, Pallas kernels, stage_a(): pl.pallas_call(kern_a, grid_spec=pltpu.PrefetchScalarGridSpec(num_scalar_...  12.8 us
    all_to_all x1, starting transfers between devices, on_device(): lax.all_to_all(cols, ('pair', 'grow'), 0, 0, tiled=True).reshape(8, 256, NG)  8.76 us
    pallas_call x1, Pallas kernels, stage_c(): pl.pallas_call(kern_c, in_specs=[pl.BlockSpec(memory_space=pltpu.SMEM)] +...  6.19 us
    ppermute x4, waiting for transfers between devices, swap(): lax.ppermute(block, both, [(k, k ^ flip_pair * 4 + flip_gcol) for k in ra...  5.58 us
    ppermute x3, waiting for transfers between devices, spread_rows(): got.append(lax.ppermute(at(rows, (x_at + d) % 4, 1), 'pair', perm))  5.33 us
    ppermute x4, starting transfers between devices, swap(): lax.ppermute(block, both, [(k, k ^ flip_pair * 4 + flip_gcol) for k in ra...  4.49 us
  transfers between devices with their start and end apart: 9, of which 7 were waited for; matrix products, arithmetic and copies ran while one was open for 6% of the time, Pallas kernels for 0%

profile of v3, /device:TPU:1, one launch (start us, length us, event | category | flops | bytes accessed | tf_op | source)
XLA Modules:
  0.0 115.7 jit_solution(5144246723760289091)
XLA Ops:
  0.0 0.0 copy-start
  0.0 12.8 %partial_transform.1 = bf16[256,4096]{1,0:T(8,128)(2,1)} custom-call(s32[32]{0:T(128)} %bitcast.75, bf16[2,64,512,128]{3,2,1,0:T(8,128)(2,1)} %bitcast.58, bf16[2,512,128]{2,1,0:T(8,128)(2,1)} %bitcast.63, bf16[256,256]{1,0:T(8,128)(2,1)} %constant.271.clone.t3, bf16[4,256,256]{2,1,0:T(8,128)(2,1)} %constant.272.clone.t2_hbm, ...), custom_call_target="tpu_custom_call" | custom-call | tf_op jit(solution)/shard_map/partial_transform/pallas_call | solution.py:117
  12.8 0.0 copy-start.6
  12.9 0.0 copy-start.5
  12.9 0.0 copy-start.7
  12.9 0.0 copy-start.3
  12.9 0.0 copy-start.4
  12.9 13.0 %all-to-all-start = ((bf16[32,8,4096]{2,1,0:T(8,128)(2,1)}), bf16[32,8,4096]{2,1,0:T(8,128)(2,1)}, u32[]{:S(2)}, u32[]{:S(2)}) async-start(bf16[32,8,4096]{2,1,0:T(8,128)(2,1)} %bitcast.59), calls=%async_computation | async-start | bytes 4194304 | tf_op jit(solution)/shard_map/all_to_all | solution.py:273
  25.9 0.1 reshape.197
  26.0 0.1 reshape_squeeze.3
  26.1 0.3 reshape.193
  26.4 0.2 slice_reduce_fusion
  26.6 0.1 reshape.194
  26.7 0.1 pad_add_fusion.1
  26.8 0.1 reshape.195
  26.9 0.1 reshape.196
  27.0 0.1 copy.27
  27.1 0.2 concatenate.31
  27.3 0.1 copy.30
  28.1 0.0 copy-done.7
  28.2 0.0 copy-done
  28.2 0.7 gather_fusion
  28.9 0.1 reshape_tile.3.weight
  29.1 1.4 %eq.45 = s32[544,2,128]{2,1,0:T(2,128)S(1)} broadcast(s32[544,2]{1,0:T(8,128)S(1)} %copy.30), dimensions={0,1} | broadcast | bytes 561408 | tf_op jit(solution)/shard_map/eq | solution.py:184
  30.5 0.1 fusion.2.mask
  30.5 0.0 copy-start.2
  30.5 2.7 %fusion.1.lp = bf16[1024,1024]{1,0:T(8,128)(2,1)} fusion(s32[1024]{0:T(1024)S(1)} %get-tuple-element.17, s32[1024]{0:T(1024)S(1)} %get-tuple-element.20, s32[1024]{0:T(1024)S(1)} %get-tuple-element.18, s32[1024]{0:T(1024)S(1)} %get-tuple-element.19, pred[1024]{0:T(1024)(128)(4,1)S(1)} %get-tuple-element.21, pred[1024]{0:T(1024)(128)(4,1)S(1)} %get-tuple-element.22), kind=kLoop, calls=%fused_computation.4 | loop fusion | flops 8388608 | bytes 2115584 | tf_op jit(solution)/shard_map/convert_element_type | solution.py:189
  33.2 42.8 %all-to-all-done = bf16[32,8,4096]{2,1,0:T(8,128)(2,1)} async-done(((bf16[32,8,4096]{2,1,0:T(8,128)(2,1)}), bf16[32,8,4096]{2,1,0:T(8,128)(2,1)}, u32[]{:S(2)}, u32[]{:S(2)}) %all-to-all-start) | async-done | bytes 2097184 | tf_op jit(solution)/shard_map/all_to_all | solution.py:273
  76.0 1.6 %copy-done.1 = bf16[1024,1024]{1,0:T(8,128)(2,1)S(1)} copy-done((bf16[1024,1024]{1,0:T(8,128)(2,1)S(1)}, bf16[1024,1024]{1,0:T(8,128)(2,1)}, u32[]{:S(2)}) %copy-start.1) | copy-done | bytes 2097176
  77.6 6.2 %last_transform.1 = (bf16[512,128]{1,0:T(8,128)(2,1)S(1)}, bf16[64,32,128]{2,1,0:T(8,128)(2,1)}) custom-call(s32[1088]{0:T(1024)S(1)} %fusion.6.place, bf16[256,4096]{1,0:T(8,128)(2,1)} %bitcast.11.x, bf16[256,256]{1,0:T(8,128)(2,1)S(1)} %copy-done.3, bf16[1024,1024]{1,0:T(8,128)(2,1)S(1)} %copy-done.1, bf16[512,128]{1,0:T(8,128)(2,1)S(1)} %copy-done.4, ...), custom_call_target="tpu_custom_call" | custom-call | tf_op jit(solution)/shard_map/last_transform/pallas_call | solution.py:191
  83.8 8.8 %all-to-all-start.1 = ((bf16[64,32,128]{2,1,0:T(8,128)(2,1)}), bf16[64,32,128]{2,1,0:T(8,128)(2,1)S(1)}, u32[]{:S(2)}, u32[]{:S(2)}) async-start(bf16[64,32,128]{2,1,0:T(8,128)(2,1)} %get-tuple-element.8), calls=%async_computation.1 | async-start | bytes 1048576 | tf_op jit(solution)/shard_map/all_to_all | solution.py:278
  92.6 2.3 %collective-permute-start.2 = (bf16[2,64,128]{2,1,0:T(8,128)(2,1)S(1)}, bf16[2,64,128]{2,1,0:T(8,128)(2,1)S(1)}, u32[]{:S(2)}, u32[]{:S(2)}) collective-permute-start(bf16[2,64,128]{2,1,0:T(8,128)(2,1)S(1)} %get-tuple-element.12), channel_id=1, source_target_pairs={{0,96},{32,0},{64,32},{96,64},{128,224},{160,128},{192,160},{224,1... | collective-permute-start | bytes 98312 | tf_op jit(solution)/shard_map/ppermute | solution.py:253
  95.0 0.5 collective-permute-start.1
  95.5 0.6 collective-permute-start
  96.1 0.0 collective-permute-done.2
  96.1 4.7 %collective-permute-done.1 = bf16[2,64,128]{2,1,0:T(8,128)(2,1)S(1)} collective-permute-done((bf16[2,64,128]{2,1,0:T(8,128)(2,1)S(1)}, bf16[2,64,128]{2,1,0:T(8,128)(2,1)S(1)}, u32[]{:S(2)}, u32[]{:S(2)}) %collective-permute-start.1) | collective-permute-done | bytes 32800 | tf_op jit(solution)/shard_map/ppermute | solution.py:253
  100.8 0.6 collective-permute-done
  101.5 0.3 collective-permute-start.5
  101.8 3.0 %collective-permute-start.4 = (bf16[4,64,128]{2,1,0:T(8,128)(2,1)S(1)}, bf16[4,64,128]{2,1,0:T(8,128)(2,1)S(1)}, u32[]{:S(2)}, u32[]{:S(2)}) collective-permute-start(bf16[4,64,128]{2,1,0:T(8,128)(2,1)S(1)} %bitcast.64), channel_id=1, source_target_pairs={{0,2},{1,3},{2,0},{3,1},{32,34},{33,35},{34,32},{35,33},{64,66},{6... | collective-permute-start | bytes 196616 | tf_op jit(solution)/shard_map/ppermute | solution.py:258
  104.8 0.1 collective-permute-start.3
  104.8 1.4 %collective-permute-done.5 = bf16[4,64,128]{2,1,0:T(8,128)(2,1)S(1)} collective-permute-done((bf16[4,64,128]{2,1,0:T(8,128)(2,1)S(1)}, bf16[4,64,128]{2,1,0:T(8,128)(2,1)S(1)}, u32[]{:S(2)}, u32[]{:S(2)}) %collective-permute-start.5) | collective-permute-done | bytes 65568 | tf_op jit(solution)/shard_map/ppermute | solution.py:258
  106.2 1.2 %collective-permute-done.4 = bf16[4,64,128]{2,1,0:T(8,128)(2,1)S(1)} collective-permute-done((bf16[4,64,128]{2,1,0:T(8,128)(2,1)S(1)}, bf16[4,64,128]{2,1,0:T(8,128)(2,1)S(1)}, u32[]{:S(2)}, u32[]{:S(2)}) %collective-permute-start.4) | collective-permute-done | bytes 65568 | tf_op jit(solution)/shard_map/ppermute | solution.py:258
  107.4 1.9 %collective-permute-done.3 = bf16[4,64,128]{2,1,0:T(8,128)(2,1)S(1)} collective-permute-done((bf16[4,64,128]{2,1,0:T(8,128)(2,1)S(1)}, bf16[4,64,128]{2,1,0:T(8,128)(2,1)S(1)}, u32[]{:S(2)}, u32[]{:S(2)}) %collective-permute-start.3) | collective-permute-done | bytes 65568 | tf_op jit(solution)/shard_map/ppermute | solution.py:258
  109.4 1.1 collective-permute-start.6
  110.6 0.1 pad_add_fusion.2.order
  110.6 1.1 collective-permute-done.6
  111.7 0.0 all-to-all-done.1
  111.8 3.9 %pair_sums.1 = f32[2,4,120,512]{3,2,1,0:T(8,128)} custom-call(s32[12]{0:T(128)S(1)} %pad_add_fusion.2.order, bf16[4,8,64,128]{3,2,1,0:T(8,128)(2,1)S(1)} %pad_maximum_fusion.rows, bf16[8,256,128]{2,1,0:T(8,128)(2,1)S(1)} %bitcast.56, bf16[256,512]{1,0:T(8,128)(2,1)S(1)} %copy-done.2), custom_call_target="tpu_custom_call" | custom-call | tf_op jit(solution)/shard_map/pair_sums/pallas_call | solution.py:233
  (27 shorter events, 0.3 us)
Async XLA Ops:
  0.0 28.2 %copy-start = (f32[64]{0:T(128)S(1)}, f32[64]{0:T(128)}, u32[]{:S(2)}) copy-start(f32[64]{0:T(128)} %param.16) | copy-start | bytes 772
  12.8 13.0 %copy-start.6 = (s32[2048]{0:T(1024)S(1)}, s32[2048]{0:T(1024)}, u32[]{:S(2)}) copy-start(s32[2048]{0:T(1024)} %param.19) | copy-start | bytes 24580
  12.9 13.3 %copy-start.5 = (s32[30720]{0:T(1024)S(1)}, s32[30720]{0:T(1024)}, u32[]{:S(2)}) copy-start(s32[30720]{0:T(1024)} %param.18) | copy-start | bytes 368644
  12.9 15.3 %copy-start.7 = (s32[1,32]{1,0:T(1,128)S(1)}, s32[1,32]{1,0:T(1,128)}, u32[]{:S(2)}) copy-start(s32[1,32]{1,0:T(1,128)} %param.15) | copy-start | bytes 388
  12.9 63.1 %copy-start.3 = (bf16[256,256]{1,0:T(8,128)(2,1)S(1)}, bf16[256,256]{1,0:T(8,128)(2,1)}, u32[]{:S(2)}) copy-start(bf16[256,256]{1,0:T(8,128)(2,1)} %constant.274.clone.t1) | copy-start | bytes 393220
  12.9 63.1 %copy-start.4 = (bf16[512,128]{1,0:T(8,128)(2,1)S(1)}, bf16[512,128]{1,0:T(8,128)(2,1)}, u32[]{:S(2)}) copy-start(bf16[512,128]{1,0:T(8,128)(2,1)} %constant.275.clone.pick) | copy-start | bytes 393220
  12.9 63.1 %all-to-all-start = ((bf16[32,8,4096]{2,1,0:T(8,128)(2,1)}), bf16[32,8,4096]{2,1,0:T(8,128)(2,1)}, u32[]{:S(2)}, u32[]{:S(2)}) async-start(bf16[32,8,4096]{2,1,0:T(8,128)(2,1)} %bitcast.59), calls=%async_computation | async-start | bytes 4194304 | tf_op jit(solution)/shard_map/all_to_all | solution.py:273
  30.5 81.2 %copy-start.2 = (bf16[256,512]{1,0:T(8,128)(2,1)S(1)}, bf16[256,512]{1,0:T(8,128)(2,1)}, u32[]{:S(2)}) copy-start(bf16[256,512]{1,0:T(8,128)(2,1)} %constant.276.clone.turn) | copy-start | bytes 786436
  76.0 1.6 %copy-start.1 = (bf16[1024,1024]{1,0:T(8,128)(2,1)S(1)}, bf16[1024,1024]{1,0:T(8,128)(2,1)}, u32[]{:S(2)}) copy-start(bf16[1024,1024]{1,0:T(8,128)(2,1)} %fusion.1.lp) | copy-start | bytes 6291460
  83.8 28.0 %all-to-all-start.1 = ((bf16[64,32,128]{2,1,0:T(8,128)(2,1)}), bf16[64,32,128]{2,1,0:T(8,128)(2,1)S(1)}, u32[]{:S(2)}, u32[]{:S(2)}) async-start(bf16[64,32,128]{2,1,0:T(8,128)(2,1)} %get-tuple-element.8), calls=%async_computation.1 | async-start | bytes 1048576 | tf_op jit(solution)/shard_map/all_to_all | solution.py:278
  92.6 3.5 %collective-permute-start.2 = (bf16[2,64,128]{2,1,0:T(8,128)(2,1)S(1)}, bf16[2,64,128]{2,1,0:T(8,128)(2,1)S(1)}, u32[]{:S(2)}, u32[]{:S(2)}) collective-permute-start(bf16[2,64,128]{2,1,0:T(8,128)(2,1)S(1)} %get-tuple-element.12), channel_id=1, source_target_pairs={{0,96},{32,0},{64,32},{96,64},{128,224},{160,128},{192,160},{224,1... | collective-permute-start | bytes 98312 | tf_op jit(solution)/shard_map/ppermute | solution.py:253
  95.0 5.8 %collective-permute-start.1 = (bf16[2,64,128]{2,1,0:T(8,128)(2,1)S(1)}, bf16[2,64,128]{2,1,0:T(8,128)(2,1)S(1)}, u32[]{:S(2)}, u32[]{:S(2)}) collective-permute-start(bf16[2,64,128]{2,1,0:T(8,128)(2,1)S(1)} %get-tuple-element.13), channel_id=1, source_target_pairs={{0,64},{32,96},{64,0},{96,32},{128,192},{160,224},{192,128},{224,1... | collective-permute-start | bytes 98312 | tf_op jit(solution)/shard_map/ppermute | solution.py:253
  95.5 5.9 %collective-permute-start = (bf16[2,64,128]{2,1,0:T(8,128)(2,1)S(1)}, bf16[2,64,128]{2,1,0:T(8,128)(2,1)S(1)}, u32[]{:S(2)}, u32[]{:S(2)}) collective-permute-start(bf16[2,64,128]{2,1,0:T(8,128)(2,1)S(1)} %get-tuple-element.14), channel_id=1, source_target_pairs={{0,32},{32,64},{64,96},{96,0},{128,160},{160,192},{192,224},{224,1... | collective-permute-start | bytes 98312 | tf_op jit(solution)/shard_map/ppermute | solution.py:253
  101.5 4.7 %collective-permute-start.5 = (bf16[4,64,128]{2,1,0:T(8,128)(2,1)S(1)}, bf16[4,64,128]{2,1,0:T(8,128)(2,1)S(1)}, u32[]{:S(2)}, u32[]{:S(2)}) collective-permute-start(bf16[4,64,128]{2,1,0:T(8,128)(2,1)S(1)} %get-tuple-element.10), channel_id=1, source_target_pairs={{0,130},{1,131},{2,128},{3,129},{32,162},{33,163},{34,160},{35,161... | collective-permute-start | bytes 196616 | tf_op jit(solution)/shard_map/ppermute | solution.py:258
  101.8 5.7 %collective-permute-start.4 = (bf16[4,64,128]{2,1,0:T(8,128)(2,1)S(1)}, bf16[4,64,128]{2,1,0:T(8,128)(2,1)S(1)}, u32[]{:S(2)}, u32[]{:S(2)}) collective-permute-start(bf16[4,64,128]{2,1,0:T(8,128)(2,1)S(1)} %bitcast.64), channel_id=1, source_target_pairs={{0,2},{1,3},{2,0},{3,1},{32,34},{33,35},{34,32},{35,33},{64,66},{6... | collective-permute-start | bytes 196616 | tf_op jit(solution)/shard_map/ppermute | solution.py:258
  104.8 4.6 %collective-permute-start.3 = (bf16[4,64,128]{2,1,0:T(8,128)(2,1)S(1)}, bf16[4,64,128]{2,1,0:T(8,128)(2,1)S(1)}, u32[]{:S(2)}, u32[]{:S(2)}) collective-permute-start(bf16[4,64,128]{2,1,0:T(8,128)(2,1)S(1)} %get-tuple-element.10), channel_id=1, source_target_pairs={{0,128},{1,129},{2,130},{3,131},{32,160},{33,161},{34,162},{35,163... | collective-permute-start | bytes 196616 | tf_op jit(solution)/shard_map/ppermute | solution.py:258
  109.4 2.3 %collective-permute-start.6 = (bf16[2,8,64,128]{3,2,1,0:T(8,128)(2,1)S(1)}, bf16[2,8,64,128]{3,2,1,0:T(8,128)(2,1)S(1)}, u32[]{:S(2)}, u32[]{:S(2)}) collective-permute-start(bf16[2,8,64,128]{3,2,1,0:T(8,128)(2,1)S(1)} %bitcast.61), channel_id=1, source_target_pairs={{0,1},{1,0},{2,3},{3,2},{32,33},{33,32},{34,35},{35,34},{64,65},{6... | collective-permute-start | bytes 786440 | tf_op jit(solution)/shard_map/ppermute | solution.py:258

commit v4 on v3

--- a/solution.py
+++ b/solution.py
@@ -26,13 +26,13 @@
     q3=((g*GC+c)*PL+w).reshape(-1)
     co,si=cs(q3,ar)
     t3=np.block([[co,si],[-si,co]])
-    t2=np.zeros((GC,2,NG,2,J,QW))
+    t2=np.zeros((GC,2,NG,2,QW,J))
     for cc in range(GC):
         co,si=cs(cc*QW+np.arange(QW),ar)
-        t2[cc,0,:,0]=co.T[:,None]
-        t2[cc,1,:,0]=si.T[:,None]
-        t2[cc,0,:,1]=-si.T[:,None]
-        t2[cc,1,:,1]=co.T[:,None]
+        t2[cc,0,:,0]=co.T[:,:,None]
+        t2[cc,1,:,0]=si.T[:,:,None]
+        t2[cc,0,:,1]=-si.T[:,:,None]
+        t2[cc,1,:,1]=co.T[:,:,None]
     t2=t2.reshape(GC,2*NG,2*J*QW)
     perm=np.zeros((256,256))
     for cc in range(GC):
@@ -42,21 +42,26 @@
                     perm[((g_*GC+cc)*PL+s)*2+o, ((cc*PL+s)*2+o)*GR+g_]=1
     return [np.asarray(t,np.float32).astype(ml_dtypes.bfloat16) for t in (t3,t2,perm)]
 
-def kern_a(bands, val, cnd, t3, t2_hbm, perm_hbm, out, vbuf, dens, third, cond, t2_all, t2, perm, sems, vsems):
+def kern_a(bands, val, cnd_hbm, t3_hbm, t2_hbm, perm_hbm, out, vbuf, dens, third, cnd, cond, t3, t2_all, t2, perm, sems, vsems):
     step = pl.program_id(0)
     first = step == 0
-    loads = [pltpu.make_async_copy(a, b, sems.at[k]) for k, (a, b) in enumerate(((t2_hbm, t2_all), (perm_hbm, perm)))]
+    loads = [pltpu.make_async_copy(a, b, sems.at[k]) for k, (a, b) in enumerate(((cnd_hbm, cnd), (t3_hbm, t3), (t2_hbm, t2_all), (perm_hbm, perm)))]
 
     def band_load(k):
         return pltpu.make_async_copy(val.at[:, bands[k]], vbuf.at[k], vsems.at[k])
 
     @pl.when(first)
     def _():
-        for k in range(Q*J):
+        loads[0].start()
+        band_load(0).start()
+        loads[1].start()
+        for k in range(1, Q*J):
             band_load(k).start()
-        for load in loads:
-            load.start()
+        loads[2].start()
+        loads[3].start()
+        loads[0].wait()
         cond[...] = cnd[...].astype(jnp.float32)
+        loads[1].wait()
 
     @pl.when(step < PAIRS//(Q*J) - 1)
     def _():
@@ -84,9 +89,9 @@
 
     @pl.when(first)
     def _():
-        for load in loads:
-            load.wait()
-        part = lax.broadcasted_iota(jnp.int32, (2*NG, 2*J*QW), 1) // QW % J
+        loads[2].wait()
+        loads[3].wait()
+        part = lax.broadcasted_iota(jnp.int32, (2*NG, 2*J*QW), 1) % J
         for c in range(GC):
             for j in range(J):
                 t2[c, j*2*NG:(j+1)*2*NG] = jnp.where(part == j, t2_all[c].astype(jnp.float32), 0.0).astype(BF)
@@ -108,18 +113,19 @@
             y=jnp.concatenate(cols,axis=1)
             out[:,(q*2+wp)*256:(q*2+wp+1)*256]=jnp.dot(perm[...],y,preferred_element_type=jnp.float32).astype(BF)
 
+
 def stage_a(valence, cond, bands):
     nval=valence.shape[1]
     v=jnp.transpose(valence.reshape(2,nval,PL,NG,NG),(0,1,3,2,4)).reshape(2,nval,NG*PL,NG)
     cf=jnp.transpose(cond.reshape(2,PL,NG,NG),(0,2,1,3)).reshape(2,NG*PL,NG)
     t3,t2,perm=tables()
-    full=lambda shape: pl.BlockSpec(shape,lambda q,b:(0,)*len(shape))
     return pl.pallas_call(kern_a,
         grid_spec=pltpu.PrefetchScalarGridSpec(num_scalar_prefetch=1,grid=(bands.shape[0]//(Q*J),),
-            in_specs=[pl.BlockSpec(memory_space=pltpu.HBM),full((2,NG*PL,NG)),full((256,256))]+[pl.BlockSpec(memory_space=pltpu.HBM)]*2,
+            in_specs=[pl.BlockSpec(memory_space=pltpu.HBM)]*5,
             out_specs=pl.BlockSpec((256,512*Q),lambda q,b:(0,q)),
-            scratch_shapes=[pltpu.VMEM((PAIRS,2,NG*PL,NG),BF),pltpu.VMEM((Q*J,2,NG*PL,NG),jnp.float32),pltpu.VMEM((Q*J,PL//2,256,256),BF),pltpu.VMEM((2,NG*PL,NG),jnp.float32),
-                pltpu.VMEM((GC,256,256),BF),pltpu.VMEM((GC,1024,256),BF),pltpu.VMEM((256,256),BF),pltpu.SemaphoreType.DMA((2,)),pltpu.SemaphoreType.DMA((PAIRS,))]),
+            scratch_shapes=[pltpu.VMEM((PAIRS,2,NG*PL,NG),BF),pltpu.VMEM((Q*J,2,NG*PL,NG),jnp.float32),pltpu.VMEM((Q*J,PL//2,256,256),BF),pltpu.VMEM((2,NG*PL,NG),BF),pltpu.VMEM((2,NG*PL,NG),jnp.float32),pltpu.VMEM((256,256),BF),
+                pltpu.VMEM((GC,256,256),BF),pltpu.VMEM((GC,1024,256),BF),pltpu.VMEM((256,256),BF),
+                pltpu.SemaphoreType.DMA((4,)),pltpu.SemaphoreType.DMA((PAIRS,))]),
         out_shape=jax.ShapeDtypeStruct((256,bands.shape[0]//J*512),BF),
         compiler_params=pltpu.CompilerParams(vmem_limit_bytes=VM_A*2**20),
         name="partial_transform")(bands,v,cf,t3,t2,perm)
@@ -132,21 +138,26 @@
     t1=np.zeros((NG,2,NG,2))
     t1[:,0,:,0]=co; t1[:,0,:,1]=si; t1[:,1,:,0]=-si; t1[:,1,:,1]=co
     t1=t1.reshape(256,256)
-    pick=np.zeros((2,2,4,PAIRS,2,2,PAIRS))
+    pick=np.zeros((2,2,8,4,J,2,2,8,J))
     for h in range(2):
         for o in range(2):
-            for p in range(PAIRS):
-                pick[h,o,:,p,h,o,p]=1
+            for q in range(8):
+                for j in range(J):
+                    pick[h,o,q,:,j,h,o,q,j]=1
     pick=pick.reshape(512,128)
     return [np.asarray(t,np.float32).astype(ml_dtypes.bfloat16) for t in (t1,pick)]
 
-def kern_c(place, x, t1, lp, pick, mask, weight, rows_out, cols_hbm, field, found, cols, sem):
+def kern_c(place, x, t1, pick, mask, weight, rows_out, cols_hbm, field, found, cols, sem):
+    group=lax.broadcasted_iota(jnp.int32,(256,NG),1)//16
     for w in range(PL):
         xw=jnp.concatenate([x[:,(q*PL+w)*NG:(q*PL+w+1)*NG] for q in range(8)],axis=1)
-        e=jnp.dot(t1[...],xw,preferred_element_type=jnp.float32).astype(BF)
-        f=jnp.dot(e,lp[...],preferred_element_type=jnp.float32)
+        f=jnp.dot(t1[...],xw,preferred_element_type=jnp.float32).astype(BF).astype(jnp.float32)
+        f=[f[:,t*NG:(t+1)*NG] for t in range(8)]
+        for k in (1,2,4):
+            low=group//k%2==0
+            f=[jnp.where(low,f[t],pltpu.roll(f[t^k],16*k,1)) if t&k==0 else jnp.where(low,pltpu.roll(f[t^k],NG-16*k,1),f[t]) for t in range(8)]
         for t in range(8):
-            field[(w*8+t)*256:(w*8+t+1)*256,:]=f[:,t*NG:(t+1)*NG]
+            field[(w*8+t)*256:(w*8+t+1)*256,:]=f[t]
 
     def find(first, last):
         def body(r,carry):
@@ -180,21 +191,18 @@
 def stage_c(moved, ids, weight):
     q1=ids//(NG*NG); q2=ids//NG%QW; w=ids%PL
     place=((w*8+q2//4)*256+2*q1).reshape(-1)
-    lane=jnp.arange(NG,dtype=jnp.int32)//PAIRS
+    lane=jnp.arange(NG,dtype=jnp.int32)//J%4
     mask=((q2%4)[:,:,None]==lane).astype(BF).reshape(PTS,2*NG)
     wl=jnp.tile(weight,4).reshape(1,NG)
     t1,pick=tables_c()
-    r=lax.broadcasted_iota(jnp.int32,(1024,1024),0)
-    l=lax.broadcasted_iota(jnp.int32,(1024,1024),1)
-    lp=((r//QW==l%PAIRS)&(r%QW==l//PAIRS)).astype(BF)
     vm=pl.BlockSpec(memory_space=pltpu.VMEM)
     return pl.pallas_call(kern_c,
-        in_specs=[pl.BlockSpec(memory_space=pltpu.SMEM)]+[vm]*6,
+        in_specs=[pl.BlockSpec(memory_space=pltpu.SMEM)]+[vm]*5,
         out_specs=[vm,pl.BlockSpec(memory_space=pltpu.HBM)],
         out_shape=[jax.ShapeDtypeStruct((ROWS,NG),BF),jax.ShapeDtypeStruct((COPIES,COLS,NG),BF)],
         scratch_shapes=[pltpu.VMEM((PL*8*256,NG),jnp.float32),pltpu.VMEM((4*PTS,NG),jnp.float32),pltpu.VMEM((COPIES,COLS,NG),BF),pltpu.SemaphoreType.DMA],
         compiler_params=pltpu.CompilerParams(vmem_limit_bytes=40*2**20),
-        name="last_transform")(place,moved,t1,lp,pick,mask,wl)
+        name="last_transform")(place,moved,t1,pick,mask,wl)
 
 def tables_d():
     q=np.zeros((2,2,2,PAIRS,2,2,2,2,PAIRS))

time: 116 us -> 114 us (0.983)
  waiting for transfers between devices: 53.7 us -> 56.4 us
  other arithmetic: 3.09 us -> 0.42 us
  local copies, waits for them, and re-layouts: 5.25 us -> 3.66 us
    all_to_all x1, waiting for transfers between devices: 42.8 us -> 45.5 us  [on_device(): lax.all_to_all(part.reshape(32, 8, 4096), ('grow', 'gcol'), 0, 0, tiled=T...]
    convert_element_type x1 -> x0, other arithmetic: 2.65 us -> none  [stage_c(): lp = ((r // QW == l % PAIRS) & (r % QW == l // PAIRS)).astype(BF)]
    unnamed x16 -> x14, local copies, waits for them, and re-layouts: 1.64 us -> 0.04 us
  transfers between devices with their start and end apart: 9 -> 9, of which waited for: 7 -> 7; matrix products, arithmetic and copies ran while one was open for 6% -> 4% of each run, Pallas kernels for 0% -> 0%
where the time goes in v4:
time: 114 us; the launch traced here: 113 us
  waiting for transfers between devices  56.4 us (49%)
  starting transfers between devices  29.8 us (26%)
  Pallas kernels  22 us (19%)
  local copies, waits for them, and re-layouts  3.66 us (3%)
    all_to_all x1, waiting for transfers between devices, on_device(): lax.all_to_all(part.reshape(32, 8, 4096), ('grow', 'gcol'), 0, 0, tiled=T...  45.5 us
    all_to_all x1, starting transfers between devices, on_device(): lax.all_to_all(part.reshape(32, 8, 4096), ('grow', 'gcol'), 0, 0, tiled=T...  12.9 us
    pallas_call x1, Pallas kernels, stage_a(): pl.pallas_call(kern_a, grid_spec=pltpu.PrefetchScalarGridSpec(num_scalar_...  12.8 us
    all_to_all x1, starting transfers between devices, on_device(): lax.all_to_all(cols, ('pair', 'grow'), 0, 0, tiled=True).reshape(8, 256, NG)  8.9 us
    ppermute x4, waiting for transfers between devices, swap(): lax.ppermute(block, both, [(k, k ^ flip_pair * 4 + flip_gcol) for k in ra...  5.59 us
    ppermute x3, waiting for transfers between devices, spread_rows(): got.append(lax.ppermute(at(rows, (x_at + d) % 4, 1), 'pair', perm))  5.32 us
    pallas_call x1, Pallas kernels, stage_c(): pl.pallas_call(kern_c, in_specs=[pl.BlockSpec(memory_space=pltpu.SMEM)] +...  5.28 us
    ppermute x4, starting transfers between devices, swap(): lax.ppermute(block, both, [(k, k ^ flip_pair * 4 + flip_gcol) for k in ra...  4.48 us
  transfers between devices with their start and end apart: 9, of which 7 were waited for; matrix products, arithmetic and copies ran while one was open for 4% of the time, Pallas kernels for 0%

profile of v4, /device:TPU:1, one launch (start us, length us, event | category | flops | bytes accessed | tf_op | source)
XLA Modules:
  0.0 113.3 jit_solution(16811977361997767290)
XLA Ops:
  0.0 0.0 copy-start
  0.0 12.8 %partial_transform.1 = bf16[256,4096]{1,0:T(8,128)(2,1)} custom-call(s32[32]{0:T(128)} %bitcast.75, bf16[2,64,512,128]{3,2,1,0:T(8,128)(2,1)} %bitcast.58, bf16[2,512,128]{2,1,0:T(8,128)(2,1)} %bitcast.63, bf16[256,256]{1,0:T(8,128)(2,1)} %constant.243.clone.t3_hbm, bf16[4,256,256]{2,1,0:T(8,128)(2,1)} %constant.244.clone.t2_hbm, ...), custom_call_target="tpu_custom_call" | custom-call | tf_op jit(solution)/shard_map/partial_transform/pallas_call | solution.py:122
  12.8 0.0 copy-start.5
  12.9 0.0 copy-start.4
  12.9 0.0 copy-start.6
  12.9 12.9 %all-to-all-start = ((bf16[32,8,4096]{2,1,0:T(8,128)(2,1)}), bf16[32,8,4096]{2,1,0:T(8,128)(2,1)}, u32[]{:S(2)}, u32[]{:S(2)}) async-start(bf16[32,8,4096]{2,1,0:T(8,128)(2,1)} %bitcast.59), calls=%async_computation | async-start | bytes 4194304 | tf_op jit(solution)/shard_map/all_to_all | solution.py:281
  25.8 0.0 copy-start.2
  25.8 0.0 copy-start.3
  25.9 0.0 copy-done.5
  25.9 0.1 reshape.208
  26.0 0.1 reshape_squeeze.3
  26.1 0.0 copy-done.4
  26.1 0.3 reshape.204
  26.4 0.2 slice_reduce_fusion
  26.6 0.1 reshape.205
  26.7 0.1 pad_add_fusion.1
  26.8 0.1 reshape.206
  26.8 0.1 reshape.207
  27.0 0.1 copy.27
  27.1 0.2 concatenate.31
  27.3 0.1 copy.30
  28.1 0.0 copy-done.6
  28.2 0.0 copy-done
  28.2 0.7 gather_fusion
  28.9 0.1 reshape_tile.3.weight
  29.0 1.4 %eq.36 = s32[544,2,128]{2,1,0:T(2,128)S(1)} broadcast(s32[544,2]{1,0:T(8,128)S(1)} %copy.30), dimensions={0,1} | broadcast | bytes 561408 | tf_op jit(solution)/shard_map/eq | solution.py:195
  30.4 0.1 fusion.mask
  30.5 45.5 %all-to-all-done = bf16[32,8,4096]{2,1,0:T(8,128)(2,1)} async-done(((bf16[32,8,4096]{2,1,0:T(8,128)(2,1)}), bf16[32,8,4096]{2,1,0:T(8,128)(2,1)}, u32[]{:S(2)}, u32[]{:S(2)}) %all-to-all-start) | async-done | bytes 2097184 | tf_op jit(solution)/shard_map/all_to_all | solution.py:281
  76.0 5.3 %last_transform.1 = (bf16[512,128]{1,0:T(8,128)(2,1)S(1)}, bf16[64,32,128]{2,1,0:T(8,128)(2,1)}) custom-call(s32[1088]{0:T(1024)S(1)} %fusion.4.place, bf16[256,4096]{1,0:T(8,128)(2,1)} %bitcast.11.x, bf16[256,256]{1,0:T(8,128)(2,1)S(1)} %copy-done.2, bf16[512,128]{1,0:T(8,128)(2,1)S(1)} %copy-done.3, bf16[544,256]{1,0:T(8,128)(2,1)S(1)} %fusion.mask, ...), custom_call_target="tpu_custom_call" | custom-call | tf_op jit(solution)/shard_map/last_transform/pallas_call | solution.py:199
  81.2 0.0 copy-start.1
  81.2 8.9 %all-to-all-start.1 = ((bf16[64,32,128]{2,1,0:T(8,128)(2,1)}), bf16[64,32,128]{2,1,0:T(8,128)(2,1)S(1)}, u32[]{:S(2)}, u32[]{:S(2)}) async-start(bf16[64,32,128]{2,1,0:T(8,128)(2,1)} %get-tuple-element.8), calls=%async_computation.1 | async-start | bytes 1048576 | tf_op jit(solution)/shard_map/all_to_all | solution.py:286
  90.3 2.3 %collective-permute-start.2 = (bf16[2,64,128]{2,1,0:T(8,128)(2,1)S(1)}, bf16[2,64,128]{2,1,0:T(8,128)(2,1)S(1)}, u32[]{:S(2)}, u32[]{:S(2)}) collective-permute-start(bf16[2,64,128]{2,1,0:T(8,128)(2,1)S(1)} %get-tuple-element.12), channel_id=1, source_target_pairs={{0,96},{32,0},{64,32},{96,64},{128,224},{160,128},{192,160},{224,1... | collective-permute-start | bytes 98312 | tf_op jit(solution)/shard_map/ppermute | solution.py:261
  92.6 0.5 collective-permute-start.1
  93.1 0.6 collective-permute-start
  93.7 0.0 collective-permute-done.2
  93.7 4.7 %collective-permute-done.1 = bf16[2,64,128]{2,1,0:T(8,128)(2,1)S(1)} collective-permute-done((bf16[2,64,128]{2,1,0:T(8,128)(2,1)S(1)}, bf16[2,64,128]{2,1,0:T(8,128)(2,1)S(1)}, u32[]{:S(2)}, u32[]{:S(2)}) %collective-permute-start.1) | collective-permute-done | bytes 32800 | tf_op jit(solution)/shard_map/ppermute | solution.py:261
  98.4 0.6 collective-permute-done
  99.1 0.3 collective-permute-start.5
  99.4 3.0 %collective-permute-start.4 = (bf16[4,64,128]{2,1,0:T(8,128)(2,1)S(1)}, bf16[4,64,128]{2,1,0:T(8,128)(2,1)S(1)}, u32[]{:S(2)}, u32[]{:S(2)}) collective-permute-start(bf16[4,64,128]{2,1,0:T(8,128)(2,1)S(1)} %bitcast.64), channel_id=1, source_target_pairs={{0,2},{1,3},{2,0},{3,1},{32,34},{33,35},{34,32},{35,33},{64,66},{6... | collective-permute-start | bytes 196616 | tf_op jit(solution)/shard_map/ppermute | solution.py:266
  102.4 0.1 collective-permute-start.3
  102.4 1.4 %collective-permute-done.5 = bf16[4,64,128]{2,1,0:T(8,128)(2,1)S(1)} collective-permute-done((bf16[4,64,128]{2,1,0:T(8,128)(2,1)S(1)}, bf16[4,64,128]{2,1,0:T(8,128)(2,1)S(1)}, u32[]{:S(2)}, u32[]{:S(2)}) %collective-permute-start.5) | collective-permute-done | bytes 65568 | tf_op jit(solution)/shard_map/ppermute | solution.py:266
  103.8 1.2 %collective-permute-done.4 = bf16[4,64,128]{2,1,0:T(8,128)(2,1)S(1)} collective-permute-done((bf16[4,64,128]{2,1,0:T(8,128)(2,1)S(1)}, bf16[4,64,128]{2,1,0:T(8,128)(2,1)S(1)}, u32[]{:S(2)}, u32[]{:S(2)}) %collective-permute-start.4) | collective-permute-done | bytes 65568 | tf_op jit(solution)/shard_map/ppermute | solution.py:266
  105.1 1.9 %collective-permute-done.3 = bf16[4,64,128]{2,1,0:T(8,128)(2,1)S(1)} collective-permute-done((bf16[4,64,128]{2,1,0:T(8,128)(2,1)S(1)}, bf16[4,64,128]{2,1,0:T(8,128)(2,1)S(1)}, u32[]{:S(2)}, u32[]{:S(2)}) %collective-permute-start.3) | collective-permute-done | bytes 65568 | tf_op jit(solution)/shard_map/ppermute | solution.py:266
  107.0 1.1 %collective-permute-start.6 = (bf16[2,8,64,128]{3,2,1,0:T(8,128)(2,1)S(1)}, bf16[2,8,64,128]{3,2,1,0:T(8,128)(2,1)S(1)}, u32[]{:S(2)}, u32[]{:S(2)}) collective-permute-start(bf16[2,8,64,128]{3,2,1,0:T(8,128)(2,1)S(1)} %bitcast.61), channel_id=1, source_target_pairs={{0,1},{1,0},{2,3},{3,2},{32,33},{33,32},{34,35},{35,34},{64,65},{6... | collective-permute-start | bytes 786440 | tf_op jit(solution)/shard_map/ppermute | solution.py:266
  108.2 0.1 pad_add_fusion.2.order
  108.2 1.1 collective-permute-done.6
  109.4 0.0 all-to-all-done.1
  109.4 3.9 %pair_sums.1 = f32[2,4,120,512]{3,2,1,0:T(8,128)} custom-call(s32[12]{0:T(128)S(1)} %pad_add_fusion.2.order, bf16[4,8,64,128]{3,2,1,0:T(8,128)(2,1)S(1)} %pad_maximum_fusion.rows, bf16[8,256,128]{2,1,0:T(8,128)(2,1)S(1)} %bitcast.56, bf16[256,512]{1,0:T(8,128)(2,1)S(1)} %copy-done.1), custom_call_target="tpu_custom_call" | custom-call | tf_op jit(solution)/shard_map/pair_sums/pallas_call | solution.py:241
  (21 shorter events, 0.3 us)
Async XLA Ops:
  0.0 28.2 %copy-start = (f32[64]{0:T(128)S(1)}, f32[64]{0:T(128)}, u32[]{:S(2)}) copy-start(f32[64]{0:T(128)} %param.16) | copy-start | bytes 772
  12.8 13.0 %copy-start.5 = (s32[2048]{0:T(1024)S(1)}, s32[2048]{0:T(1024)}, u32[]{:S(2)}) copy-start(s32[2048]{0:T(1024)} %param.19) | copy-start | bytes 24580
  12.9 13.2 %copy-start.4 = (s32[30720]{0:T(1024)S(1)}, s32[30720]{0:T(1024)}, u32[]{:S(2)}) copy-start(s32[30720]{0:T(1024)} %param.18) | copy-start | bytes 368644
  12.9 15.3 %copy-start.6 = (s32[1,32]{1,0:T(1,128)S(1)}, s32[1,32]{1,0:T(1,128)}, u32[]{:S(2)}) copy-start(s32[1,32]{1,0:T(1,128)} %param.15) | copy-start | bytes 388
  12.9 63.1 %all-to-all-start = ((bf16[32,8,4096]{2,1,0:T(8,128)(2,1)}), bf16[32,8,4096]{2,1,0:T(8,128)(2,1)}, u32[]{:S(2)}, u32[]{:S(2)}) async-start(bf16[32,8,4096]{2,1,0:T(8,128)(2,1)} %bitcast.59), calls=%async_computation | async-start | bytes 4194304 | tf_op jit(solution)/shard_map/all_to_all | solution.py:281
  25.8 50.1 %copy-start.2 = (bf16[256,256]{1,0:T(8,128)(2,1)S(1)}, bf16[256,256]{1,0:T(8,128)(2,1)}, u32[]{:S(2)}) copy-start(bf16[256,256]{1,0:T(8,128)(2,1)} %constant.246.clone.t1) | copy-start | bytes 393220
  25.8 50.1 %copy-start.3 = (bf16[512,128]{1,0:T(8,128)(2,1)S(1)}, bf16[512,128]{1,0:T(8,128)(2,1)}, u32[]{:S(2)}) copy-start(bf16[512,128]{1,0:T(8,128)(2,1)} %constant.247.clone.pick) | copy-start | bytes 393220
  81.2 28.1 %copy-start.1 = (bf16[256,512]{1,0:T(8,128)(2,1)S(1)}, bf16[256,512]{1,0:T(8,128)(2,1)}, u32[]{:S(2)}) copy-start(bf16[256,512]{1,0:T(8,128)(2,1)} %constant.248.clone.turn) | copy-start | bytes 786436
  81.2 28.1 %all-to-all-start.1 = ((bf16[64,32,128]{2,1,0:T(8,128)(2,1)}), bf16[64,32,128]{2,1,0:T(8,128)(2,1)S(1)}, u32[]{:S(2)}, u32[]{:S(2)}) async-start(bf16[64,32,128]{2,1,0:T(8,128)(2,1)} %get-tuple-element.8), calls=%async_computation.1 | async-start | bytes 1048576 | tf_op jit(solution)/shard_map/all_to_all | solution.py:286
  90.3 3.5 %collective-permute-start.2 = (bf16[2,64,128]{2,1,0:T(8,128)(2,1)S(1)}, bf16[2,64,128]{2,1,0:T(8,128)(2,1)S(1)}, u32[]{:S(2)}, u32[]{:S(2)}) collective-permute-start(bf16[2,64,128]{2,1,0:T(8,128)(2,1)S(1)} %get-tuple-element.12), channel_id=1, source_target_pairs={{0,96},{32,0},{64,32},{96,64},{128,224},{160,128},{192,160},{224,1... | collective-permute-start | bytes 98312 | tf_op jit(solution)/shard_map/ppermute | solution.py:261
  92.6 5.8 %collective-permute-start.1 = (bf16[2,64,128]{2,1,0:T(8,128)(2,1)S(1)}, bf16[2,64,128]{2,1,0:T(8,128)(2,1)S(1)}, u32[]{:S(2)}, u32[]{:S(2)}) collective-permute-start(bf16[2,64,128]{2,1,0:T(8,128)(2,1)S(1)} %get-tuple-element.13), channel_id=1, source_target_pairs={{0,64},{32,96},{64,0},{96,32},{128,192},{160,224},{192,128},{224,1... | collective-permute-start | bytes 98312 | tf_op jit(solution)/shard_map/ppermute | solution.py:261
  93.1 5.9 %collective-permute-start = (bf16[2,64,128]{2,1,0:T(8,128)(2,1)S(1)}, bf16[2,64,128]{2,1,0:T(8,128)(2,1)S(1)}, u32[]{:S(2)}, u32[]{:S(2)}) collective-permute-start(bf16[2,64,128]{2,1,0:T(8,128)(2,1)S(1)} %get-tuple-element.14), channel_id=1, source_target_pairs={{0,32},{32,64},{64,96},{96,0},{128,160},{160,192},{192,224},{224,1... | collective-permute-start | bytes 98312 | tf_op jit(solution)/shard_map/ppermute | solution.py:261
  99.1 4.7 %collective-permute-start.5 = (bf16[4,64,128]{2,1,0:T(8,128)(2,1)S(1)}, bf16[4,64,128]{2,1,0:T(8,128)(2,1)S(1)}, u32[]{:S(2)}, u32[]{:S(2)}) collective-permute-start(bf16[4,64,128]{2,1,0:T(8,128)(2,1)S(1)} %get-tuple-element.10), channel_id=1, source_target_pairs={{0,130},{1,131},{2,128},{3,129},{32,162},{33,163},{34,160},{35,161... | collective-permute-start | bytes 196616 | tf_op jit(solution)/shard_map/ppermute | solution.py:266
  99.4 5.7 %collective-permute-start.4 = (bf16[4,64,128]{2,1,0:T(8,128)(2,1)S(1)}, bf16[4,64,128]{2,1,0:T(8,128)(2,1)S(1)}, u32[]{:S(2)}, u32[]{:S(2)}) collective-permute-start(bf16[4,64,128]{2,1,0:T(8,128)(2,1)S(1)} %bitcast.64), channel_id=1, source_target_pairs={{0,2},{1,3},{2,0},{3,1},{32,34},{33,35},{34,32},{35,33},{64,66},{6... | collective-permute-start | bytes 196616 | tf_op jit(solution)/shard_map/ppermute | solution.py:266
  102.4 4.6 %collective-permute-start.3 = (bf16[4,64,128]{2,1,0:T(8,128)(2,1)S(1)}, bf16[4,64,128]{2,1,0:T(8,128)(2,1)S(1)}, u32[]{:S(2)}, u32[]{:S(2)}) collective-permute-start(bf16[4,64,128]{2,1,0:T(8,128)(2,1)S(1)} %get-tuple-element.10), channel_id=1, source_target_pairs={{0,128},{1,129},{2,130},{3,131},{32,160},{33,161},{34,162},{35,163... | collective-permute-start | bytes 196616 | tf_op jit(solution)/shard_map/ppermute | solution.py:266
  107.0 2.3 %collective-permute-start.6 = (bf16[2,8,64,128]{3,2,1,0:T(8,128)(2,1)S(1)}, bf16[2,8,64,128]{3,2,1,0:T(8,128)(2,1)S(1)}, u32[]{:S(2)}, u32[]{:S(2)}) collective-permute-start(bf16[2,8,64,128]{3,2,1,0:T(8,128)(2,1)S(1)} %bitcast.61), channel_id=1, source_target_pairs={{0,1},{1,0},{2,3},{3,2},{32,33},{33,32},{34,35},{35,34},{64,65},{6... | collective-permute-start | bytes 786440 | tf_op jit(solution)/shard_map/ppermute | solution.py:266

commit v5 on v4

--- a/solution.py
+++ b/solution.py
@@ -1,3 +1,4 @@
+import functools
 import math
 import numpy as np
 import ml_dtypes
@@ -10,7 +11,6 @@
 BF=jnp.bfloat16
 VM_A=62
 CH=64
-Q=4
 NG=128; GR=8; GC=4; PL=4; QW=32; PAIRS=32; J=4
 NT=(((1,),(1,)),((),()))
 NN=(((1,),(0,)),((),()))
@@ -42,7 +42,7 @@
                     perm[((g_*GC+cc)*PL+s)*2+o, ((cc*PL+s)*2+o)*GR+g_]=1
     return [np.asarray(t,np.float32).astype(ml_dtypes.bfloat16) for t in (t3,t2,perm)]
 
-def kern_a(bands, val, cnd_hbm, t3_hbm, t2_hbm, perm_hbm, out, vbuf, dens, third, cnd, cond, t3, t2_all, t2, perm, sems, vsems):
+def kern_a(Q, steps, bands, val, cnd_hbm, t3_hbm, t2_hbm, perm_hbm, out, vbuf, dens, third, cnd, cond, t3, t2_all, t2, perm, sems, vsems):
     step = pl.program_id(0)
     first = step == 0
     loads = [pltpu.make_async_copy(a, b, sems.at[k]) for k, (a, b) in enumerate(((cnd_hbm, cnd), (t3_hbm, t3), (t2_hbm, t2_all), (perm_hbm, perm)))]
@@ -63,7 +63,7 @@
         cond[...] = cnd[...].astype(jnp.float32)
         loads[1].wait()
 
-    @pl.when(step < PAIRS//(Q*J) - 1)
+    @pl.when(step < steps - 1)
     def _():
         for k in range(Q*J):
             band_load((step+1)*Q*J+k).start()
@@ -114,13 +114,14 @@
             out[:,(q*2+wp)*256:(q*2+wp+1)*256]=jnp.dot(perm[...],y,preferred_element_type=jnp.float32).astype(BF)
 
 
-def stage_a(valence, cond, bands):
+def stage_a(valence, cond, bands, Q=4):
     nval=valence.shape[1]
     v=jnp.transpose(valence.reshape(2,nval,PL,NG,NG),(0,1,3,2,4)).reshape(2,nval,NG*PL,NG)
     cf=jnp.transpose(cond.reshape(2,PL,NG,NG),(0,2,1,3)).reshape(2,NG*PL,NG)
     t3,t2,perm=tables()
-    return pl.pallas_call(kern_a,
-        grid_spec=pltpu.PrefetchScalarGridSpec(num_scalar_prefetch=1,grid=(bands.shape[0]//(Q*J),),
+    steps=bands.shape[0]//(Q*J)
+    return pl.pallas_call(functools.partial(kern_a,Q,steps),
+        grid_spec=pltpu.PrefetchScalarGridSpec(num_scalar_prefetch=1,grid=(steps,),
             in_specs=[pl.BlockSpec(memory_space=pltpu.HBM)]*5,
             out_specs=pl.BlockSpec((256,512*Q),lambda q,b:(0,q)),
             scratch_shapes=[pltpu.VMEM((PAIRS,2,NG*PL,NG),BF),pltpu.VMEM((Q*J,2,NG*PL,NG),jnp.float32),pltpu.VMEM((Q*J,PL//2,256,256),BF),pltpu.VMEM((2,NG*PL,NG),BF),pltpu.VMEM((2,NG*PL,NG),jnp.float32),pltpu.VMEM((256,256),BF),
@@ -165,7 +166,7 @@
                 at=pl.multiple_of(place[2*r+h],2)
                 found[pl.ds(pl.multiple_of(4*r+2*h,2),2),:]=field[pl.ds(at,2),:]
             return carry
-        lax.fori_loop(first,last,body,0,unroll=8)
+        lax.fori_loop(first,last,body,0,unroll=32)
         parts=[]
         for h in range(2):
             for o in range(2):
@@ -213,40 +214,46 @@
                 q[b,h,1,p,h,0,b,1,p]=1
                 q[b,h,1,p,h,1,b,0,p]=1
                 q[b,h,0,p,h,1,b,1,p]=-1
-    return np.asarray(q.reshape(256,512),np.float32).astype(ml_dtypes.bfloat16)
-
-def kern_d(order, rows, cols, turn, out, slab):
-    @pl.when(pl.program_id(0) == 0)
-    def _():
+    r=np.zeros((2,2,64,2,2,64))
+    for b in range(2):
+        for h in range(2):
+            for k in range(64):
+                r[b,h,k,h,b,k]=1
+    return [np.asarray(t,np.float32).astype(ml_dtypes.bfloat16) for t in (q.reshape(256,512),r.reshape(256,256))]
+
+def kern_d(order, rows, cols, turn, halves, out, slab, buf, sems):
+    for pp in range(4):
+        both=jnp.concatenate([cols[2*pp],cols[2*pp+1]],axis=1)
+        v=jnp.dot(both,halves[...],preferred_element_type=jnp.float32)
+        v=jnp.concatenate([v[(g*4+pb)*8:(g*4+pb+1)*8] for pb in range(4) for g in range(8)],axis=0).astype(BF)
+        for h in range(2):
+            slab[h*256:(h+1)*256,pp*NG:(pp+1)*NG]=v[:,h*NG:(h+1)*NG]
+    sends=[]
+    for c in range(4):
+        turned=[]
         for pp in range(4):
-            a=cols[2*pp].astype(jnp.float32)
-            b=cols[2*pp+1].astype(jnp.float32)
-            for h in range(2):
-                v=jnp.concatenate([a[:,h*64:(h+1)*64],b[:,h*64:(h+1)*64]],axis=1)
-                v=jnp.concatenate([v[(g*4+pb)*8:(g*4+pb+1)*8] for pb in range(4) for g in range(8)],axis=0)
-                slab[h*256:(h+1)*256,pp*NG:(pp+1)*NG]=v.astype(BF)
-    turned=[]
-    for pp in range(4):
-        pair=jnp.concatenate([rows[0,order[4+2*pp+k]] for k in range(2)],axis=1)
-        turned.append(jnp.dot(pair,turn[...],preferred_element_type=jnp.float32).astype(BF))
-    lhs=jnp.concatenate([jnp.concatenate([t[:,k*NG:(k+1)*NG] for t in turned],axis=1) for k in range(4)],axis=0)
-    z=lax.dot_general(lhs,slab[...],NT,preferred_element_type=jnp.float32)
-    for hr in range(2):
-        n=64 if hr==0 else 56
-        for o in range(2):
-            k=hr*2+o
-            out[o,0,64*hr:64*hr+n,:]=z[k*64:k*64+n]
+            pair=jnp.concatenate([rows[order[c],order[4+2*pp+k]] for k in range(2)],axis=1)
+            turned.append(jnp.dot(pair,turn[...],preferred_element_type=jnp.float32).astype(BF))
+        lhs=jnp.concatenate([jnp.concatenate([t[:,k*NG:(k+1)*NG] for t in turned],axis=1) for k in range(4)],axis=0)
+        z=lax.dot_general(lhs,slab[...],NT,preferred_element_type=jnp.float32)
+        for hr in range(2):
+            n=64 if hr==0 else 56
+            for o in range(2):
+                k=hr*2+o
+                buf[c,o,64*hr:64*hr+n,:]=z[k*64:k*64+n]
+        sends.append(pltpu.make_async_copy(buf.at[c],out.at[:,c],sems.at[c]))
+        sends[-1].start()
+    for send in sends:
+        send.wait()
 
 def stage_d(order, rows, cols):
+    vm=pl.BlockSpec(memory_space=pltpu.VMEM)
     return pl.pallas_call(kern_d,
-        grid_spec=pltpu.PrefetchScalarGridSpec(num_scalar_prefetch=1,grid=(4,),
-            in_specs=[pl.BlockSpec((1,8,64,NG),lambda c,o:(o[c],0,0,0)),
-                pl.BlockSpec((8,256,NG),lambda c,o:(0,0,0)),pl.BlockSpec((256,512),lambda c,o:(0,0))],
-            out_specs=pl.BlockSpec((2,1,120,512),lambda c,o:(0,c,0,0)),
-            scratch_shapes=[pltpu.VMEM((512,512),BF)]),
+        in_specs=[pl.BlockSpec(memory_space=pltpu.SMEM)]+[vm]*4,out_specs=pl.BlockSpec(memory_space=pltpu.HBM),
         out_shape=jax.ShapeDtypeStruct((2,4,120,512),jnp.float32),
+        scratch_shapes=[pltpu.VMEM((512,512),BF),pltpu.VMEM((4,2,120,512),jnp.float32),pltpu.SemaphoreType.DMA((4,))],
         compiler_params=pltpu.CompilerParams(vmem_limit_bytes=32*2**20),
-        name="pair_sums")(order,rows,cols,tables_d()).reshape(2,480,512)
+        name="pair_sums")(order,rows,cols,*tables_d()).reshape(2,480,512)
 
 def at(x, k, axis):
     return lax.dynamic_index_in_dim(x, k, axis, False)

time: 114 us -> 113 us (level)
  no operation moved by 1% of the time
where the time goes in v5:
time: 113 us; the launch traced here: 112 us
  waiting for transfers between devices  56.4 us (50%)
  starting transfers between devices  30 us (27%)
  Pallas kernels  20.9 us (18%)
  local copies, waits for them, and re-layouts  3.67 us (3%)
  between operations  1.18 us (1%)
    all_to_all x1, waiting for transfers between devices, on_device(): lax.all_to_all(part.reshape(32, 8, 4096), ('grow', 'gcol'), 0, 0, tiled=T...  45.5 us
    all_to_all x1, starting transfers between devices, on_device(): lax.all_to_all(part.reshape(32, 8, 4096), ('grow', 'gcol'), 0, 0, tiled=T...  13 us
    pallas_call x1, Pallas kernels, stage_a(): pl.pallas_call(functools.partial(kern_a, Q, steps), grid_spec=pltpu.Prefe...  12.7 us
    all_to_all x1, starting transfers between devices, on_device(): lax.all_to_all(cols, ('pair', 'grow'), 0, 0, tiled=True).reshape(8, 256, NG)  8.9 us
    ppermute x4, waiting for transfers between devices, swap(): lax.ppermute(block, both, [(k, k ^ flip_pair * 4 + flip_gcol) for k in ra...  5.55 us
    ppermute x3, waiting for transfers between devices, spread_rows(): got.append(lax.ppermute(at(rows, (x_at + d) % 4, 1), 'pair', perm))  5.33 us
    pallas_call x1, Pallas kernels, stage_c(): pl.pallas_call(kern_c, in_specs=[pl.BlockSpec(memory_space=pltpu.SMEM)] +...  5 us
    ppermute x4, starting transfers between devices, swap(): lax.ppermute(block, both, [(k, k ^ flip_pair * 4 + flip_gcol) for k in ra...  4.63 us
  transfers between devices with their start and end apart: 9, of which 7 were waited for; matrix products, arithmetic and copies ran while one was open for 4% of the time, Pallas kernels for 0%

profile of v5, /device:TPU:1, one launch (start us, length us, event | category | flops | bytes accessed | tf_op | source)
XLA Modules:
  0.0 112.4 jit_solution(9877846791943900260)
XLA Ops:
  0.0 0.0 copy-start
  0.0 12.7 %partial_transform.1 = bf16[256,4096]{1,0:T(8,128)(2,1)} custom-call(s32[32]{0:T(128)} %bitcast.75, bf16[2,64,512,128]{3,2,1,0:T(8,128)(2,1)} %bitcast.58, bf16[2,512,128]{2,1,0:T(8,128)(2,1)} %bitcast.63, bf16[256,256]{1,0:T(8,128)(2,1)} %constant.245.clone.t3_hbm, bf16[4,256,256]{2,1,0:T(8,128)(2,1)} %constant.246.clone.t2_hbm, ...), custom_call_target="tpu_custom_call" | custom-call | tf_op jit(solution)/shard_map/partial_transform/pallas_call | solution.py:123
  12.8 0.0 copy-start.6
  12.8 0.0 copy-start.5
  12.8 0.0 copy-start.7
  12.8 13.0 %all-to-all-start = ((bf16[32,8,4096]{2,1,0:T(8,128)(2,1)}), bf16[32,8,4096]{2,1,0:T(8,128)(2,1)}, u32[]{:S(2)}, u32[]{:S(2)}) async-start(bf16[32,8,4096]{2,1,0:T(8,128)(2,1)} %bitcast.59), calls=%async_computation | async-start | bytes 4194304 | tf_op jit(solution)/shard_map/all_to_all | solution.py:288
  25.8 0.0 copy-start.3
  25.8 0.0 copy-start.4
  25.8 0.0 copy-done.6
  25.8 0.1 reshape.208
  25.9 0.1 reshape_squeeze.3
  26.0 0.3 reshape.204
  26.4 0.2 slice_reduce_fusion
  26.5 0.1 reshape.205
  26.6 0.1 pad_add_fusion.1
  26.7 0.1 reshape.206
  26.8 0.1 reshape.207
  26.9 0.1 copy.28
  27.1 0.2 concatenate.31
  27.3 0.1 copy.31
  28.1 0.7 gather_fusion
  28.8 0.1 reshape_tile.3.weight
  29.0 1.4 %eq.36 = s32[544,2,128]{2,1,0:T(2,128)S(1)} broadcast(s32[544,2]{1,0:T(8,128)S(1)} %copy.31), dimensions={0,1} | broadcast | bytes 561408 | tf_op jit(solution)/shard_map/eq | solution.py:196
  30.4 0.1 fusion.mask
  30.4 45.5 %all-to-all-done = bf16[32,8,4096]{2,1,0:T(8,128)(2,1)} async-done(((bf16[32,8,4096]{2,1,0:T(8,128)(2,1)}), bf16[32,8,4096]{2,1,0:T(8,128)(2,1)}, u32[]{:S(2)}, u32[]{:S(2)}) %all-to-all-start) | async-done | bytes 2097184 | tf_op jit(solution)/shard_map/all_to_all | solution.py:288
  75.9 5.0 %last_transform.1 = (bf16[512,128]{1,0:T(8,128)(2,1)S(1)}, bf16[64,32,128]{2,1,0:T(8,128)(2,1)}) custom-call(s32[1088]{0:T(1024)S(1)} %fusion.4.place, bf16[256,4096]{1,0:T(8,128)(2,1)} %bitcast.11.x, bf16[256,256]{1,0:T(8,128)(2,1)S(1)} %copy-done.3, bf16[512,128]{1,0:T(8,128)(2,1)S(1)} %copy-done.4, bf16[544,256]{1,0:T(8,128)(2,1)S(1)} %fusion.mask, ...), custom_call_target="tpu_custom_call" | custom-call | tf_op jit(solution)/shard_map/last_transform/pallas_call | solution.py:200
  80.9 0.0 copy-start.1
  80.9 0.0 copy-start.2
  80.9 8.9 %all-to-all-start.1 = ((bf16[64,32,128]{2,1,0:T(8,128)(2,1)}), bf16[64,32,128]{2,1,0:T(8,128)(2,1)S(1)}, u32[]{:S(2)}, u32[]{:S(2)}) async-start(bf16[64,32,128]{2,1,0:T(8,128)(2,1)} %get-tuple-element.8), calls=%async_computation.1 | async-start | bytes 1048576 | tf_op jit(solution)/shard_map/all_to_all | solution.py:293
  89.9 2.3 %collective-permute-start.2 = (bf16[2,64,128]{2,1,0:T(8,128)(2,1)S(1)}, bf16[2,64,128]{2,1,0:T(8,128)(2,1)S(1)}, u32[]{:S(2)}, u32[]{:S(2)}) collective-permute-start(bf16[2,64,128]{2,1,0:T(8,128)(2,1)S(1)} %get-tuple-element.12), channel_id=1, source_target_pairs={{0,96},{32,0},{64,32},{96,64},{128,224},{160,128},{192,160},{224,1... | collective-permute-start | bytes 98312 | tf_op jit(solution)/shard_map/ppermute | solution.py:268
  92.3 0.5 collective-permute-start.1
  92.8 0.6 collective-permute-start
  93.4 0.0 collective-permute-done.2
  93.4 4.7 %collective-permute-done.1 = bf16[2,64,128]{2,1,0:T(8,128)(2,1)S(1)} collective-permute-done((bf16[2,64,128]{2,1,0:T(8,128)(2,1)S(1)}, bf16[2,64,128]{2,1,0:T(8,128)(2,1)S(1)}, u32[]{:S(2)}, u32[]{:S(2)}) %collective-permute-start.1) | collective-permute-done | bytes 32800 | tf_op jit(solution)/shard_map/ppermute | solution.py:268
  98.1 0.6 collective-permute-done
  98.8 0.5 collective-permute-start.5
  99.2 3.0 %collective-permute-start.4 = (bf16[4,64,128]{2,1,0:T(8,128)(2,1)S(1)}, bf16[4,64,128]{2,1,0:T(8,128)(2,1)S(1)}, u32[]{:S(2)}, u32[]{:S(2)}) collective-permute-start(bf16[4,64,128]{2,1,0:T(8,128)(2,1)S(1)} %bitcast.64), channel_id=1, source_target_pairs={{0,2},{1,3},{2,0},{3,1},{32,34},{33,35},{34,32},{35,33},{64,66},{6... | collective-permute-start | bytes 196616 | tf_op jit(solution)/shard_map/ppermute | solution.py:273
  102.2 0.1 collective-permute-start.3
  102.3 1.4 %collective-permute-done.5 = bf16[4,64,128]{2,1,0:T(8,128)(2,1)S(1)} collective-permute-done((bf16[4,64,128]{2,1,0:T(8,128)(2,1)S(1)}, bf16[4,64,128]{2,1,0:T(8,128)(2,1)S(1)}, u32[]{:S(2)}, u32[]{:S(2)}) %collective-permute-start.5) | collective-permute-done | bytes 65568 | tf_op jit(solution)/shard_map/ppermute | solution.py:273
  103.7 1.1 collective-permute-done.4
  104.7 2.0 %collective-permute-done.3 = bf16[4,64,128]{2,1,0:T(8,128)(2,1)S(1)} collective-permute-done((bf16[4,64,128]{2,1,0:T(8,128)(2,1)S(1)}, bf16[4,64,128]{2,1,0:T(8,128)(2,1)S(1)}, u32[]{:S(2)}, u32[]{:S(2)}) %collective-permute-start.3) | collective-permute-done | bytes 65568 | tf_op jit(solution)/shard_map/ppermute | solution.py:273
  106.8 1.1 collective-permute-start.6
  108.0 0.1 pad_add_fusion.2.order
  108.0 1.1 collective-permute-done.6
  109.2 0.0 all-to-all-done.1
  109.2 0.0 copy-done.1
  109.2 0.0 copy-done.2
  109.2 3.1 %pair_sums.1 = f32[2,4,120,512]{3,2,1,0:T(8,128)} custom-call(s32[12]{0:T(128)S(1)} %pad_add_fusion.2.order, bf16[4,8,64,128]{3,2,1,0:T(8,128)(2,1)S(1)} %pad_maximum_fusion.rows, bf16[8,256,128]{2,1,0:T(8,128)(2,1)S(1)} %bitcast.56, bf16[256,512]{1,0:T(8,128)(2,1)S(1)} %copy-done.1, bf16[256,256]{1,0:T(8,128)(2,1)S(1)} %copy-done.2), custom_call_target="tpu_custom_call" | custom-call | tf_op jit(solution)/shard_map/pair_sums/pallas_call | solution.py:251
  (23 shorter events, 0.3 us)
Async XLA Ops:
  0.0 28.1 %copy-start = (f32[64]{0:T(128)S(1)}, f32[64]{0:T(128)}, u32[]{:S(2)}) copy-start(f32[64]{0:T(128)} %param.17) | copy-start | bytes 772
  12.8 13.0 %copy-start.6 = (s32[2048]{0:T(1024)S(1)}, s32[2048]{0:T(1024)}, u32[]{:S(2)}) copy-start(s32[2048]{0:T(1024)} %param.20) | copy-start | bytes 24580
  12.8 13.3 %copy-start.5 = (s32[30720]{0:T(1024)S(1)}, s32[30720]{0:T(1024)}, u32[]{:S(2)}) copy-start(s32[30720]{0:T(1024)} %param.19) | copy-start | bytes 368644
  12.8 15.3 %copy-start.7 = (s32[1,32]{1,0:T(1,128)S(1)}, s32[1,32]{1,0:T(1,128)}, u32[]{:S(2)}) copy-start(s32[1,32]{1,0:T(1,128)} %param.16) | copy-start | bytes 388
  12.8 63.1 %all-to-all-start = ((bf16[32,8,4096]{2,1,0:T(8,128)(2,1)}), bf16[32,8,4096]{2,1,0:T(8,128)(2,1)}, u32[]{:S(2)}, u32[]{:S(2)}) async-start(bf16[32,8,4096]{2,1,0:T(8,128)(2,1)} %bitcast.59), calls=%async_computation | async-start | bytes 4194304 | tf_op jit(solution)/shard_map/all_to_all | solution.py:288
  25.8 50.1 %copy-start.3 = (bf16[256,256]{1,0:T(8,128)(2,1)S(1)}, bf16[256,256]{1,0:T(8,128)(2,1)}, u32[]{:S(2)}) copy-start(bf16[256,256]{1,0:T(8,128)(2,1)} %constant.248.clone.t1) | copy-start | bytes 393220
  25.8 50.1 %copy-start.4 = (bf16[512,128]{1,0:T(8,128)(2,1)S(1)}, bf16[512,128]{1,0:T(8,128)(2,1)}, u32[]{:S(2)}) copy-start(bf16[512,128]{1,0:T(8,128)(2,1)} %constant.249.clone.pick) | copy-start | bytes 393220
  80.9 28.3 %copy-start.1 = (bf16[256,512]{1,0:T(8,128)(2,1)S(1)}, bf16[256,512]{1,0:T(8,128)(2,1)}, u32[]{:S(2)}) copy-start(bf16[256,512]{1,0:T(8,128)(2,1)} %constant.250.clone.turn) | copy-start | bytes 786436
  80.9 28.3 %copy-start.2 = (bf16[256,256]{1,0:T(8,128)(2,1)S(1)}, bf16[256,256]{1,0:T(8,128)(2,1)}, u32[]{:S(2)}) copy-start(bf16[256,256]{1,0:T(8,128)(2,1)} %constant.251.clone.halves) | copy-start | bytes 393220
  80.9 28.2 %all-to-all-start.1 = ((bf16[64,32,128]{2,1,0:T(8,128)(2,1)}), bf16[64,32,128]{2,1,0:T(8,128)(2,1)S(1)}, u32[]{:S(2)}, u32[]{:S(2)}) async-start(bf16[64,32,128]{2,1,0:T(8,128)(2,1)} %get-tuple-element.8), calls=%async_computation.1 | async-start | bytes 1048576 | tf_op jit(solution)/shard_map/all_to_all | solution.py:293
  89.9 3.5 %collective-permute-start.2 = (bf16[2,64,128]{2,1,0:T(8,128)(2,1)S(1)}, bf16[2,64,128]{2,1,0:T(8,128)(2,1)S(1)}, u32[]{:S(2)}, u32[]{:S(2)}) collective-permute-start(bf16[2,64,128]{2,1,0:T(8,128)(2,1)S(1)} %get-tuple-element.12), channel_id=1, source_target_pairs={{0,96},{32,0},{64,32},{96,64},{128,224},{160,128},{192,160},{224,1... | collective-permute-start | bytes 98312 | tf_op jit(solution)/shard_map/ppermute | solution.py:268
  92.3 5.8 %collective-permute-start.1 = (bf16[2,64,128]{2,1,0:T(8,128)(2,1)S(1)}, bf16[2,64,128]{2,1,0:T(8,128)(2,1)S(1)}, u32[]{:S(2)}, u32[]{:S(2)}) collective-permute-start(bf16[2,64,128]{2,1,0:T(8,128)(2,1)S(1)} %get-tuple-element.13), channel_id=1, source_target_pairs={{0,64},{32,96},{64,0},{96,32},{128,192},{160,224},{192,128},{224,1... | collective-permute-start | bytes 98312 | tf_op jit(solution)/shard_map/ppermute | solution.py:268
  92.8 5.9 %collective-permute-start = (bf16[2,64,128]{2,1,0:T(8,128)(2,1)S(1)}, bf16[2,64,128]{2,1,0:T(8,128)(2,1)S(1)}, u32[]{:S(2)}, u32[]{:S(2)}) collective-permute-start(bf16[2,64,128]{2,1,0:T(8,128)(2,1)S(1)} %get-tuple-element.14), channel_id=1, source_target_pairs={{0,32},{32,64},{64,96},{96,0},{128,160},{160,192},{192,224},{224,1... | collective-permute-start | bytes 98312 | tf_op jit(solution)/shard_map/ppermute | solution.py:268
  98.8 4.9 %collective-permute-start.5 = (bf16[4,64,128]{2,1,0:T(8,128)(2,1)S(1)}, bf16[4,64,128]{2,1,0:T(8,128)(2,1)S(1)}, u32[]{:S(2)}, u32[]{:S(2)}) collective-permute-start(bf16[4,64,128]{2,1,0:T(8,128)(2,1)S(1)} %get-tuple-element.10), channel_id=1, source_target_pairs={{0,130},{1,131},{2,128},{3,129},{32,162},{33,163},{34,160},{35,161... | collective-permute-start | bytes 196616 | tf_op jit(solution)/shard_map/ppermute | solution.py:273
  99.2 5.5 %collective-permute-start.4 = (bf16[4,64,128]{2,1,0:T(8,128)(2,1)S(1)}, bf16[4,64,128]{2,1,0:T(8,128)(2,1)S(1)}, u32[]{:S(2)}, u32[]{:S(2)}) collective-permute-start(bf16[4,64,128]{2,1,0:T(8,128)(2,1)S(1)} %bitcast.64), channel_id=1, source_target_pairs={{0,2},{1,3},{2,0},{3,1},{32,34},{33,35},{34,32},{35,33},{64,66},{6... | collective-permute-start | bytes 196616 | tf_op jit(solution)/shard_map/ppermute | solution.py:273
  102.2 4.6 %collective-permute-start.3 = (bf16[4,64,128]{2,1,0:T(8,128)(2,1)S(1)}, bf16[4,64,128]{2,1,0:T(8,128)(2,1)S(1)}, u32[]{:S(2)}, u32[]{:S(2)}) collective-permute-start(bf16[4,64,128]{2,1,0:T(8,128)(2,1)S(1)} %get-tuple-element.10), channel_id=1, source_target_pairs={{0,128},{1,129},{2,130},{3,131},{32,160},{33,161},{34,162},{35,163... | collective-permute-start | bytes 196616 | tf_op jit(solution)/shard_map/ppermute | solution.py:273
  106.8 2.3 %collective-permute-start.6 = (bf16[2,8,64,128]{3,2,1,0:T(8,128)(2,1)S(1)}, bf16[2,8,64,128]{3,2,1,0:T(8,128)(2,1)S(1)}, u32[]{:S(2)}, u32[]{:S(2)}) collective-permute-start(bf16[2,8,64,128]{3,2,1,0:T(8,128)(2,1)S(1)} %bitcast.61), channel_id=1, source_target_pairs={{0,1},{1,0},{2,3},{3,2},{32,33},{33,32},{34,35},{35,34},{64,65},{6... | collective-permute-start | bytes 786440 | tf_op jit(solution)/shard_map/ppermute | solution.py:273

commit v6 on v5

--- a/solution.py
+++ b/solution.py
@@ -223,7 +223,7 @@
 
 def kern_d(order, rows, cols, turn, halves, out, slab, buf, sems):
     for pp in range(4):
-        both=jnp.concatenate([cols[2*pp],cols[2*pp+1]],axis=1)
+        both=jnp.concatenate([jnp.concatenate([cols[g*8+2*pp+k] for g in range(8)],axis=0) for k in range(2)],axis=1)
         v=jnp.dot(both,halves[...],preferred_element_type=jnp.float32)
         v=jnp.concatenate([v[(g*4+pb)*8:(g*4+pb+1)*8] for pb in range(4) for g in range(8)],axis=0).astype(BF)
         for h in range(2):
@@ -290,7 +290,7 @@
     gaps = jnp.take(e_val, bands) - e_cond[0]
     weight = 2.0 / (gaps * math.sqrt(PAIRS * n_pair))
     rows, cols = stage_c(moved.reshape(256, 4096), ids, weight)
-    cols = lax.all_to_all(cols, ("pair", "grow"), 0, 0, tiled=True).reshape(8, 256, NG)
+    cols = lax.all_to_all(cols, ("grow", "pair"), 0, 0, tiled=True)
     rows = spread_rows(rows.reshape(2, 4, 64, NG), pair_at, gcol_at)
     c = jnp.arange(4, dtype=jnp.int32)
     blocks = (c % 2 ^ gcol_at % 2) * 2 + (c // 2 ^ gcol_at // 2)

time: 113 us -> 112 us (level)
  transfers between devices with their start and end apart: 9 -> 9, of which waited for: 7 -> 8; matrix products, arithmetic and copies ran while one was open for 4% -> 4% of each run, Pallas kernels for 0% -> 0%
where the time goes in v6:
time: 112 us
  waiting for transfers between devices  55.6 us (50%)
  starting transfers between devices  30.2 us (27%)
  Pallas kernels  20.9 us (19%)
  local copies, waits for them, and re-layouts  3.67 us (3%)
  between operations  1.18 us (1%)
    all_to_all x1, waiting for transfers between devices, on_device(): lax.all_to_all(part.reshape(32, 8, 4096), ('grow', 'gcol'), 0, 0, tiled=T...  45.5 us
    all_to_all x1, starting transfers between devices, on_device(): lax.all_to_all(part.reshape(32, 8, 4096), ('grow', 'gcol'), 0, 0, tiled=T...  13 us
    pallas_call x1, Pallas kernels, stage_a(): pl.pallas_call(functools.partial(kern_a, Q, steps), grid_spec=pltpu.Prefe...  12.7 us
    all_to_all x1, starting transfers between devices, on_device(): cols = lax.all_to_all(cols, ('grow', 'pair'), 0, 0, tiled=True)  8.9 us
    ppermute x3, waiting for transfers between devices, spread_rows(): got.append(lax.ppermute(at(rows, (x_at + d) % 4, 1), 'pair', perm))  5.17 us
    pallas_call x1, Pallas kernels, stage_c(): pl.pallas_call(kern_c, in_specs=[pl.BlockSpec(memory_space=pltpu.SMEM)] +...  5 us
    ppermute x4, waiting for transfers between devices, swap(): lax.ppermute(block, both, [(k, k ^ flip_pair * 4 + flip_gcol) for k in ra...  5 us
    ppermute x4, starting transfers between devices, swap(): lax.ppermute(block, both, [(k, k ^ flip_pair * 4 + flip_gcol) for k in ra...  4.88 us
  transfers between devices with their start and end apart: 9, of which 8 were waited for; matrix products, arithmetic and copies ran while one was open for 4% of the time, Pallas kernels for 0%

profile of v6, /device:TPU:1, one launch (start us, length us, event | category | flops | bytes accessed | tf_op | source)
XLA Modules:
  0.0 112.0 jit_solution(2853928192142680849)
XLA Ops:
  0.0 0.0 copy-start
  0.0 12.7 %partial_transform.1 = bf16[256,4096]{1,0:T(8,128)(2,1)} custom-call(s32[32]{0:T(128)} %bitcast.73, bf16[2,64,512,128]{3,2,1,0:T(8,128)(2,1)} %bitcast.56, bf16[2,512,128]{2,1,0:T(8,128)(2,1)} %bitcast.61, bf16[256,256]{1,0:T(8,128)(2,1)} %constant.245.clone.t3_hbm, bf16[4,256,256]{2,1,0:T(8,128)(2,1)} %constant.246.clone.t2_hbm, ...), custom_call_target="tpu_custom_call" | custom-call | tf_op jit(solution)/shard_map/partial_transform/pallas_call | solution.py:123
  12.8 0.0 copy-start.6
  12.8 0.0 copy-start.5
  12.8 0.0 copy-start.7
  12.8 13.0 %all-to-all-start = ((bf16[32,8,4096]{2,1,0:T(8,128)(2,1)}), bf16[32,8,4096]{2,1,0:T(8,128)(2,1)}, u32[]{:S(2)}, u32[]{:S(2)}) async-start(bf16[32,8,4096]{2,1,0:T(8,128)(2,1)} %bitcast.57), calls=%async_computation | async-start | bytes 4194304 | tf_op jit(solution)/shard_map/all_to_all | solution.py:288
  25.8 0.0 copy-start.3
  25.8 0.0 copy-start.4
  25.8 0.0 copy-done.6
  25.8 0.1 reshape.205
  25.9 0.1 reshape_squeeze.3
  26.0 0.0 copy-done.5
  26.0 0.3 reshape.201
  26.4 0.2 slice_reduce_fusion
  26.5 0.1 reshape.202
  26.6 0.1 pad_add_fusion.1
  26.7 0.1 reshape.203
  26.8 0.1 reshape.204
  26.9 0.1 copy.28
  27.1 0.2 concatenate.31
  27.3 0.1 copy.31
  28.1 0.0 copy-done.7
  28.1 0.7 gather_fusion
  28.8 0.1 reshape_tile.3.weight
  29.0 1.4 %eq.36 = s32[544,2,128]{2,1,0:T(2,128)S(1)} broadcast(s32[544,2]{1,0:T(8,128)S(1)} %copy.31), dimensions={0,1} | broadcast | bytes 561408 | tf_op jit(solution)/shard_map/eq | solution.py:196
  30.4 0.1 fusion.mask
  30.4 45.5 %all-to-all-done = bf16[32,8,4096]{2,1,0:T(8,128)(2,1)} async-done(((bf16[32,8,4096]{2,1,0:T(8,128)(2,1)}), bf16[32,8,4096]{2,1,0:T(8,128)(2,1)}, u32[]{:S(2)}, u32[]{:S(2)}) %all-to-all-start) | async-done | bytes 2097184 | tf_op jit(solution)/shard_map/all_to_all | solution.py:288
  75.9 5.0 %last_transform.1 = (bf16[512,128]{1,0:T(8,128)(2,1)S(1)}, bf16[64,32,128]{2,1,0:T(8,128)(2,1)}) custom-call(s32[1088]{0:T(1024)S(1)} %fusion.4.place, bf16[256,4096]{1,0:T(8,128)(2,1)} %bitcast.11.x, bf16[256,256]{1,0:T(8,128)(2,1)S(1)} %copy-done.3, bf16[512,128]{1,0:T(8,128)(2,1)S(1)} %copy-done.4, bf16[544,256]{1,0:T(8,128)(2,1)S(1)} %fusion.mask, ...), custom_call_target="tpu_custom_call" | custom-call | tf_op jit(solution)/shard_map/last_transform/pallas_call | solution.py:200
  80.9 0.0 copy-start.1
  80.9 0.0 copy-start.2
  80.9 8.9 %all-to-all-start.1 = ((bf16[64,32,128]{2,1,0:T(8,128)(2,1)}), bf16[64,32,128]{2,1,0:T(8,128)(2,1)S(1)}, u32[]{:S(2)}, u32[]{:S(2)}) async-start(bf16[64,32,128]{2,1,0:T(8,128)(2,1)} %get-tuple-element.8), calls=%async_computation.1 | async-start | bytes 1048576 | tf_op jit(solution)/shard_map/all_to_all | solution.py:293
  89.9 2.3 %collective-permute-start.2 = (bf16[2,64,128]{2,1,0:T(8,128)(2,1)S(1)}, bf16[2,64,128]{2,1,0:T(8,128)(2,1)S(1)}, u32[]{:S(2)}, u32[]{:S(2)}) collective-permute-start(bf16[2,64,128]{2,1,0:T(8,128)(2,1)S(1)} %get-tuple-element.12), channel_id=1, source_target_pairs={{0,96},{32,0},{64,32},{96,64},{128,224},{160,128},{192,160},{224,1... | collective-permute-start | bytes 98312 | tf_op jit(solution)/shard_map/ppermute | solution.py:268
  92.2 0.6 collective-permute-start.1
  92.8 0.6 collective-permute-start
  93.4 1.3 %collective-permute-done.2 = bf16[2,64,128]{2,1,0:T(8,128)(2,1)S(1)} collective-permute-done((bf16[2,64,128]{2,1,0:T(8,128)(2,1)S(1)}, bf16[2,64,128]{2,1,0:T(8,128)(2,1)S(1)}, u32[]{:S(2)}, u32[]{:S(2)}) %collective-permute-start.2) | collective-permute-done | bytes 32800 | tf_op jit(solution)/shard_map/ppermute | solution.py:268
  94.7 2.8 %collective-permute-done.1 = bf16[2,64,128]{2,1,0:T(8,128)(2,1)S(1)} collective-permute-done((bf16[2,64,128]{2,1,0:T(8,128)(2,1)S(1)}, bf16[2,64,128]{2,1,0:T(8,128)(2,1)S(1)}, u32[]{:S(2)}, u32[]{:S(2)}) %collective-permute-start.1) | collective-permute-done | bytes 32800 | tf_op jit(solution)/shard_map/ppermute | solution.py:268
  97.5 1.1 collective-permute-done
  98.6 0.8 collective-permute-start.5
  99.4 2.5 %collective-permute-start.4 = (bf16[4,64,128]{2,1,0:T(8,128)(2,1)S(1)}, bf16[4,64,128]{2,1,0:T(8,128)(2,1)S(1)}, u32[]{:S(2)}, u32[]{:S(2)}) collective-permute-start(bf16[4,64,128]{2,1,0:T(8,128)(2,1)S(1)} %bitcast.62), channel_id=1, source_target_pairs={{0,2},{1,3},{2,0},{3,1},{32,34},{33,35},{34,32},{35,33},{64,66},{6... | collective-permute-start | bytes 196616 | tf_op jit(solution)/shard_map/ppermute | solution.py:273
  101.9 0.2 collective-permute-start.3
  102.1 1.4 %collective-permute-done.5 = bf16[4,64,128]{2,1,0:T(8,128)(2,1)S(1)} collective-permute-done((bf16[4,64,128]{2,1,0:T(8,128)(2,1)S(1)}, bf16[4,64,128]{2,1,0:T(8,128)(2,1)S(1)}, u32[]{:S(2)}, u32[]{:S(2)}) %collective-permute-start.5) | collective-permute-done | bytes 65568 | tf_op jit(solution)/shard_map/ppermute | solution.py:273
  103.5 1.3 %collective-permute-done.4 = bf16[4,64,128]{2,1,0:T(8,128)(2,1)S(1)} collective-permute-done((bf16[4,64,128]{2,1,0:T(8,128)(2,1)S(1)}, bf16[4,64,128]{2,1,0:T(8,128)(2,1)S(1)}, u32[]{:S(2)}, u32[]{:S(2)}) %collective-permute-start.4) | collective-permute-done | bytes 65568 | tf_op jit(solution)/shard_map/ppermute | solution.py:273
  104.8 1.2 %collective-permute-done.3 = bf16[4,64,128]{2,1,0:T(8,128)(2,1)S(1)} collective-permute-done((bf16[4,64,128]{2,1,0:T(8,128)(2,1)S(1)}, bf16[4,64,128]{2,1,0:T(8,128)(2,1)S(1)}, u32[]{:S(2)}, u32[]{:S(2)}) %collective-permute-start.3) | collective-permute-done | bytes 65568 | tf_op jit(solution)/shard_map/ppermute | solution.py:273
  106.1 1.4 %collective-permute-start.6 = (bf16[2,8,64,128]{3,2,1,0:T(8,128)(2,1)S(1)}, bf16[2,8,64,128]{3,2,1,0:T(8,128)(2,1)S(1)}, u32[]{:S(2)}, u32[]{:S(2)}) collective-permute-start(bf16[2,8,64,128]{3,2,1,0:T(8,128)(2,1)S(1)} %bitcast.59), channel_id=1, source_target_pairs={{0,1},{1,0},{2,3},{3,2},{32,33},{33,32},{34,35},{35,34},{64,65},{6... | collective-permute-start | bytes 786440 | tf_op jit(solution)/shard_map/ppermute | solution.py:273
  107.5 0.1 pad_add_fusion.2.order
  107.6 1.1 collective-permute-done.6
  108.7 0.0 all-to-all-done.1.cols
  108.7 3.1 %pair_sums.1 = f32[2,4,120,512]{3,2,1,0:T(8,128)} custom-call(s32[12]{0:T(128)S(1)} %pad_add_fusion.2.order, bf16[4,8,64,128]{3,2,1,0:T(8,128)(2,1)S(1)} %pad_maximum_fusion.rows, bf16[64,32,128]{2,1,0:T(8,128)(2,1)S(1)} %all-to-all-done.1.cols, bf16[256,512]{1,0:T(8,128)(2,1)S(1)} %copy-done.1, bf16[256,256]{1,0:T(8,128)(2,1)S(1)} %copy-done.2), custom_call_target="tpu_custom_call" | custom-call | tf_op jit(solution)/shard_map/pair_sums/pallas_call | solution.py:251
  (23 shorter events, 0.3 us)
Async XLA Ops:
  0.0 28.1 %copy-start = (f32[64]{0:T(128)S(1)}, f32[64]{0:T(128)}, u32[]{:S(2)}) copy-start(f32[64]{0:T(128)} %param.17) | copy-start | bytes 772
  12.8 13.0 %copy-start.6 = (s32[2048]{0:T(1024)S(1)}, s32[2048]{0:T(1024)}, u32[]{:S(2)}) copy-start(s32[2048]{0:T(1024)} %param.20) | copy-start | bytes 24580
  12.8 13.3 %copy-start.5 = (s32[30720]{0:T(1024)S(1)}, s32[30720]{0:T(1024)}, u32[]{:S(2)}) copy-start(s32[30720]{0:T(1024)} %param.19) | copy-start | bytes 368644
  12.8 15.3 %copy-start.7 = (s32[1,32]{1,0:T(1,128)S(1)}, s32[1,32]{1,0:T(1,128)}, u32[]{:S(2)}) copy-start(s32[1,32]{1,0:T(1,128)} %param.16) | copy-start | bytes 388
  12.8 63.1 %all-to-all-start = ((bf16[32,8,4096]{2,1,0:T(8,128)(2,1)}), bf16[32,8,4096]{2,1,0:T(8,128)(2,1)}, u32[]{:S(2)}, u32[]{:S(2)}) async-start(bf16[32,8,4096]{2,1,0:T(8,128)(2,1)} %bitcast.57), calls=%async_computation | async-start | bytes 4194304 | tf_op jit(solution)/shard_map/all_to_all | solution.py:288
  25.8 50.1 %copy-start.3 = (bf16[256,256]{1,0:T(8,128)(2,1)S(1)}, bf16[256,256]{1,0:T(8,128)(2,1)}, u32[]{:S(2)}) copy-start(bf16[256,256]{1,0:T(8,128)(2,1)} %constant.248.clone.t1) | copy-start | bytes 393220
  25.8 50.1 %copy-start.4 = (bf16[512,128]{1,0:T(8,128)(2,1)S(1)}, bf16[512,128]{1,0:T(8,128)(2,1)}, u32[]{:S(2)}) copy-start(bf16[512,128]{1,0:T(8,128)(2,1)} %constant.249.clone.pick) | copy-start | bytes 393220
  80.9 27.8 %copy-start.1 = (bf16[256,512]{1,0:T(8,128)(2,1)S(1)}, bf16[256,512]{1,0:T(8,128)(2,1)}, u32[]{:S(2)}) copy-start(bf16[256,512]{1,0:T(8,128)(2,1)} %constant.250.clone.turn) | copy-start | bytes 786436
  80.9 27.8 %copy-start.2 = (bf16[256,256]{1,0:T(8,128)(2,1)S(1)}, bf16[256,256]{1,0:T(8,128)(2,1)}, u32[]{:S(2)}) copy-start(bf16[256,256]{1,0:T(8,128)(2,1)} %constant.251.clone.halves) | copy-start | bytes 393220
  80.9 27.7 %all-to-all-start.1 = ((bf16[64,32,128]{2,1,0:T(8,128)(2,1)}), bf16[64,32,128]{2,1,0:T(8,128)(2,1)S(1)}, u32[]{:S(2)}, u32[]{:S(2)}) async-start(bf16[64,32,128]{2,1,0:T(8,128)(2,1)} %get-tuple-element.8), calls=%async_computation.1 | async-start | bytes 1048576 | tf_op jit(solution)/shard_map/all_to_all | solution.py:293
  89.9 4.8 %collective-permute-start.2 = (bf16[2,64,128]{2,1,0:T(8,128)(2,1)S(1)}, bf16[2,64,128]{2,1,0:T(8,128)(2,1)S(1)}, u32[]{:S(2)}, u32[]{:S(2)}) collective-permute-start(bf16[2,64,128]{2,1,0:T(8,128)(2,1)S(1)} %get-tuple-element.12), channel_id=1, source_target_pairs={{0,96},{32,0},{64,32},{96,64},{128,224},{160,128},{192,160},{224,1... | collective-permute-start | bytes 98312 | tf_op jit(solution)/shard_map/ppermute | solution.py:268
  92.2 5.2 %collective-permute-start.1 = (bf16[2,64,128]{2,1,0:T(8,128)(2,1)S(1)}, bf16[2,64,128]{2,1,0:T(8,128)(2,1)S(1)}, u32[]{:S(2)}, u32[]{:S(2)}) collective-permute-start(bf16[2,64,128]{2,1,0:T(8,128)(2,1)S(1)} %get-tuple-element.13), channel_id=1, source_target_pairs={{0,64},{32,96},{64,0},{96,32},{128,192},{160,224},{192,128},{224,1... | collective-permute-start | bytes 98312 | tf_op jit(solution)/shard_map/ppermute | solution.py:268
  92.8 5.7 %collective-permute-start = (bf16[2,64,128]{2,1,0:T(8,128)(2,1)S(1)}, bf16[2,64,128]{2,1,0:T(8,128)(2,1)S(1)}, u32[]{:S(2)}, u32[]{:S(2)}) collective-permute-start(bf16[2,64,128]{2,1,0:T(8,128)(2,1)S(1)} %get-tuple-element.14), channel_id=1, source_target_pairs={{0,32},{32,64},{64,96},{96,0},{128,160},{160,192},{192,224},{224,1... | collective-permute-start | bytes 98312 | tf_op jit(solution)/shard_map/ppermute | solution.py:268
  98.6 4.9 %collective-permute-start.5 = (bf16[4,64,128]{2,1,0:T(8,128)(2,1)S(1)}, bf16[4,64,128]{2,1,0:T(8,128)(2,1)S(1)}, u32[]{:S(2)}, u32[]{:S(2)}) collective-permute-start(bf16[4,64,128]{2,1,0:T(8,128)(2,1)S(1)} %get-tuple-element.10), channel_id=1, source_target_pairs={{0,130},{1,131},{2,128},{3,129},{32,162},{33,163},{34,160},{35,161... | collective-permute-start | bytes 196616 | tf_op jit(solution)/shard_map/ppermute | solution.py:273
  99.4 5.5 %collective-permute-start.4 = (bf16[4,64,128]{2,1,0:T(8,128)(2,1)S(1)}, bf16[4,64,128]{2,1,0:T(8,128)(2,1)S(1)}, u32[]{:S(2)}, u32[]{:S(2)}) collective-permute-start(bf16[4,64,128]{2,1,0:T(8,128)(2,1)S(1)} %bitcast.62), channel_id=1, source_target_pairs={{0,2},{1,3},{2,0},{3,1},{32,34},{33,35},{34,32},{35,33},{64,66},{6... | collective-permute-start | bytes 196616 | tf_op jit(solution)/shard_map/ppermute | solution.py:273
  101.9 4.2 %collective-permute-start.3 = (bf16[4,64,128]{2,1,0:T(8,128)(2,1)S(1)}, bf16[4,64,128]{2,1,0:T(8,128)(2,1)S(1)}, u32[]{:S(2)}, u32[]{:S(2)}) collective-permute-start(bf16[4,64,128]{2,1,0:T(8,128)(2,1)S(1)} %get-tuple-element.10), channel_id=1, source_target_pairs={{0,128},{1,129},{2,130},{3,131},{32,160},{33,161},{34,162},{35,163... | collective-permute-start | bytes 196616 | tf_op jit(solution)/shard_map/ppermute | solution.py:273
  106.1 2.5 %collective-permute-start.6 = (bf16[2,8,64,128]{3,2,1,0:T(8,128)(2,1)S(1)}, bf16[2,8,64,128]{3,2,1,0:T(8,128)(2,1)S(1)}, u32[]{:S(2)}, u32[]{:S(2)}) collective-permute-start(bf16[2,8,64,128]{3,2,1,0:T(8,128)(2,1)S(1)} %bitcast.59), channel_id=1, source_target_pairs={{0,1},{1,0},{2,3},{3,2},{32,33},{33,32},{34,35},{35,34},{64,65},{6... | collective-permute-start | bytes 786440 | tf_op jit(solution)/shard_map/ppermute | solution.py:273

commit v7 on v6

--- a/solution.py
+++ b/solution.py
@@ -152,13 +152,13 @@
     group=lax.broadcasted_iota(jnp.int32,(256,NG),1)//16
     for w in range(PL):
         xw=jnp.concatenate([x[:,(q*PL+w)*NG:(q*PL+w+1)*NG] for q in range(8)],axis=1)
-        f=jnp.dot(t1[...],xw,preferred_element_type=jnp.float32).astype(BF).astype(jnp.float32)
+        f=jnp.dot(t1[...],xw,preferred_element_type=jnp.float32).astype(BF)
         f=[f[:,t*NG:(t+1)*NG] for t in range(8)]
         for k in (1,2,4):
             low=group//k%2==0
             f=[jnp.where(low,f[t],pltpu.roll(f[t^k],16*k,1)) if t&k==0 else jnp.where(low,pltpu.roll(f[t^k],NG-16*k,1),f[t]) for t in range(8)]
         for t in range(8):
-            field[(w*8+t)*256:(w*8+t+1)*256,:]=f[t]
+            field[(w*8+t)*256:(w*8+t+1)*256,:]=f[t].astype(jnp.float32)
 
     def find(first, last):
         def body(r,carry):
@@ -263,10 +263,10 @@
     x_at, y_at = pair_at % 4, pair_at // 4
     both = ("pair", "gcol")
     got = [at(rows, x_at, 1)]
-    for d in range(1, 4):
+    for d in (1, 3, 2):
         perm = [(y * 4 + x, y * 4 + (x + d) % 4) for y in range(2) for x in range(4)]
         got.append(lax.ppermute(at(rows, (x_at + d) % 4, 1), "pair", perm))
-    got = jnp.stack(got, axis=1)
+    got = jnp.stack([got[0], got[1], got[3], got[2]], axis=1)
     own, other = at(got, y_at, 0), at(got, 1 - y_at, 0)
 
     def swap(block, flip_pair, flip_gcol):

time: 112 us -> 112 us (level)
  no operation moved by 1% of the time
where the time goes in v7:
time: 112 us
  waiting for transfers between devices  55.6 us (50%)
  starting transfers between devices  30.2 us (27%)
  Pallas kernels  20.8 us (19%)
  local copies, waits for them, and re-layouts  3.67 us (3%)
  between operations  1.18 us (1%)
    all_to_all x1, waiting for transfers between devices, on_device(): lax.all_to_all(part.reshape(32, 8, 4096), ('grow', 'gcol'), 0, 0, tiled=T...  45.5 us
    all_to_all x1, starting transfers between devices, on_device(): lax.all_to_all(part.reshape(32, 8, 4096), ('grow', 'gcol'), 0, 0, tiled=T...  13 us
    pallas_call x1, Pallas kernels, stage_a(): pl.pallas_call(functools.partial(kern_a, Q, steps), grid_spec=pltpu.Prefe...  12.7 us
    all_to_all x1, starting transfers between devices, on_device(): cols = lax.all_to_all(cols, ('grow', 'pair'), 0, 0, tiled=True)  8.9 us
    ppermute x3, waiting for transfers between devices, spread_rows(): got.append(lax.ppermute(at(rows, (x_at + d) % 4, 1), 'pair', perm))  5.17 us
    ppermute x4, waiting for transfers between devices, swap(): lax.ppermute(block, both, [(k, k ^ flip_pair * 4 + flip_gcol) for k in ra...  5 us
    pallas_call x1, Pallas kernels, stage_c(): pl.pallas_call(kern_c, in_specs=[pl.BlockSpec(memory_space=pltpu.SMEM)] +...  4.92 us
    ppermute x4, starting transfers between devices, swap(): lax.ppermute(block, both, [(k, k ^ flip_pair * 4 + flip_gcol) for k in ra...  4.84 us
  transfers between devices with their start and end apart: 9, of which 8 were waited for; matrix products, arithmetic and copies ran while one was open for 4% of the time, Pallas kernels for 0%

profile of v7, /device:TPU:1, one launch (start us, length us, event | category | flops | bytes accessed | tf_op | source)
XLA Modules:
  0.0 111.8 jit_solution(17587719233472403117)
XLA Ops:
  0.0 0.0 copy-start
  0.0 12.7 %partial_transform.1 = bf16[256,4096]{1,0:T(8,128)(2,1)} custom-call(s32[32]{0:T(128)} %bitcast.73, bf16[2,64,512,128]{3,2,1,0:T(8,128)(2,1)} %bitcast.56, bf16[2,512,128]{2,1,0:T(8,128)(2,1)} %bitcast.61, bf16[256,256]{1,0:T(8,128)(2,1)} %constant.245.clone.t3_hbm, bf16[4,256,256]{2,1,0:T(8,128)(2,1)} %constant.246.clone.t2_hbm, ...), custom_call_target="tpu_custom_call" | custom-call | tf_op jit(solution)/shard_map/partial_transform/pallas_call | solution.py:123
  12.8 0.0 copy-start.6
  12.8 0.0 copy-start.5
  12.8 0.0 copy-start.7
  12.8 13.0 %all-to-all-start = ((bf16[32,8,4096]{2,1,0:T(8,128)(2,1)}), bf16[32,8,4096]{2,1,0:T(8,128)(2,1)}, u32[]{:S(2)}, u32[]{:S(2)}) async-start(bf16[32,8,4096]{2,1,0:T(8,128)(2,1)} %bitcast.57), calls=%async_computation | async-start | bytes 4194304 | tf_op jit(solution)/shard_map/all_to_all | solution.py:288
  25.8 0.0 copy-start.3
  25.8 0.0 copy-start.4
  25.8 0.0 copy-done.6
  25.8 0.1 reshape.205
  25.9 0.1 reshape_squeeze.3
  26.0 0.0 copy-done.5
  26.0 0.3 reshape.201
  26.4 0.2 slice_reduce_fusion
  26.5 0.1 reshape.202
  26.6 0.1 pad_add_fusion.1
  26.7 0.1 reshape.203
  26.8 0.1 reshape.204
  26.9 0.1 copy.28
  27.1 0.2 concatenate.31
  27.3 0.1 copy.31
  28.1 0.0 copy-done.7
  28.1 0.7 gather_fusion
  28.8 0.1 reshape_tile.3.weight
  29.0 1.4 %eq.36 = s32[544,2,128]{2,1,0:T(2,128)S(1)} broadcast(s32[544,2]{1,0:T(8,128)S(1)} %copy.31), dimensions={0,1} | broadcast | bytes 561408 | tf_op jit(solution)/shard_map/eq | solution.py:196
  30.4 0.1 fusion.mask
  30.4 45.5 %all-to-all-done = bf16[32,8,4096]{2,1,0:T(8,128)(2,1)} async-done(((bf16[32,8,4096]{2,1,0:T(8,128)(2,1)}), bf16[32,8,4096]{2,1,0:T(8,128)(2,1)}, u32[]{:S(2)}, u32[]{:S(2)}) %all-to-all-start) | async-done | bytes 2097184 | tf_op jit(solution)/shard_map/all_to_all | solution.py:288
  75.9 4.9 %last_transform.1 = (bf16[512,128]{1,0:T(8,128)(2,1)S(1)}, bf16[64,32,128]{2,1,0:T(8,128)(2,1)}) custom-call(s32[1088]{0:T(1024)S(1)} %fusion.4.place, bf16[256,4096]{1,0:T(8,128)(2,1)} %bitcast.11.x, bf16[256,256]{1,0:T(8,128)(2,1)S(1)} %copy-done.3, bf16[512,128]{1,0:T(8,128)(2,1)S(1)} %copy-done.4, bf16[544,256]{1,0:T(8,128)(2,1)S(1)} %fusion.mask, ...), custom_call_target="tpu_custom_call" | custom-call | tf_op jit(solution)/shard_map/last_transform/pallas_call | solution.py:200
  80.8 0.0 copy-start.1
  80.8 0.0 copy-start.2
  80.8 8.9 %all-to-all-start.1 = ((bf16[64,32,128]{2,1,0:T(8,128)(2,1)}), bf16[64,32,128]{2,1,0:T(8,128)(2,1)S(1)}, u32[]{:S(2)}, u32[]{:S(2)}) async-start(bf16[64,32,128]{2,1,0:T(8,128)(2,1)} %get-tuple-element.8), calls=%async_computation.1 | async-start | bytes 1048576 | tf_op jit(solution)/shard_map/all_to_all | solution.py:293
  89.8 2.3 %collective-permute-start.2 = (bf16[2,64,128]{2,1,0:T(8,128)(2,1)S(1)}, bf16[2,64,128]{2,1,0:T(8,128)(2,1)S(1)}, u32[]{:S(2)}, u32[]{:S(2)}) collective-permute-start(bf16[2,64,128]{2,1,0:T(8,128)(2,1)S(1)} %get-tuple-element.12), channel_id=1, source_target_pairs={{0,96},{32,0},{64,32},{96,64},{128,224},{160,128},{192,160},{224,1... | collective-permute-start | bytes 98312 | tf_op jit(solution)/shard_map/ppermute | solution.py:268
  92.1 0.6 collective-permute-start.1
  92.7 0.6 collective-permute-start
  93.3 1.3 %collective-permute-done.2 = bf16[2,64,128]{2,1,0:T(8,128)(2,1)S(1)} collective-permute-done((bf16[2,64,128]{2,1,0:T(8,128)(2,1)S(1)}, bf16[2,64,128]{2,1,0:T(8,128)(2,1)S(1)}, u32[]{:S(2)}, u32[]{:S(2)}) %collective-permute-start.2) | collective-permute-done | bytes 32800 | tf_op jit(solution)/shard_map/ppermute | solution.py:268
  94.6 2.8 %collective-permute-done.1 = bf16[2,64,128]{2,1,0:T(8,128)(2,1)S(1)} collective-permute-done((bf16[2,64,128]{2,1,0:T(8,128)(2,1)S(1)}, bf16[2,64,128]{2,1,0:T(8,128)(2,1)S(1)}, u32[]{:S(2)}, u32[]{:S(2)}) %collective-permute-start.1) | collective-permute-done | bytes 32800 | tf_op jit(solution)/shard_map/ppermute | solution.py:268
  97.4 1.1 collective-permute-done
  98.5 0.8 collective-permute-start.5
  99.3 2.5 %collective-permute-start.4 = (bf16[4,64,128]{2,1,0:T(8,128)(2,1)S(1)}, bf16[4,64,128]{2,1,0:T(8,128)(2,1)S(1)}, u32[]{:S(2)}, u32[]{:S(2)}) collective-permute-start(bf16[4,64,128]{2,1,0:T(8,128)(2,1)S(1)} %bitcast.62), channel_id=1, source_target_pairs={{0,2},{1,3},{2,0},{3,1},{32,34},{33,35},{34,32},{35,33},{64,66},{6... | collective-permute-start | bytes 196616 | tf_op jit(solution)/shard_map/ppermute | solution.py:273
  101.8 0.2 collective-permute-start.3
  102.0 1.4 %collective-permute-done.5 = bf16[4,64,128]{2,1,0:T(8,128)(2,1)S(1)} collective-permute-done((bf16[4,64,128]{2,1,0:T(8,128)(2,1)S(1)}, bf16[4,64,128]{2,1,0:T(8,128)(2,1)S(1)}, u32[]{:S(2)}, u32[]{:S(2)}) %collective-permute-start.5) | collective-permute-done | bytes 65568 | tf_op jit(solution)/shard_map/ppermute | solution.py:273
  103.4 1.3 %collective-permute-done.4 = bf16[4,64,128]{2,1,0:T(8,128)(2,1)S(1)} collective-permute-done((bf16[4,64,128]{2,1,0:T(8,128)(2,1)S(1)}, bf16[4,64,128]{2,1,0:T(8,128)(2,1)S(1)}, u32[]{:S(2)}, u32[]{:S(2)}) %collective-permute-start.4) | collective-permute-done | bytes 65568 | tf_op jit(solution)/shard_map/ppermute | solution.py:273
  104.8 1.2 %collective-permute-done.3 = bf16[4,64,128]{2,1,0:T(8,128)(2,1)S(1)} collective-permute-done((bf16[4,64,128]{2,1,0:T(8,128)(2,1)S(1)}, bf16[4,64,128]{2,1,0:T(8,128)(2,1)S(1)}, u32[]{:S(2)}, u32[]{:S(2)}) %collective-permute-start.3) | collective-permute-done | bytes 65568 | tf_op jit(solution)/shard_map/ppermute | solution.py:273
  106.0 1.3 %collective-permute-start.6 = (bf16[2,8,64,128]{3,2,1,0:T(8,128)(2,1)S(1)}, bf16[2,8,64,128]{3,2,1,0:T(8,128)(2,1)S(1)}, u32[]{:S(2)}, u32[]{:S(2)}) collective-permute-start(bf16[2,8,64,128]{3,2,1,0:T(8,128)(2,1)S(1)} %bitcast.59), channel_id=1, source_target_pairs={{0,1},{1,0},{2,3},{3,2},{32,33},{33,32},{34,35},{35,34},{64,65},{6... | collective-permute-start | bytes 786440 | tf_op jit(solution)/shard_map/ppermute | solution.py:273
  107.4 0.1 pad_add_fusion.2.order
  107.4 1.1 collective-permute-done.6
  108.6 0.0 all-to-all-done.1.cols
  108.6 3.1 %pair_sums.1 = f32[2,4,120,512]{3,2,1,0:T(8,128)} custom-call(s32[12]{0:T(128)S(1)} %pad_add_fusion.2.order, bf16[4,8,64,128]{3,2,1,0:T(8,128)(2,1)S(1)} %pad_maximum_fusion.rows, bf16[64,32,128]{2,1,0:T(8,128)(2,1)S(1)} %all-to-all-done.1.cols, bf16[256,512]{1,0:T(8,128)(2,1)S(1)} %copy-done.1, bf16[256,256]{1,0:T(8,128)(2,1)S(1)} %copy-done.2), custom_call_target="tpu_custom_call" | custom-call | tf_op jit(solution)/shard_map/pair_sums/pallas_call | solution.py:251
  (23 shorter events, 0.3 us)
Async XLA Ops:
  0.0 28.1 %copy-start = (f32[64]{0:T(128)S(1)}, f32[64]{0:T(128)}, u32[]{:S(2)}) copy-start(f32[64]{0:T(128)} %param.17) | copy-start | bytes 772
  12.8 13.0 %copy-start.6 = (s32[2048]{0:T(1024)S(1)}, s32[2048]{0:T(1024)}, u32[]{:S(2)}) copy-start(s32[2048]{0:T(1024)} %param.20) | copy-start | bytes 24580
  12.8 13.3 %copy-start.5 = (s32[30720]{0:T(1024)S(1)}, s32[30720]{0:T(1024)}, u32[]{:S(2)}) copy-start(s32[30720]{0:T(1024)} %param.19) | copy-start | bytes 368644
  12.8 15.3 %copy-start.7 = (s32[1,32]{1,0:T(1,128)S(1)}, s32[1,32]{1,0:T(1,128)}, u32[]{:S(2)}) copy-start(s32[1,32]{1,0:T(1,128)} %param.16) | copy-start | bytes 388
  12.8 63.1 %all-to-all-start = ((bf16[32,8,4096]{2,1,0:T(8,128)(2,1)}), bf16[32,8,4096]{2,1,0:T(8,128)(2,1)}, u32[]{:S(2)}, u32[]{:S(2)}) async-start(bf16[32,8,4096]{2,1,0:T(8,128)(2,1)} %bitcast.57), calls=%async_computation | async-start | bytes 4194304 | tf_op jit(solution)/shard_map/all_to_all | solution.py:288
  25.8 50.1 %copy-start.3 = (bf16[256,256]{1,0:T(8,128)(2,1)S(1)}, bf16[256,256]{1,0:T(8,128)(2,1)}, u32[]{:S(2)}) copy-start(bf16[256,256]{1,0:T(8,128)(2,1)} %constant.248.clone.t1) | copy-start | bytes 393220
  25.8 50.1 %copy-start.4 = (bf16[512,128]{1,0:T(8,128)(2,1)S(1)}, bf16[512,128]{1,0:T(8,128)(2,1)}, u32[]{:S(2)}) copy-start(bf16[512,128]{1,0:T(8,128)(2,1)} %constant.249.clone.pick) | copy-start | bytes 393220
  80.8 27.7 %copy-start.1 = (bf16[256,512]{1,0:T(8,128)(2,1)S(1)}, bf16[256,512]{1,0:T(8,128)(2,1)}, u32[]{:S(2)}) copy-start(bf16[256,512]{1,0:T(8,128)(2,1)} %constant.250.clone.turn) | copy-start | bytes 786436
  80.8 27.7 %copy-start.2 = (bf16[256,256]{1,0:T(8,128)(2,1)S(1)}, bf16[256,256]{1,0:T(8,128)(2,1)}, u32[]{:S(2)}) copy-start(bf16[256,256]{1,0:T(8,128)(2,1)} %constant.251.clone.halves) | copy-start | bytes 393220
  80.8 27.7 %all-to-all-start.1 = ((bf16[64,32,128]{2,1,0:T(8,128)(2,1)}), bf16[64,32,128]{2,1,0:T(8,128)(2,1)S(1)}, u32[]{:S(2)}, u32[]{:S(2)}) async-start(bf16[64,32,128]{2,1,0:T(8,128)(2,1)} %get-tuple-element.8), calls=%async_computation.1 | async-start | bytes 1048576 | tf_op jit(solution)/shard_map/all_to_all | solution.py:293
  89.8 4.8 %collective-permute-start.2 = (bf16[2,64,128]{2,1,0:T(8,128)(2,1)S(1)}, bf16[2,64,128]{2,1,0:T(8,128)(2,1)S(1)}, u32[]{:S(2)}, u32[]{:S(2)}) collective-permute-start(bf16[2,64,128]{2,1,0:T(8,128)(2,1)S(1)} %get-tuple-element.12), channel_id=1, source_target_pairs={{0,96},{32,0},{64,32},{96,64},{128,224},{160,128},{192,160},{224,1... | collective-permute-start | bytes 98312 | tf_op jit(solution)/shard_map/ppermute | solution.py:268
  92.1 5.2 %collective-permute-start.1 = (bf16[2,64,128]{2,1,0:T(8,128)(2,1)S(1)}, bf16[2,64,128]{2,1,0:T(8,128)(2,1)S(1)}, u32[]{:S(2)}, u32[]{:S(2)}) collective-permute-start(bf16[2,64,128]{2,1,0:T(8,128)(2,1)S(1)} %get-tuple-element.13), channel_id=1, source_target_pairs={{0,64},{32,96},{64,0},{96,32},{128,192},{160,224},{192,128},{224,1... | collective-permute-start | bytes 98312 | tf_op jit(solution)/shard_map/ppermute | solution.py:268
  92.7 5.7 %collective-permute-start = (bf16[2,64,128]{2,1,0:T(8,128)(2,1)S(1)}, bf16[2,64,128]{2,1,0:T(8,128)(2,1)S(1)}, u32[]{:S(2)}, u32[]{:S(2)}) collective-permute-start(bf16[2,64,128]{2,1,0:T(8,128)(2,1)S(1)} %get-tuple-element.14), channel_id=1, source_target_pairs={{0,32},{32,64},{64,96},{96,0},{128,160},{160,192},{192,224},{224,1... | collective-permute-start | bytes 98312 | tf_op jit(solution)/shard_map/ppermute | solution.py:268
  98.5 4.9 %collective-permute-start.5 = (bf16[4,64,128]{2,1,0:T(8,128)(2,1)S(1)}, bf16[4,64,128]{2,1,0:T(8,128)(2,1)S(1)}, u32[]{:S(2)}, u32[]{:S(2)}) collective-permute-start(bf16[4,64,128]{2,1,0:T(8,128)(2,1)S(1)} %get-tuple-element.10), channel_id=1, source_target_pairs={{0,130},{1,131},{2,128},{3,129},{32,162},{33,163},{34,160},{35,161... | collective-permute-start | bytes 196616 | tf_op jit(solution)/shard_map/ppermute | solution.py:273
  99.3 5.5 %collective-permute-start.4 = (bf16[4,64,128]{2,1,0:T(8,128)(2,1)S(1)}, bf16[4,64,128]{2,1,0:T(8,128)(2,1)S(1)}, u32[]{:S(2)}, u32[]{:S(2)}) collective-permute-start(bf16[4,64,128]{2,1,0:T(8,128)(2,1)S(1)} %bitcast.62), channel_id=1, source_target_pairs={{0,2},{1,3},{2,0},{3,1},{32,34},{33,35},{34,32},{35,33},{64,66},{6... | collective-permute-start | bytes 196616 | tf_op jit(solution)/shard_map/ppermute | solution.py:273
  101.8 4.2 %collective-permute-start.3 = (bf16[4,64,128]{2,1,0:T(8,128)(2,1)S(1)}, bf16[4,64,128]{2,1,0:T(8,128)(2,1)S(1)}, u32[]{:S(2)}, u32[]{:S(2)}) collective-permute-start(bf16[4,64,128]{2,1,0:T(8,128)(2,1)S(1)} %get-tuple-element.10), channel_id=1, source_target_pairs={{0,128},{1,129},{2,130},{3,131},{32,160},{33,161},{34,162},{35,163... | collective-permute-start | bytes 196616 | tf_op jit(solution)/shard_map/ppermute | solution.py:273
  106.0 2.5 %collective-permute-start.6 = (bf16[2,8,64,128]{3,2,1,0:T(8,128)(2,1)S(1)}, bf16[2,8,64,128]{3,2,1,0:T(8,128)(2,1)S(1)}, u32[]{:S(2)}, u32[]{:S(2)}) collective-permute-start(bf16[2,8,64,128]{3,2,1,0:T(8,128)(2,1)S(1)} %bitcast.59), channel_id=1, source_target_pairs={{0,1},{1,0},{2,3},{3,2},{32,33},{33,32},{34,35},{35,34},{64,65},{6... | collective-permute-start | bytes 786440 | tf_op jit(solution)/shard_map/ppermute | solution.py:273
